TPU v7x, 256 devices: a whole 4x4x8 slice. The times are simulated.
256 devices in a mesh: ta: 16 (over y, x), ha: 8 (over z_hi, core), hd: 2 (over z_lo).
Axes of the slice: x: 4, y: 4, z: 8 (z_hi: 4, z_lo: 2; z = z_hi * 2 + z_lo), core: 2. Of those that a mesh axis runs over, the one named last changes fastest.
Arguments:
- query: bfloat16 [32, 32, 64, 1536], P('ta', 'ha', None, 'hd'), may hold values from -6 to 6
- keys: bfloat16 [32, 32, 64, 1536], P('ta', 'ha', None, 'hd'), may hold values from -6 to 6
- values: bfloat16 [32, 32, 64, 1536], P('ta', 'ha', None, 'hd'), may hold values from -6 to 6
- selected: int32 [16, 8, 4, 4], P('ta', 'ha'), may hold values from 0 to 15, all different within a row; in each aligned block of 4 rows (0 to 3, 4 to 7, ..., all dimensions but the last counted through in order) at most 2 rows name the same one
- window_mask: int32 [16, 8, 4, 27], P('ta', 'ha'), may hold values 0 or 1
Outputs:
- attended: bfloat16 [32, 32, 64, 1536], P('ta', 'ha', None, 'hd')
Inputs may be any that keep to these rules, and one draw needn't show every extreme that they name: `selected`: each query tile names 4 different time shards; among the 4 query tiles of one shard no time shard is named more than 2 times, and in every draw some shard names one exactly 2 times. `window_mask`: entry 13 (the tile itself) is not read.
All inputs are finite; a program needn't handle non-finite values. No bound on the sum of `window_mask` on one device may be relied on, other than what follows from the above.
Results may differ from a plain program's by a relative error of at most 0.011.
Values may be sent and summed in bfloat16 or wider, within the bound.
No kernel may reach another device: no remote copies, remote signals or barrier semaphores. Data moves between devices by JAX's collectives and lax.ppermute only.
A program may use at most 128 MiB of HBM per device.

v0:
```python
import jax
import jax.numpy as jnp
import numpy as np
from jax import lax
from jax.sharding import PartitionSpec as P

HEAD_DIM = 128
TILE_H = 4
TILE_W = 32
SEL = 4


def with_halo(block, sides, width):
    for axis, dim in sides:
        count = lax.axis_size(axis)
        forward = [(i, i + 1) for i in range(count - 1)]
        backward = [(target, source) for source, target in forward]
        low = lax.ppermute(
            lax.slice_in_dim(block, block.shape[dim] - width, None, axis=dim), axis, forward
        )
        high = lax.ppermute(lax.slice_in_dim(block, 0, width, axis=dim), axis, backward)
        block = jnp.concatenate([low, block, high], axis=dim)
    return block


def attend_two(query_tile, near_keys, near_values, near_usable, far_keys, far_values):
    head_count = query_tile.shape[-1] // HEAD_DIM
    query_heads = query_tile.reshape(-1, head_count, HEAD_DIM)
    near_k = near_keys.reshape(-1, head_count, HEAD_DIM)
    near_v = near_values.reshape(-1, head_count, HEAD_DIM)
    far_k = far_keys.reshape(-1, head_count, HEAD_DIM)
    far_v = far_values.reshape(-1, head_count, HEAD_DIM)
    scale = HEAD_DIM ** (-0.5)
    near_scores = (
        jnp.einsum("qhd,khd->hqk", query_heads, near_k, preferred_element_type=jnp.float32) * scale
    )
    near_scores = jnp.where(near_usable[None, None, :], near_scores, -jnp.inf)
    far_scores = (
        jnp.einsum("qhd,khd->hqk", query_heads, far_k, preferred_element_type=jnp.float32) * scale
    )
    highest = jnp.maximum(
        jnp.max(near_scores, axis=-1, keepdims=True), jnp.max(far_scores, axis=-1, keepdims=True)
    )
    near_raised = jnp.exp(near_scores - highest)
    far_raised = jnp.exp(far_scores - highest)
    totals = jnp.sum(near_raised, axis=-1, keepdims=True) + jnp.sum(
        far_raised, axis=-1, keepdims=True
    )
    near_weights = (near_raised / totals).astype(jnp.bfloat16)
    far_weights = (far_raised / totals).astype(jnp.bfloat16)
    mixed = jnp.einsum("hqk,khd->qhd", near_weights, near_v, preferred_element_type=jnp.float32)
    mixed = mixed + jnp.einsum(
        "hqk,khd->qhd", far_weights, far_v, preferred_element_type=jnp.float32
    )
    return mixed.reshape(-1, head_count * HEAD_DIM).astype(jnp.bfloat16)


def body(query, keys, values, selected, window_mask):
    frames_here, rows_here, columns, channels = query.shape
    row_blocks = rows_here // TILE_H
    col_blocks = columns // TILE_W
    tile_count = frames_here * row_blocks * col_blocks
    tile_size = TILE_H * TILE_W
    shards = lax.axis_size("ta")
    frames_all = frames_here * shards
    rows_all = row_blocks * lax.axis_size("ha")
    frame_base = lax.axis_index("ta") * frames_here
    row_base = lax.axis_index("ha") * row_blocks
    paired = jnp.stack([keys, values], 0)
    zero = jnp.zeros((), jnp.int32)
    extended = with_halo(paired, (("ta", 1),), 1)
    extended = with_halo(extended, (("ha", 2),), TILE_H)
    extended = jnp.pad(extended, ((0, 0), (0, 0), (0, 0), (TILE_W, TILE_W), (0, 0)))
    owners = selected.reshape(-1)
    entries = tile_count * SEL
    capacity = max(2, -(-entries // shards))
    slot_ids = jnp.arange(capacity, dtype=jnp.int32)
    tile_of = jnp.arange(entries, dtype=jnp.int32) // SEL
    owner_hits = (owners[:, None] == jnp.arange(shards, dtype=jnp.int32)[None, :]).astype(jnp.int32)
    places = jnp.sum(owner_hits * (jnp.cumsum(owner_hits, 0) - owner_hits), 1)
    matched = (owner_hits[:, :, None] == 1) & (places[:, None, None] == slot_ids[None, None, :])
    tables = jnp.sum(jnp.where(matched, tile_of[:, None, None] + 1, 0), 0) - 1
    wanted = lax.all_to_all(tables, "ta", split_axis=0, concat_axis=0, tiled=True)

    def serve_one(request):
        number = jnp.maximum(request, 0)
        frame_tile = number // (row_blocks * col_blocks)
        row_start = number // col_blocks % row_blocks * TILE_H
        col_start = number % col_blocks * TILE_W
        piece = lax.dynamic_slice(
            paired, (zero, frame_tile, row_start, col_start, zero), (2, 1, TILE_H, TILE_W, channels)
        )
        piece = piece.reshape(2, tile_size, channels)
        return jnp.where(request >= 0, piece, jnp.zeros((), jnp.bfloat16))

    served = lax.map(serve_one, wanted.reshape(-1)).reshape(
        shards, capacity, 2, tile_size, channels
    )
    arrived = lax.all_to_all(served, "ta", split_axis=0, concat_axis=0, tiled=True)
    owner_tiles = owners.reshape(tile_count, SEL)
    place_tiles = places.reshape(tile_count, SEL)
    window_marks = window_mask.reshape(tile_count, 27)
    step_time = jnp.asarray(np.repeat([-1, 0, 1], 9), jnp.int32)
    step_rows = jnp.asarray(np.tile(np.repeat([-1, 0, 1], 3), 3), jnp.int32)
    step_cols = jnp.asarray(np.tile([-1, 0, 1], 9), jnp.int32)

    def one_tile(number, output):
        frame_tile = (number // (row_blocks * col_blocks)).astype(jnp.int32)
        row_tile = (number // col_blocks % row_blocks).astype(jnp.int32)
        col_tile = (number % col_blocks).astype(jnp.int32)
        row_start = row_tile * TILE_H
        col_start = col_tile * TILE_W
        query_tile = lax.dynamic_slice(
            query, (frame_tile, row_start, col_start, zero), (1, TILE_H, TILE_W, channels)
        ).reshape(tile_size, channels)
        region = lax.dynamic_slice(
            extended,
            (zero, frame_tile, row_start, col_start, zero),
            (2, 3, 3 * TILE_H, 3 * TILE_W, channels),
        )
        region = region.reshape(2, 27 * tile_size, channels)
        frame_near = frame_base + frame_tile + step_time
        row_near = row_base + row_tile + step_rows
        col_near = col_tile + step_cols
        inside = (
            (frame_near >= 0)
            & (frame_near < frames_all)
            & (row_near >= 0)
            & (row_near < rows_all)
            & (col_near >= 0)
            & (col_near < col_blocks)
        )
        tile_marks = lax.dynamic_index_in_dim(window_marks, number, 0, False)
        switched = inside & ((tile_marks == 1) | (jnp.arange(27, dtype=jnp.int32) == 13))
        spread = jnp.repeat(jnp.repeat(switched.reshape(3, 3, 3), TILE_H, axis=1), TILE_W, axis=2)
        near_usable = spread.reshape(27 * tile_size)
        tile_owners = lax.dynamic_index_in_dim(owner_tiles, number, 0, False)
        tile_places = lax.dynamic_index_in_dim(place_tiles, number, 0, False)
        far_pair = arrived[tile_owners, tile_places]
        far_keys = far_pair[:, 0].reshape(SEL * tile_size, channels)
        far_values = far_pair[:, 1].reshape(SEL * tile_size, channels)
        result = attend_two(query_tile, region[0], region[1], near_usable, far_keys, far_values)
        return lax.dynamic_update_slice(
            output,
            result.reshape(1, TILE_H, TILE_W, channels),
            (frame_tile, row_start, col_start, zero),
        )

    empty = jnp.zeros((frames_here, rows_here, columns, channels), jnp.bfloat16)
    return lax.fori_loop(0, tile_count, one_tile, empty)


def solution(mesh):
    in_specs = (
        P("ta", "ha", None, "hd"),
        P("ta", "ha", None, "hd"),
        P("ta", "ha", None, "hd"),
        P("ta", "ha", None, None),
        P("ta", "ha", None, None),
    )
    out_specs = P("ta", "ha", None, "hd")
    return jax.shard_map(body, mesh=mesh, in_specs=in_specs, out_specs=out_specs, check_vma=False)
```

profile of v0, /device:TPU:1, one launch (start us, length us, event | category | flops | bytes accessed | tf_op | source)
XLA Modules:
  0.0 715.9 jit_solution(9093788998351866340)
XLA Ops:
  1.9 7.6 %all-to-all-start = ((s32[16,1,2]{2,1,0:T(1,128)}), s32[16,1,2]{2,1,0:T(1,128)S(1)}, u32[]{:S(2)}, u32[]{:S(2)}) async-start(s32[16,1,2]{2,1,0:T(1,128)} %copy.51), calls=%async_computation | async-start | bytes 16384 | tf_op jit(solution)/shard_map/all_to_all | solution.py:83
  17.1 88.5 %while.28 = (s32[]{:T(128)}, bf16[32,2,128,768]{3,2,1,0:T(8,128)(2,1)}, s32[32]{0:T(128)S(1)}, bf16[2,2,4,64,768]{4,3,2,1,0:T(8,128)(2,1)S(1)}, s32[]{:T(128)}, ...) while((s32[]{:T(128)}, ...), condition=%wide.region_4.5_spmd, body=%wide.region_3.4_spmd.sunk | while | flops 196631 | bytes 1573230 | solution.py:96
  116.2 193.0 %collective-permute-done.1 = bf16[2,1,4,64,768]{4,3,2,1,0:T(8,128)(2,1)S(1)} collective-permute-done((bf16[2,1,4,64,768]{4,3,2,1,0:T(8,128)(2,1)S(1)}, bf16[2,1,4,64,768]{4,3,2,1,0:T(8,128)(2,1)S(1)}, u32[]{:S(2)}, u32[]{:S(2)}) %collective-permute-start.1) | collective-permute-done | bytes 786464 | tf_op jit(solution)/shard_map/ppermute | solution.py:21
  320.7 66.9 %collective-permute-done.3 = bf16[2,4,4,64,768]{4,3,2,1,0:T(8,128)(2,1)} collective-permute-done((bf16[2,4,4,64,768]{4,3,2,1,0:T(8,128)(2,1)}, bf16[2,4,4,64,768]{4,3,2,1,0:T(8,128)(2,1)}, u32[]{:S(2)}, u32[]{:S(2)}) %collective-permute-start.3) | collective-permute-done | bytes 3145760 | tf_op jit(solution)/shard_map/ppermute | solution.py:21
  387.6 14.7 %select_maximum_fusion = bf16[2,4,12,128,768]{4,3,2,1,0:T(8,128)(2,1)} fusion(bf16[2,4,4,64,768]{4,3,2,1,0:T(8,128)(2,1)} %collective-permute-done.3, bf16[2,4,4,64,768]{4,3,2,1,0:T(8,128)(2,1)} %collective-permute-done.2, bf16[2,1,4,64,768]{4,3,2,1,0:T(8,128)(2,1)S(1)} %collective-permute-done.1, bf16[2,1,4,64,768]{4,3,2,1,0:T(8,128)(2,1)S(1)} %collective-permute-done, ...), kind=kLoop, calls=%fused_computation.45 | loop fusion | flops 198180864 | bytes 28311552 | tf_op jit(solution)/shard_map/concatenate | solution.py:22
  403.2 312.7 %while.29 = (s32[]{:T(128)}, bf16[2,4,64,768]{3,2,1,0:T(8,128)(2,1)}, bf16[2,4,12,128,768]{4,3,2,1,0:T(8,128)(2,1)}, s32[]{:T(128)}, s32[]{:T(128)}, /*index=5*/...) while((s32[]{:T(128)}, ...), condition=%wide.region_10.11_spmd.clone, body=%wide.region_5.10_spmd.sunk.clone.sunk | while | flops 1595079936 | bytes 133175576 | solution.py:150
  403.4 9.2 %constant_dynamic-slice_fusion.8 = (bf16[1,3,12,96,768]{4,3,2,1,0:T(8,128)(2,1)}, bf16[1,3,12,96,768]{4,3,2,1,0:T(8,128)(2,1)}) fusion(bf16[2,4,12,128,768]{4,3,2,1,0:T(8,128)(2,1)} %get-tuple-element.652, s32[]{:T(128)S(6)} %select_n.292, s32[]{:T(128)S(6)} %select_n.294, s32[]{:T(128)S(6)} %add.403), kind=kLoop, calls=%fused_computation.36.clone.1 | loop fusion | bytes 21233676 | tf_op jit(solution)/shard_map/while/body/eval_jaxpr/slice | solution.py:142
  412.6 11.7 %squeeze.75 = bf16[3456,6,128]{2,1,0:T(8,128)(2,1)} reshape(bf16[1,3,12,96,768]{4,3,2,1,0:T(8,128)(2,1)} %get-tuple-element.562) | data formatting | bytes 10616832 | tf_op jit(solution)/shard_map/while/body/eval_jaxpr/reshape;while/body/eval_jaxpr/squeeze | solution.py:30
  425.9 11.7 %squeeze.76 = bf16[3456,6,128]{2,1,0:T(8,128)(2,1)} reshape(bf16[1,3,12,96,768]{4,3,2,1,0:T(8,128)(2,1)} %get-tuple-element.563) | data formatting | bytes 10616832 | tf_op jit(solution)/shard_map/while/body/eval_jaxpr/reshape;while/body/eval_jaxpr/squeeze | solution.py:29
  438.8 9.1 %fusion.48 = (f32[6,128]{1,0:T(8,128)S(1)}, f32[6,128,3456]{2,1,0:T(8,128)}) fusion(pred[3456]{0:T(1024)(128)(4,1)S(1)} %broadcast_in_dim.150, bf16[3456,6,128]{2,1,0:T(8,128)(2,1)} %squeeze.76, bf16[128,6,128]{2,1,0:T(8,128)(2,1)S(1)} %reshape.360), kind=kOutput, calls=%fused_computation.6.clone.1 | convolution fusion | flops 687439104 | bytes 16128384 | tf_op jit(solution)/shard_map/while/body/eval_jaxpr/qhd,khd->hqk/dot_general | solution.py:35
  462.2 6.9 fusion.51
  481.6 9.2 %constant_dynamic-slice_fusion.8 = (bf16[1,3,12,96,768]{4,3,2,1,0:T(8,128)(2,1)}, bf16[1,3,12,96,768]{4,3,2,1,0:T(8,128)(2,1)}) fusion(bf16[2,4,12,128,768]{4,3,2,1,0:T(8,128)(2,1)} %get-tuple-element.652, s32[]{:T(128)S(6)} %select_n.292, s32[]{:T(128)S(6)} %select_n.294, s32[]{:T(128)S(6)} %add.403), kind=kLoop, calls=%fused_computation.36.clone.1 | loop fusion | bytes 21233676 | tf_op jit(solution)/shard_map/while/body/eval_jaxpr/slice | solution.py:142
  490.8 11.7 %squeeze.75 = bf16[3456,6,128]{2,1,0:T(8,128)(2,1)} reshape(bf16[1,3,12,96,768]{4,3,2,1,0:T(8,128)(2,1)} %get-tuple-element.562) | data formatting | bytes 10616832 | tf_op jit(solution)/shard_map/while/body/eval_jaxpr/reshape;while/body/eval_jaxpr/squeeze | solution.py:30
  504.0 11.7 %squeeze.76 = bf16[3456,6,128]{2,1,0:T(8,128)(2,1)} reshape(bf16[1,3,12,96,768]{4,3,2,1,0:T(8,128)(2,1)} %get-tuple-element.563) | data formatting | bytes 10616832 | tf_op jit(solution)/shard_map/while/body/eval_jaxpr/reshape;while/body/eval_jaxpr/squeeze | solution.py:29
  516.9 9.1 %fusion.48 = (f32[6,128]{1,0:T(8,128)S(1)}, f32[6,128,3456]{2,1,0:T(8,128)}) fusion(pred[3456]{0:T(1024)(128)(4,1)S(1)} %broadcast_in_dim.150, bf16[3456,6,128]{2,1,0:T(8,128)(2,1)} %squeeze.76, bf16[128,6,128]{2,1,0:T(8,128)(2,1)S(1)} %reshape.360), kind=kOutput, calls=%fused_computation.6.clone.1 | convolution fusion | flops 687439104 | bytes 16128384 | tf_op jit(solution)/shard_map/while/body/eval_jaxpr/qhd,khd->hqk/dot_general | solution.py:35
  559.7 9.2 %constant_dynamic-slice_fusion.8 = (bf16[1,3,12,96,768]{4,3,2,1,0:T(8,128)(2,1)}, bf16[1,3,12,96,768]{4,3,2,1,0:T(8,128)(2,1)}) fusion(bf16[2,4,12,128,768]{4,3,2,1,0:T(8,128)(2,1)} %get-tuple-element.652, s32[]{:T(128)S(6)} %select_n.292, s32[]{:T(128)S(6)} %select_n.294, s32[]{:T(128)S(6)} %add.403), kind=kLoop, calls=%fused_computation.36.clone.1 | loop fusion | bytes 21233676 | tf_op jit(solution)/shard_map/while/body/eval_jaxpr/slice | solution.py:142
  568.9 11.7 %squeeze.75 = bf16[3456,6,128]{2,1,0:T(8,128)(2,1)} reshape(bf16[1,3,12,96,768]{4,3,2,1,0:T(8,128)(2,1)} %get-tuple-element.562) | data formatting | bytes 10616832 | tf_op jit(solution)/shard_map/while/body/eval_jaxpr/reshape;while/body/eval_jaxpr/squeeze | solution.py:30
  582.1 11.7 %squeeze.76 = bf16[3456,6,128]{2,1,0:T(8,128)(2,1)} reshape(bf16[1,3,12,96,768]{4,3,2,1,0:T(8,128)(2,1)} %get-tuple-element.563) | data formatting | bytes 10616832 | tf_op jit(solution)/shard_map/while/body/eval_jaxpr/reshape;while/body/eval_jaxpr/squeeze | solution.py:29
  595.0 9.1 %fusion.48 = (f32[6,128]{1,0:T(8,128)S(1)}, f32[6,128,3456]{2,1,0:T(8,128)}) fusion(pred[3456]{0:T(1024)(128)(4,1)S(1)} %broadcast_in_dim.150, bf16[3456,6,128]{2,1,0:T(8,128)(2,1)} %squeeze.76, bf16[128,6,128]{2,1,0:T(8,128)(2,1)S(1)} %reshape.360), kind=kOutput, calls=%fused_computation.6.clone.1 | convolution fusion | flops 687439104 | bytes 16128384 | tf_op jit(solution)/shard_map/while/body/eval_jaxpr/qhd,khd->hqk/dot_general | solution.py:35
  637.8 9.2 %constant_dynamic-slice_fusion.8 = (bf16[1,3,12,96,768]{4,3,2,1,0:T(8,128)(2,1)}, bf16[1,3,12,96,768]{4,3,2,1,0:T(8,128)(2,1)}) fusion(bf16[2,4,12,128,768]{4,3,2,1,0:T(8,128)(2,1)} %get-tuple-element.652, s32[]{:T(128)S(6)} %select_n.292, s32[]{:T(128)S(6)} %select_n.294, s32[]{:T(128)S(6)} %add.403), kind=kLoop, calls=%fused_computation.36.clone.1 | loop fusion | bytes 21233676 | tf_op jit(solution)/shard_map/while/body/eval_jaxpr/slice | solution.py:142
  647.0 11.7 %squeeze.75 = bf16[3456,6,128]{2,1,0:T(8,128)(2,1)} reshape(bf16[1,3,12,96,768]{4,3,2,1,0:T(8,128)(2,1)} %get-tuple-element.562) | data formatting | bytes 10616832 | tf_op jit(solution)/shard_map/while/body/eval_jaxpr/reshape;while/body/eval_jaxpr/squeeze | solution.py:30
  660.2 11.7 %squeeze.76 = bf16[3456,6,128]{2,1,0:T(8,128)(2,1)} reshape(bf16[1,3,12,96,768]{4,3,2,1,0:T(8,128)(2,1)} %get-tuple-element.563) | data formatting | bytes 10616832 | tf_op jit(solution)/shard_map/while/body/eval_jaxpr/reshape;while/body/eval_jaxpr/squeeze | solution.py:29
  673.1 9.1 %fusion.48 = (f32[6,128]{1,0:T(8,128)S(1)}, f32[6,128,3456]{2,1,0:T(8,128)}) fusion(pred[3456]{0:T(1024)(128)(4,1)S(1)} %broadcast_in_dim.150, bf16[3456,6,128]{2,1,0:T(8,128)(2,1)} %squeeze.76, bf16[128,6,128]{2,1,0:T(8,128)(2,1)S(1)} %reshape.360), kind=kOutput, calls=%fused_computation.6.clone.1 | convolution fusion | flops 687439104 | bytes 16128384 | tf_op jit(solution)/shard_map/while/body/eval_jaxpr/qhd,khd->hqk/dot_general | solution.py:35
  696.5 6.9 fusion.51
  (275 shorter events, 210.1 us)
Async XLA Ops:
  1.9 13.9 %all-to-all-start = ((s32[16,1,2]{2,1,0:T(1,128)}), s32[16,1,2]{2,1,0:T(1,128)S(1)}, u32[]{:S(2)}, u32[]{:S(2)}) async-start(s32[16,1,2]{2,1,0:T(1,128)} %copy.51), calls=%async_computation | async-start | bytes 16384 | tf_op jit(solution)/shard_map/all_to_all | solution.py:83
  105.6 5.1 copy-start.1
  105.6 5.1 copy-start.2
  105.6 296.7 %all-to-all-start.1 = ((bf16[16,2,2,128,768]{4,3,2,1,0:T(8,128)(2,1)}), bf16[16,2,2,128,768]{4,3,2,1,0:T(8,128)(2,1)}, u32[]{:S(2)}, u32[]{:S(2)}) async-start(bf16[16,2,2,128,768]{4,3,2,1,0:T(8,128)(2,1)} %bitcast.76), calls=%async_computation.1 | async-start | bytes 25165824 | tf_op jit(solution)/shard_map/all_to_all | solution.py:99
  110.8 198.3 %collective-permute-start.1 = (bf16[2,1,4,64,768]{4,3,2,1,0:T(8,128)(2,1)S(1)}, bf16[2,1,4,64,768]{4,3,2,1,0:T(8,128)(2,1)S(1)}, u32[]{:S(2)}, u32[]{:S(2)}) collective-permute-start(bf16[2,1,4,64,768]{4,3,2,1,0:T(8,128)(2,1)S(1)} %get-tuple-element.465), channel_id=1, source_target_pairs={{16,0},{32,16},{48,32},{64,48},{80,64},{96,80},{112,96},{128,112},... | collective-permute-start | bytes 2359304 | tf_op jit(solution)/shard_map/ppermute | solution.py:21
  112.1 197.0 %collective-permute-start = (bf16[2,1,4,64,768]{4,3,2,1,0:T(8,128)(2,1)S(1)}, bf16[2,1,4,64,768]{4,3,2,1,0:T(8,128)(2,1)S(1)}, u32[]{:S(2)}, u32[]{:S(2)}) collective-permute-start(bf16[2,1,4,64,768]{4,3,2,1,0:T(8,128)(2,1)S(1)} %get-tuple-element.464), channel_id=1, source_target_pairs={{0,16},{16,32},{32,48},{48,64},{64,80},{80,96},{96,112},{112,128},... | collective-permute-start | bytes 2359304 | tf_op jit(solution)/shard_map/ppermute | solution.py:18
  311.0 76.6 %collective-permute-start.3 = (bf16[2,4,4,64,768]{4,3,2,1,0:T(8,128)(2,1)}, bf16[2,4,4,64,768]{4,3,2,1,0:T(8,128)(2,1)}, u32[]{:S(2)}, u32[]{:S(2)}) collective-permute-start(bf16[2,4,4,64,768]{4,3,2,1,0:T(8,128)(2,1)} %pad_maximum_fusion), channel_id=1, source_target_pairs={{2,0},{4,2},{6,4},{8,6},{10,8},{12,10},{14,12},{3,1},{5,3},{7,5},{... | collective-permute-start | bytes 9437192 | tf_op jit(solution)/shard_map/ppermute | solution.py:21
  315.8 71.8 %collective-permute-start.2 = (bf16[2,4,4,64,768]{4,3,2,1,0:T(8,128)(2,1)}, bf16[2,4,4,64,768]{4,3,2,1,0:T(8,128)(2,1)}, u32[]{:S(2)}, u32[]{:S(2)}) collective-permute-start(bf16[2,4,4,64,768]{4,3,2,1,0:T(8,128)(2,1)} %pad_maximum_fusion), channel_id=1, source_target_pairs={{0,2},{2,4},{4,6},{6,8},{8,10},{10,12},{12,14},{1,3},{3,5},{5,7},{... | collective-permute-start | bytes 9437192 | tf_op jit(solution)/shard_map/ppermute | solution.py:18
  320.6 82.6 %copy-start.3 = (s32[27]{0:T(128)S(1)}, s32[27]{0:T(128)}, u32[]{:S(2)}) copy-start(s32[27]{0:T(128)} %constant.359.clone..sunk.2) | copy-start | bytes 328
  320.6 82.6 %copy-start.4 = (s32[27]{0:T(128)S(1)}, s32[27]{0:T(128)}, u32[]{:S(2)}) copy-start(s32[27]{0:T(128)} %constant.358.clone..sunk.2) | copy-start | bytes 328
  320.7 82.6 %copy-start.5 = (s32[27]{0:T(128)S(1)}, s32[27]{0:T(128)}, u32[]{:S(2)}) copy-start(s32[27]{0:T(128)} %constant.357.clone..sunk.2) | copy-start | bytes 328
  454.9 14.7 %slice-start = ((s8[7077888]{0:T(1024)(128)(4,1)}), s8[2883584]{0:T(1024)(128)(4,1)S(1)}, s32[]{:S(2)}) async-start(s8[7077888]{0:T(1024)(128)(4,1)} %bitcast.65), calls=%async_computation.2 | async-start | bytes 5767168 | tf_op jit(solution)/shard_map/while
  462.1 7.0 copy-start
  462.2 7.5 %slice-start.1 = ((s8[7077888]{0:T(1024)(128)(4,1)}), s8[4194304]{0:T(1024)(128)(4,1)S(1)}, s32[]{:S(2)}) async-start(s8[7077888]{0:T(1024)(128)(4,1)} %bitcast.65), calls=%async_computation.3 | async-start | bytes 8388608 | tf_op jit(solution)/shard_map/while
  533.0 14.7 %slice-start = ((s8[7077888]{0:T(1024)(128)(4,1)}), s8[2883584]{0:T(1024)(128)(4,1)S(1)}, s32[]{:S(2)}) async-start(s8[7077888]{0:T(1024)(128)(4,1)} %bitcast.65), calls=%async_computation.2 | async-start | bytes 5767168 | tf_op jit(solution)/shard_map/while
  540.2 7.0 copy-start
  540.3 7.5 %slice-start.1 = ((s8[7077888]{0:T(1024)(128)(4,1)}), s8[4194304]{0:T(1024)(128)(4,1)S(1)}, s32[]{:S(2)}) async-start(s8[7077888]{0:T(1024)(128)(4,1)} %bitcast.65), calls=%async_computation.3 | async-start | bytes 8388608 | tf_op jit(solution)/shard_map/while
  611.2 14.7 %slice-start = ((s8[7077888]{0:T(1024)(128)(4,1)}), s8[2883584]{0:T(1024)(128)(4,1)S(1)}, s32[]{:S(2)}) async-start(s8[7077888]{0:T(1024)(128)(4,1)} %bitcast.65), calls=%async_computation.2 | async-start | bytes 5767168 | tf_op jit(solution)/shard_map/while
  618.4 7.0 copy-start
  618.4 7.5 %slice-start.1 = ((s8[7077888]{0:T(1024)(128)(4,1)}), s8[4194304]{0:T(1024)(128)(4,1)S(1)}, s32[]{:S(2)}) async-start(s8[7077888]{0:T(1024)(128)(4,1)} %bitcast.65), calls=%async_computation.3 | async-start | bytes 8388608 | tf_op jit(solution)/shard_map/while
  689.3 14.7 %slice-start = ((s8[7077888]{0:T(1024)(128)(4,1)}), s8[2883584]{0:T(1024)(128)(4,1)S(1)}, s32[]{:S(2)}) async-start(s8[7077888]{0:T(1024)(128)(4,1)} %bitcast.65), calls=%async_computation.2 | async-start | bytes 5767168 | tf_op jit(solution)/shard_map/while
  696.5 7.0 copy-start
  696.5 7.5 %slice-start.1 = ((s8[7077888]{0:T(1024)(128)(4,1)}), s8[4194304]{0:T(1024)(128)(4,1)S(1)}, s32[]{:S(2)}) async-start(s8[7077888]{0:T(1024)(128)(4,1)} %bitcast.65), calls=%async_computation.3 | async-start | bytes 8388608 | tf_op jit(solution)/shard_map/while
where the time goes:
time: 729 us; the launch traced here: 716 us
  waiting for transfers between devices  265 us (36%)
  local copies, waits for them, and re-layouts  245 us (34%)
  matrix products  78.6 us (11%)
  other arithmetic  57.2 us (8%)
  loops' own time  43 us (6%)
  starting transfers between devices  27.6 us (4%)
    ppermute x2, waiting for transfers between devices, with_halo(): lax.ppermute(lax.slice_in_dim(block, 0, width, axis=dim), axis, backward)  260 us
    squeeze x4, local copies, waits for them, and re-layouts, attend_two(): near_k = near_keys.reshape(-1, head_count, HEAD_DIM)  46.8 us
    squeeze x4, local copies, waits for them, and re-layouts, attend_two(): near_v = near_values.reshape(-1, head_count, HEAD_DIM)  46.7 us
    another operation x1, loops' own time, body(): lax.map(serve_one, wanted.reshape(-1))  42.3 us
    slice x4, local copies, waits for them, and re-layouts, one_tile(): region[0]  36.9 us
    dot_general x4, matrix products, attend_two(): jnp.einsum('qhd,khd->hqk', query_heads, near_k, preferred_element_type=jn...  36.2 us
    reduce_sum x4, other arithmetic, attend_two(): jnp.sum(near_raised, axis=-1, keepdims=True)  27.7 us
    dot_general x4, matrix products, attend_two(): jnp.einsum('hqk,khd->qhd', near_weights, near_v, preferred_element_type=j...  27.6 us
  transfers between devices with their start and end apart: 6, of which 3 were waited for; matrix products, arithmetic and copies ran while one was open for 3% of the time, Pallas kernels for 0%

commit v1 on v0

v1 whole, which is shorter than its diff:
```python
import functools
import jax
import jax.numpy as jnp
import numpy as np
from jax import lax
from jax.experimental import pallas as pl
from jax.experimental.pallas import tpu as pltpu
from jax.sharding import PartitionSpec as P

HEAD = 128
TILE = 128
SEL = 4
SIDE = 4
TA = SIDE * SIDE
HA = 8
META = 128
ROWS = 512
STAT = 32
NONE = -1e30
SCALE = float(HEAD ** -0.5)
LOG2E = float(np.log2(np.e))
VMEM_LIMIT = 50 * 1024 * 1024


def along_x(step):
    return [(SIDE * y + x, SIDE * y + (x + step) % SIDE) for y in range(SIDE) for x in range(SIDE)]


def along_y(step):
    return [(SIDE * y + x, SIDE * ((y + step) % SIDE) + x) for y in range(SIDE) for x in range(SIDE)]


def attend_tile(heads, tile, count, listed, q_ref, k_ref, v_ref, o_ref, s_ref, m_ref, l_ref, a_ref):
    frame, col = tile // 2, tile % 2
    lanes = [pl.ds(h * HEAD, HEAD) for h in range(heads)]

    def rows(r):
        return pl.ds(pl.multiple_of(frame * 256 + r * 64 + col * 32, 32), 32)

    stat_lanes = pl.ds(pl.multiple_of(tile * TILE, TILE), TILE)

    @pl.when(count == 0)
    def _():
        for r in range(4):
            o_ref[rows(r), :] = jnp.zeros((32, heads * HEAD), jnp.bfloat16)
        value = jnp.full((16, TILE), NONE, jnp.float32).astype(jnp.bfloat16)
        first = lax.broadcasted_iota(jnp.int32, (16, TILE), 0) < 8
        o_ref[pl.ds(ROWS, 16), stat_lanes] = jnp.where(first, value, jnp.zeros_like(value))
        o_ref[pl.ds(ROWS + 16, 16), stat_lanes] = jnp.zeros((16, TILE), jnp.bfloat16)

    @pl.when(count > 0)
    def _():
        for h in range(heads):
            m_ref[h] = jnp.full((TILE, TILE), NONE, jnp.float32)
            l_ref[h] = jnp.zeros((TILE, TILE), jnp.float32)
            a_ref[h] = jnp.zeros((TILE, HEAD), jnp.float32)

        def first_pass(j, carry):
            at = listed[j]
            for h in range(heads):
                q = q_ref[frame, :, col, :, lanes[h]].reshape(TILE, HEAD)
                k = k_ref[at // 2, :, at % 2, :, lanes[h]].reshape(TILE, HEAD)
                s = lax.dot_general(q, k, (((1,), (1,)), ((), ())), preferred_element_type=jnp.float32)
                s_ref[j, h] = s
                m_ref[h] = jnp.maximum(m_ref[h], s)
            return carry

        lax.fori_loop(0, count, first_pass, 0)
        for h in range(heads):
            m_ref[h] = jnp.broadcast_to(jnp.max(m_ref[h], axis=1, keepdims=True), (TILE, TILE))

        def second_pass(j, carry):
            at = listed[j]
            for h in range(heads):
                v = v_ref[at // 2, :, at % 2, :, lanes[h]].reshape(TILE, HEAD)
                p = jnp.exp2((s_ref[j, h] - m_ref[h]) * (SCALE * LOG2E))
                l_ref[h] += p
                a_ref[h] += jnp.dot(p.astype(jnp.bfloat16), v, preferred_element_type=jnp.float32)
            return carry

        lax.fori_loop(0, count, second_pass, 0)
        lane = lax.broadcasted_iota(jnp.int32, (TILE, TILE), 1)
        stats = jnp.zeros((TILE, TILE), jnp.float32)
        for h in range(heads):
            total = jnp.sum(l_ref[h], axis=1, keepdims=True)
            out = (a_ref[h] * (1.0 / total)).astype(jnp.bfloat16)
            for r in range(4):
                o_ref[rows(r), lanes[h]] = out[r * 32:(r + 1) * 32]
            stats = jnp.where(lane == h, m_ref[h] * SCALE + jnp.log(total), stats)
        turned = stats.T[0:8]
        high = turned.astype(jnp.bfloat16).astype(jnp.float32)
        mid = (turned - high).astype(jnp.bfloat16).astype(jnp.float32)
        low = turned - high - mid
        o_ref[pl.ds(ROWS, 16), stat_lanes] = jnp.concatenate([high, mid], 0).astype(jnp.bfloat16)
        o_ref[pl.ds(ROWS + 16, 16), stat_lanes] = jnp.concatenate([low, low], 0).astype(jnp.bfloat16)


def window_kernel(heads, place, meta, q0, q1, q2, k0, kr, kl, ke, v0, vr, vl, ve, o0, o1, o2,
                  qb0, qb1, qb2, kb, vb, listed, s_ref, m_ref, l_ref, a_ref, sems):
    tx, ty, height = place[0], place[1], place[2]
    shard = ty * SIDE + tx
    copies = []

    def copy(src, dst, n):
        c = pltpu.make_async_copy(src, dst, sems.at[n])
        c.start()
        copies.append(c)

    for n, (src, dst) in enumerate(((q0, qb0), (q1, qb1), (q2, qb2))):
        copy(src, dst, n)
    for n, (own, left, right, edge, dst) in enumerate(((k0, kr, kl, ke, kb), (v0, vr, vl, ve, vb))):
        copy(own, dst.at[pl.ds(1, 2)], 3 + 3 * n)

        @pl.when(tx == 0)
        def _():
            pltpu.make_async_copy(edge, dst.at[pl.ds(0, 1)], sems.at[4 + 3 * n]).start()

        @pl.when(tx != 0)
        def _():
            pltpu.make_async_copy(left.at[pl.ds(1, 1)], dst.at[pl.ds(0, 1)], sems.at[4 + 3 * n]).start()

        @pl.when(tx == SIDE - 1)
        def _():
            pltpu.make_async_copy(edge, dst.at[pl.ds(3, 1)], sems.at[5 + 3 * n]).start()

        @pl.when(tx != SIDE - 1)
        def _():
            pltpu.make_async_copy(right.at[pl.ds(0, 1)], dst.at[pl.ds(3, 1)], sems.at[5 + 3 * n]).start()

        copies.append(pltpu.make_async_copy(edge, dst.at[pl.ds(0, 1)], sems.at[4 + 3 * n]))
        copies.append(pltpu.make_async_copy(edge, dst.at[pl.ds(3, 1)], sems.at[5 + 3 * n]))
    for c in copies:
        c.wait()

    for dh, qb, o_ref in ((0, qb0, o0), (1, qb1, o1), (-1, qb2, o2)):
        asker = height - dh
        there = (asker >= 0) & (asker < HA)
        base = (shard * HA + jnp.clip(asker, 0, HA - 1)) * META + TA

        def one_tile(tile, carry):
            frame, col = tile // 2, tile % 2
            count = jnp.int32(0)
            for df in range(3):
                near = 2 * shard + frame + df - 1
                inside = there & (near >= 0) & (near < 2 * TA)
                for kw in range(2):
                    number = df * 9 + (dh + 1) * 3 + (kw - col + 1)
                    used = (meta[base + tile * 27 + number] == 1) | ((dh == 0) & (number == 13))
                    listed[count] = (frame + df) * 2 + kw
                    count = count + (used & inside).astype(jnp.int32)
            attend_tile(heads, tile, count, listed, qb, kb, vb, o_ref, s_ref, m_ref, l_ref, a_ref)
            return carry

        lax.fori_loop(0, 4, one_tile, 0)


def far_kernel(heads, place, meta, q0, q1, q2, q3, k0, k1, k2, k3, v0, v1, v2, v3, o0, o1, o2, o3,
               qb0, qb1, qb2, qb3, kb, vb, listed, s_ref, m_ref, l_ref, a_ref, sems):
    tx, ty, height = place[0], place[1], place[2]
    copies = []
    for src, dst in ((q0, qb0), (q1, qb1), (q2, qb2), (q3, qb3)):
        copies.append((src, dst))
    for n, (a, b) in enumerate(((k0, v0), (k1, v1), (k2, v2), (k3, v3))):
        copies.append((a, kb.at[pl.ds(2 * n, 2)]))
        copies.append((b, vb.at[pl.ds(2 * n, 2)]))
    copies = [pltpu.make_async_copy(src, dst, sems.at[n]) for n, (src, dst) in enumerate(copies)]
    for c in copies:
        c.start()
    for c in copies:
        c.wait()

    for back, qb, o_ref in ((0, qb0, o0), (1, qb1, o1), (2, qb2, o2), (3, qb3, o3)):
        asker = lax.rem(ty + SIDE - back, SIDE) * SIDE + tx
        base = (asker * HA + height) * META

        def one_tile(tile, carry):
            count = jnp.int32(0)
            for j in range(SEL):
                owner = meta[base + tile * SEL + j]
                piece = lax.rem(owner + SIDE - tx, SIDE)
                listed[count] = (piece * 2 + tile // 2) * 2 + tile % 2
                count = count + (owner // SIDE == ty).astype(jnp.int32)
            attend_tile(heads, tile, count, listed, qb, kb, vb, o_ref, s_ref, m_ref, l_ref, a_ref)
            return carry

        lax.fori_loop(0, 4, one_tile, 0)


def combine_kernel(heads, parts, place, *refs):
    tokens, stats, out = refs[:parts], refs[parts:2 * parts], refs[2 * parts]
    frame = pl.program_id(0)
    height = place[2]
    there = {5: height > 0, 6: height < HA - 1}
    for col in range(2):
        at = pl.ds(pl.multiple_of((frame * 2 + col) * TILE, TILE), TILE)
        logs = []
        for n in range(parts):
            s = stats[n][:, at].astype(jnp.float32)
            log = s[0:8] + s[8:16] + s[16:24]
            if n in there:
                log = jnp.where(there[n], log, NONE)
            logs.append(log)
        top = functools.reduce(jnp.maximum, logs)
        raised = [jnp.exp2((log - top) * LOG2E) for log in logs]
        under = 1.0 / functools.reduce(jnp.add, raised)
        weights = [jnp.concatenate([r * under, jnp.zeros((TILE - 8, TILE), jnp.float32)], 0).T for r in raised]
        for h in range(heads):
            lanes = pl.ds(h * HEAD, HEAD)
            mixed = None
            for n in range(parts):
                w = weights[n][:, h:h + 1]
                o = jnp.concatenate([tokens[n][pl.ds(r * 64 + col * 32, 32), lanes] for r in range(4)], 0)
                term = w * o.astype(jnp.float32)
                mixed = term if mixed is None else mixed + term
            mixed = mixed.astype(jnp.bfloat16)
            for r in range(4):
                out[pl.ds(r * 64 + col * 32, 32), lanes] = mixed[r * 32:(r + 1) * 32]


def call_attend(kernel, heads, place, meta, queries, keys, values, frames, longest, copies):
    width = heads * HEAD
    anywhere = pl.BlockSpec(memory_space=pl.ANY)
    smem = pl.BlockSpec(memory_space=pltpu.SMEM)
    held = pltpu.VMEM((frames, 4, 2, 32, width), jnp.bfloat16)
    square = pltpu.VMEM((heads, TILE, TILE), jnp.float32)
    return pl.pallas_call(
        functools.partial(kernel, heads),
        out_shape=[jax.ShapeDtypeStruct((ROWS + STAT, width), jnp.bfloat16)] * len(queries),
        in_specs=[smem, smem] + [anywhere] * (len(queries) + len(keys) + len(values)),
        out_specs=[pl.BlockSpec(memory_space=pltpu.VMEM)] * len(queries),
        scratch_shapes=[pltpu.VMEM((2, 4, 2, 32, width), jnp.bfloat16) for _ in queries]
        + [held, held, pltpu.SMEM((16,), jnp.int32)]
        + [pltpu.VMEM((longest, heads, TILE, TILE), jnp.float32), square, square, square]
        + [pltpu.SemaphoreType.DMA((copies,))],
        compiler_params=pltpu.CompilerParams(vmem_limit_bytes=VMEM_LIMIT),
    )(place, meta, *queries, *keys, *values)


def body(query, keys, values, selected, window_mask):
    frames, rows, cols, channels = query.shape
    heads = channels // HEAD
    shard = lax.axis_index("ta")
    height = lax.axis_index("ha")
    tx, ty = shard % SIDE, shard // SIDE
    place = jnp.stack([tx, ty, height]).astype(jnp.int32)
    q, k, v = [a.reshape(frames, rows, 2, 32, channels) for a in (query, keys, values)]
    meta = jnp.concatenate([selected.reshape(-1), window_mask.reshape(-1), jnp.zeros((META - 124,), jnp.int32)])
    meta = lax.all_gather(meta, ("ta", "ha"), tiled=True)

    right, left, up, down = along_x(1), along_x(-1), along_y(1), along_y(-1)
    kr, kl = lax.ppermute(k, "ta", right), lax.ppermute(k, "ta", left)
    vr, vl = lax.ppermute(v, "ta", right), lax.ppermute(v, "ta", left)
    ends = [(SIDE * y + 3, SIDE * y + 4) for y in range(SIDE - 1)]
    ends = ends + [(b, a) for a, b in ends]
    ke = lax.ppermute(jnp.where(tx == 0, k[0:1], k[1:2]), "ta", ends)
    ve = lax.ppermute(jnp.where(tx == 0, v[0:1], v[1:2]), "ta", ends)
    higher = [(i, i + 1) for i in range(HA - 1)]
    lower = [(b, a) for a, b in higher]
    q_low, q_high = lax.ppermute(q, "ha", higher), lax.ppermute(q, "ha", lower)
    q1, q2, q3 = lax.ppermute(q, "ta", up), lax.ppermute(q, "ta", along_y(2)), lax.ppermute(q, "ta", down)
    k2, v2 = lax.ppermute(kr, "ta", right), lax.ppermute(vl, "ta", left)

    own, for_low, for_high = call_attend(
        window_kernel, heads, place, meta, (q, q_low, q_high), (k, kr, kl, ke), (v, vr, vl, ve), 4, 6, 9
    )
    from_high = lax.ppermute(for_low, "ha", lower)
    from_low = lax.ppermute(for_high, "ha", higher)
    far_own, o1, o2, o3 = call_attend(
        far_kernel, heads, place, meta, (q, q1, q2, q3), (k, kl, k2, kr), (v, vl, v2, vr), 8, 4, 12
    )
    f1, f2, f3 = lax.ppermute(o1, "ta", down), lax.ppermute(o2, "ta", along_y(2)), lax.ppermute(o3, "ta", up)
    partial = [own, far_own, f1, f2, f3, from_low, from_high]
    out = pl.pallas_call(
        functools.partial(combine_kernel, heads, len(partial)),
        out_shape=jax.ShapeDtypeStruct((ROWS, channels), jnp.bfloat16),
        grid=(2,),
        in_specs=[pl.BlockSpec(memory_space=pltpu.SMEM)]
        + [pl.BlockSpec((256, channels), lambda f: (f, 0)) for _ in partial]
        + [pl.BlockSpec((STAT, channels), lambda f: (ROWS // STAT, 0)) for _ in partial],
        out_specs=pl.BlockSpec((256, channels), lambda f: (f, 0)),
        compiler_params=pltpu.CompilerParams(vmem_limit_bytes=VMEM_LIMIT),
    )(place, *partial, *partial)
    return out.reshape(frames, rows, cols, channels)


def solution(mesh):
    block = P("ta", "ha", None, "hd")
    table = P("ta", "ha", None, None)
    return jax.shard_map(
        body, mesh=mesh, in_specs=(block, block, block, table, table), out_specs=block, check_vma=False
    )
```

time: 729 us -> 368 us (0.50); the launches traced: 716 us -> 369 us
  local copies, waits for them, and re-layouts: 245 us -> 8.71 us
  waiting for transfers between devices: 265 us -> 55.4 us
  blocking collectives: 0 us -> 193 us
  matrix products: 78.6 us -> 0 us
  Pallas kernels: 0 us -> 56.3 us
  other arithmetic: 57.2 us -> 2.54 us
  loops' own time: 43 us -> 0 us
  starting transfers between devices: 27.6 us -> 53.1 us
    ppermute x4 -> x18, waiting for transfers between devices: 260 us -> 55.4 us  [the longest x1 19.3 us: body(): lax.ppermute(o1, 'ta', down)]
    all_gather x0 -> x1, blocking collectives: none -> 193 us  [body(): meta = lax.all_gather(meta, ('ta', 'ha'), tiled=True)]
    squeeze x16 -> x0, local copies, waits for them, and re-layouts: 106 us -> none  [the longest x4 46.8 us: attend_two(): near_k = near_keys.reshape(-1, head_count, HEAD_DIM)]
    dot_general x16 -> x0, matrix products: 78.6 us -> none  [the longest x4 36.2 us: attend_two(): jnp.einsum('qhd,khd->hqk', query_heads, near_k, preferred_element_type=jn...]
    pallas_call x0 -> x3, Pallas kernels: none -> 56.3 us  [the longest x2 50.4 us: call_attend(): pl.pallas_call(functools.partial(kernel, heads), out_shape=[jax.ShapeDtyp...]
    slice x12 -> x0, local copies, waits for them, and re-layouts: 54 us -> none  [the longest x4 36.9 us: one_tile(): region[0]]
    another operation x2 -> x0, loops' own time: 43 us -> none  [the longest x1 42.3 us: body(): lax.map(serve_one, wanted.reshape(-1))]
    ppermute x4 -> x18, starting transfers between devices: 14.9 us -> 53.1 us  [the longest x1 15.7 us: body(): lax.ppermute(q, 'ta', down)]
  transfers between devices with their start and end apart: 6 -> 18, of which waited for: 3 -> 4; matrix products, arithmetic and copies ran while one was open for 3% -> 1% of each run, Pallas kernels for 0% -> 14%
where the time goes in v1:
time: 368 us; the launch traced here: 369 us
  blocking collectives  193 us (52%)
  Pallas kernels  56.3 us (15%)
  waiting for transfers between devices  55.4 us (15%)
  starting transfers between devices  53.1 us (14%)
  local copies, waits for them, and re-layouts  8.71 us (2%)
    all_gather x1, blocking collectives, body(): meta = lax.all_gather(meta, ('ta', 'ha'), tiled=True)  193 us
    pallas_call x2, Pallas kernels, call_attend(): pl.pallas_call(functools.partial(kernel, heads), out_shape=[jax.ShapeDtyp...  50.4 us
    ppermute x1, waiting for transfers between devices, body(): lax.ppermute(o1, 'ta', down)  19.3 us
    ppermute x1, waiting for transfers between devices, body(): lax.ppermute(o3, 'ta', up)  18 us
    ppermute x2, waiting for transfers between devices, body(): vr, vl = (lax.ppermute(v, 'ta', right), lax.ppermute(v, 'ta', left))  16.6 us
    ppermute x1, starting transfers between devices, body(): lax.ppermute(q, 'ta', down)  15.7 us
    ppermute x2, starting transfers between devices, body(): kr, kl = (lax.ppermute(k, 'ta', right), lax.ppermute(k, 'ta', left))  9.41 us
    unnamed x36, local copies, waits for them, and re-layouts  8.54 us
  transfers between devices with their start and end apart: 18, of which 4 were waited for; matrix products, arithmetic and copies ran while one was open for 1% of the time, Pallas kernels for 14%

profile of v1, /device:TPU:1, one launch (start us, length us, event | category | flops | bytes accessed | tf_op | source)
XLA Modules:
  0.0 368.9 jit_solution(3539097011649128850)
XLA Ops:
  0.0 2.0 collective-permute-start.2
  2.0 1.2 slice_select_fusion.1
  4.1 1.2 slice_select_fusion
  6.0 7.4 %collective-permute-start.3 = (bf16[2,4,2,32,768]{4,3,2,1,0:T(8,128)(2,1)S(1)}, bf16[2,4,2,32,768]{4,3,2,1,0:T(8,128)(2,1)S(1)}, u32[]{:S(2)}, u32[]{:S(2)}) collective-permute-start(bf16[2,4,2,32,768]{4,3,2,1,0:T(8,128)(2,1)S(1)} %bitcast.13), channel_id=1, source_target_pairs={{0,48},{16,0},{32,16},{48,32},{64,112},{80,64},{96,80},{112,96},{1... | collective-permute-start | bytes 2359304 | tf_op jit(solution)/shard_map/ppermute | solution.py:251
  13.4 1.4 collective-permute-start.5
  15.6 7.3 %collective-permute-start = (bf16[2,4,2,32,768]{4,3,2,1,0:T(8,128)(2,1)S(1)}, bf16[2,4,2,32,768]{4,3,2,1,0:T(8,128)(2,1)S(1)}, u32[]{:S(2)}, u32[]{:S(2)}) collective-permute-start(bf16[2,4,2,32,768]{4,3,2,1,0:T(8,128)(2,1)S(1)} %bitcast.16), channel_id=1, source_target_pairs={{0,2},{2,4},{4,6},{6,8},{8,10},{10,12},{12,14},{1,3},{3,5},{5,7},{... | collective-permute-start | bytes 2359304 | tf_op jit(solution)/shard_map/ppermute | solution.py:259
  22.9 4.1 %collective-permute-start.1 = (bf16[2,4,2,32,768]{4,3,2,1,0:T(8,128)(2,1)S(1)}, bf16[2,4,2,32,768]{4,3,2,1,0:T(8,128)(2,1)S(1)}, u32[]{:S(2)}, u32[]{:S(2)}) collective-permute-start(bf16[2,4,2,32,768]{4,3,2,1,0:T(8,128)(2,1)S(1)} %bitcast.17), channel_id=1, source_target_pairs={{2,0},{4,2},{6,4},{8,6},{10,8},{12,10},{14,12},{3,1},{5,3},{7,5},{... | collective-permute-start | bytes 2359304 | tf_op jit(solution)/shard_map/ppermute | solution.py:259
  27.1 16.6 %collective-permute-done.6.vl.v1 = bf16[2,4,2,32,768]{4,3,2,1,0:T(8,128)(2,1)} collective-permute-done((bf16[2,4,2,32,768]{4,3,2,1,0:T(8,128)(2,1)}, bf16[2,4,2,32,768]{4,3,2,1,0:T(8,128)(2,1)}, u32[]{:S(2)}, u32[]{:S(2)}) %collective-permute-start.6) | collective-permute-done | bytes 786464 | tf_op jit(solution)/shard_map/ppermute | solution.py:252
  43.7 15.7 %collective-permute-start.10 = (bf16[2,4,2,32,768]{4,3,2,1,0:T(8,128)(2,1)S(1)}, bf16[2,4,2,32,768]{4,3,2,1,0:T(8,128)(2,1)S(1)}, u32[]{:S(2)}, u32[]{:S(2)}) collective-permute-start(bf16[2,4,2,32,768]{4,3,2,1,0:T(8,128)(2,1)S(1)} %bitcast.18), channel_id=1, source_target_pairs={{0,192},{16,208},{32,224},{48,240},{64,0},{80,16},{96,32},{112,48}... | collective-permute-start | bytes 2359304 | tf_op jit(solution)/shard_map/ppermute | solution.py:260
  59.4 1.3 collective-permute-start.9
  62.6 6.0 %collective-permute-start.12 = (bf16[2,4,2,32,768]{4,3,2,1,0:T(8,128)(2,1)}, bf16[2,4,2,32,768]{4,3,2,1,0:T(8,128)(2,1)}, u32[]{:S(2)}, u32[]{:S(2)}) collective-permute-start(bf16[2,4,2,32,768]{4,3,2,1,0:T(8,128)(2,1)} %collective-permute-done.6.vl.v1), channel_id=1, source_target_pairs={{0,48},{16,0},{32,16},{48,32},{64,112},{80,64},{96,80},{112,96},{1... | collective-permute-start | bytes 2359304 | tf_op jit(solution)/shard_map/ppermute | solution.py:261
  69.5 192.6 %all-gather = s32[128,1,128]{2,1,0:T(1,128)S(1)} all-gather(s32[1,1,128]{2,1,0:T(1,128)S(1)} %add_bitcast_fusion), channel_id=1, replica_groups=mesh['ta'=16,'ha'=8,'hd'=2] {'ta','ha'}, dimensions={0}, use_global_device_ids=true | all-gather | bytes 66048 | tf_op jit(solution)/shard_map/all_gather | solution.py:248
  262.2 1.1 copy-done.5
  263.3 1.1 copy-done.7
  265.4 29.1 %shard_map.55 = (bf16[544,768]{1,0:T(8,128)(2,1)}, bf16[544,768]{1,0:T(8,128)(2,1)}, bf16[544,768]{1,0:T(8,128)(2,1)}) custom-call(s32[3]{0:T(128)S(1)} %pad_add_fusion.place, s32[16384]{0:T(1024)S(1)} %bitcast.23, bf16[2,4,2,32,768]{4,3,2,1,0:T(8,128)(2,1)S(1)} %bitcast.21, bf16[2,4,2,32,768]{4,3,2,1,0:T(8,128)(2,1)S(1)} %copy-done.5, ...), custom_call_target="tpu_custom_call" | custom-call | tf_op jit(solution)/shard_map/pallas_call | solution.py:226
  294.5 1.9 collective-permute-start.16
  296.5 2.8 collective-permute-start.17
  299.3 21.3 %shard_map.56 = (bf16[544,768]{1,0:T(8,128)(2,1)}, bf16[544,768]{1,0:T(8,128)(2,1)}, bf16[544,768]{1,0:T(8,128)(2,1)}, bf16[544,768]{1,0:T(8,128)(2,1)}) custom-call(s32[3]{0:T(128)S(1)} %pad_add_fusion.place, s32[16384]{0:T(1024)S(1)} %bitcast.24, bf16[2,4,2,32,768]{4,3,2,1,0:T(8,128)(2,1)S(1)} %bitcast.22, ...), custom_call_target="tpu_custom_call" | custom-call | tf_op jit(solution)/shard_map/pallas_call | solution.py:226
  320.8 1.4 collective-permute-start.15
  322.2 19.3 %collective-permute-done.13.refs_2_.refs_9_ = bf16[544,768]{1,0:T(8,128)(2,1)S(1)} collective-permute-done((bf16[544,768]{1,0:T(8,128)(2,1)}, bf16[544,768]{1,0:T(8,128)(2,1)S(1)}, u32[]{:S(2)}, u32[]{:S(2)}) %collective-permute-start.13) | collective-permute-done | bytes 835616 | tf_op jit(solution)/shard_map/ppermute | solution.py:271
  341.5 1.4 collective-permute-done.14.refs_3_.refs_10_
  342.9 18.0 %collective-permute-done.15.refs_4_.refs_11_ = bf16[544,768]{1,0:T(8,128)(2,1)S(1)} collective-permute-done((bf16[544,768]{1,0:T(8,128)(2,1)}, bf16[544,768]{1,0:T(8,128)(2,1)S(1)}, u32[]{:S(2)}, u32[]{:S(2)}) %collective-permute-start.15) | collective-permute-done | bytes 835616 | tf_op jit(solution)/shard_map/ppermute | solution.py:271
  361.8 1.1 copy-done.2
  362.9 6.0 %shard_map.57 = bf16[512,768]{1,0:T(8,128)(2,1)} custom-call(s32[3]{0:T(128)S(1)} %pad_add_fusion.place, bf16[544,768]{1,0:T(8,128)(2,1)S(1)} %copy-done.1, bf16[544,768]{1,0:T(8,128)(2,1)S(1)} %copy-done.2, bf16[544,768]{1,0:T(8,128)(2,1)S(1)} %collective-permute-done.13.refs_2_.refs_9_, bf16[544,768]{1,0:T(8,128)(2,1)S(1)} %collective-permute-done.14.refs_3_.refs_10_, ...), custom_call_target="tpu_custom_call" | custom-call | tf_op jit(solution)/shard_map/pallas_call | solution.py:273
  (59 shorter events, 7.3 us)
Async XLA Ops:
  0.0 22.9 %collective-permute-start.2 = (bf16[2,4,2,32,768]{4,3,2,1,0:T(8,128)(2,1)}, bf16[2,4,2,32,768]{4,3,2,1,0:T(8,128)(2,1)S(1)}, u32[]{:S(2)}, u32[]{:S(2)}) collective-permute-start(bf16[2,4,2,32,768]{4,3,2,1,0:T(8,128)(2,1)} %bitcast.12), channel_id=1, source_target_pairs={{0,16},{16,32},{32,48},{48,0},{64,80},{80,96},{96,112},{112,64},{1... | collective-permute-start | bytes 2359304 | tf_op jit(solution)/shard_map/ppermute | solution.py:251
  2.0 13.6 %copy-start.3 = (bf16[2,4,64,768]{3,2,1,0:T(8,128)(2,1)S(1)}, bf16[2,4,64,768]{3,2,1,0:T(8,128)(2,1)}, u32[]{:S(2)}) copy-start(bf16[2,4,64,768]{3,2,1,0:T(8,128)(2,1)} %param.5) | copy-start | bytes 2359300
  3.3 2.7 copy-start
  3.3 10.2 %collective-permute-start.4 = (bf16[1,4,2,32,768]{4,3,2,1,0:T(8,128)(2,1)S(1)}, bf16[1,4,2,32,768]{4,3,2,1,0:T(8,128)(2,1)S(1)}, u32[]{:S(2)}, u32[]{:S(2)}) collective-permute-start(bf16[1,4,2,32,768]{4,3,2,1,0:T(8,128)(2,1)S(1)} %bitcast.26), channel_id=1, source_target_pairs={{48,64},{112,128},{176,192},{64,48},{128,112},{192,176},{49,65},{1... | collective-permute-start | bytes 1179656 | tf_op jit(solution)/shard_map/ppermute | solution.py:255
  5.3 9.5 %collective-permute-start.7 = (bf16[1,4,2,32,768]{4,3,2,1,0:T(8,128)(2,1)S(1)}, bf16[1,4,2,32,768]{4,3,2,1,0:T(8,128)(2,1)S(1)}, u32[]{:S(2)}, u32[]{:S(2)}) collective-permute-start(bf16[1,4,2,32,768]{4,3,2,1,0:T(8,128)(2,1)S(1)} %bitcast.25), channel_id=1, source_target_pairs={{48,64},{112,128},{176,192},{64,48},{128,112},{192,176},{49,65},{1... | collective-permute-start | bytes 1179656 | tf_op jit(solution)/shard_map/ppermute | solution.py:256
  6.0 53.4 %collective-permute-start.3 = (bf16[2,4,2,32,768]{4,3,2,1,0:T(8,128)(2,1)S(1)}, bf16[2,4,2,32,768]{4,3,2,1,0:T(8,128)(2,1)S(1)}, u32[]{:S(2)}, u32[]{:S(2)}) collective-permute-start(bf16[2,4,2,32,768]{4,3,2,1,0:T(8,128)(2,1)S(1)} %bitcast.13), channel_id=1, source_target_pairs={{0,48},{16,0},{32,16},{48,32},{64,112},{80,64},{96,80},{112,96},{1... | collective-permute-start | bytes 2359304 | tf_op jit(solution)/shard_map/ppermute | solution.py:251
  13.4 30.3 %collective-permute-start.6 = (bf16[2,4,2,32,768]{4,3,2,1,0:T(8,128)(2,1)}, bf16[2,4,2,32,768]{4,3,2,1,0:T(8,128)(2,1)}, u32[]{:S(2)}, u32[]{:S(2)}) collective-permute-start(bf16[2,4,2,32,768]{4,3,2,1,0:T(8,128)(2,1)} %bitcast.8.v0), channel_id=1, source_target_pairs={{0,48},{16,0},{32,16},{48,32},{64,112},{80,64},{96,80},{112,96},{1... | collective-permute-start | bytes 2359304 | tf_op jit(solution)/shard_map/ppermute | solution.py:252
  13.4 46.0 %collective-permute-start.5 = (bf16[2,4,2,32,768]{4,3,2,1,0:T(8,128)(2,1)}, bf16[2,4,2,32,768]{4,3,2,1,0:T(8,128)(2,1)S(1)}, u32[]{:S(2)}, u32[]{:S(2)}) collective-permute-start(bf16[2,4,2,32,768]{4,3,2,1,0:T(8,128)(2,1)} %bitcast.8.v0), channel_id=1, source_target_pairs={{0,16},{16,32},{32,48},{48,0},{64,80},{80,96},{96,112},{112,64},{1... | collective-permute-start | bytes 2359304 | tf_op jit(solution)/shard_map/ppermute | solution.py:252
  15.6 45.2 %collective-permute-start = (bf16[2,4,2,32,768]{4,3,2,1,0:T(8,128)(2,1)S(1)}, bf16[2,4,2,32,768]{4,3,2,1,0:T(8,128)(2,1)S(1)}, u32[]{:S(2)}, u32[]{:S(2)}) collective-permute-start(bf16[2,4,2,32,768]{4,3,2,1,0:T(8,128)(2,1)S(1)} %bitcast.16), channel_id=1, source_target_pairs={{0,2},{2,4},{4,6},{6,8},{8,10},{10,12},{12,14},{1,3},{3,5},{5,7},{... | collective-permute-start | bytes 2359304 | tf_op jit(solution)/shard_map/ppermute | solution.py:259
  22.9 4.1 %copy-start.13 = (bf16[2,4,2,32,768]{4,3,2,1,0:T(8,128)(2,1)}, bf16[2,4,2,32,768]{4,3,2,1,0:T(8,128)(2,1)S(1)}, u32[]{:S(2)}) copy-start(bf16[2,4,2,32,768]{4,3,2,1,0:T(8,128)(2,1)S(1)} %collective-permute-done.2.kr.k3) | copy-start | bytes 2359300
  22.9 38.7 %collective-permute-start.1 = (bf16[2,4,2,32,768]{4,3,2,1,0:T(8,128)(2,1)S(1)}, bf16[2,4,2,32,768]{4,3,2,1,0:T(8,128)(2,1)S(1)}, u32[]{:S(2)}, u32[]{:S(2)}) collective-permute-start(bf16[2,4,2,32,768]{4,3,2,1,0:T(8,128)(2,1)S(1)} %bitcast.17), channel_id=1, source_target_pairs={{2,0},{4,2},{6,4},{8,6},{10,8},{12,10},{14,12},{3,1},{5,3},{7,5},{... | collective-permute-start | bytes 2359304 | tf_op jit(solution)/shard_map/ppermute | solution.py:259
  43.7 250.8 %collective-permute-start.10 = (bf16[2,4,2,32,768]{4,3,2,1,0:T(8,128)(2,1)S(1)}, bf16[2,4,2,32,768]{4,3,2,1,0:T(8,128)(2,1)S(1)}, u32[]{:S(2)}, u32[]{:S(2)}) collective-permute-start(bf16[2,4,2,32,768]{4,3,2,1,0:T(8,128)(2,1)S(1)} %bitcast.18), channel_id=1, source_target_pairs={{0,192},{16,208},{32,224},{48,240},{64,0},{80,16},{96,32},{112,48}... | collective-permute-start | bytes 2359304 | tf_op jit(solution)/shard_map/ppermute | solution.py:260
  59.4 237.1 %collective-permute-start.8 = (bf16[2,4,2,32,768]{4,3,2,1,0:T(8,128)(2,1)S(1)}, bf16[2,4,2,32,768]{4,3,2,1,0:T(8,128)(2,1)S(1)}, u32[]{:S(2)}, u32[]{:S(2)}) collective-permute-start(bf16[2,4,2,32,768]{4,3,2,1,0:T(8,128)(2,1)S(1)} %bitcast.19), channel_id=1, source_target_pairs={{0,64},{16,80},{32,96},{48,112},{64,128},{80,144},{96,160},{112,17... | collective-permute-start | bytes 2359304 | tf_op jit(solution)/shard_map/ppermute | solution.py:260
  59.4 239.8 %collective-permute-start.9 = (bf16[2,4,2,32,768]{4,3,2,1,0:T(8,128)(2,1)S(1)}, bf16[2,4,2,32,768]{4,3,2,1,0:T(8,128)(2,1)}, u32[]{:S(2)}, u32[]{:S(2)}) collective-permute-start(bf16[2,4,2,32,768]{4,3,2,1,0:T(8,128)(2,1)S(1)} %bitcast.20), channel_id=1, source_target_pairs={{0,128},{16,144},{32,160},{48,176},{64,192},{80,208},{96,224},{112... | collective-permute-start | bytes 2359304 | tf_op jit(solution)/shard_map/ppermute | solution.py:260
  61.6 237.6 %collective-permute-start.11 = (bf16[2,4,2,32,768]{4,3,2,1,0:T(8,128)(2,1)}, bf16[2,4,2,32,768]{4,3,2,1,0:T(8,128)(2,1)}, u32[]{:S(2)}, u32[]{:S(2)}) collective-permute-start(bf16[2,4,2,32,768]{4,3,2,1,0:T(8,128)(2,1)} %copy-done.13), channel_id=1, source_target_pairs={{0,16},{16,32},{32,48},{48,0},{64,80},{80,96},{96,112},{112,64},{1... | collective-permute-start | bytes 2359304 | tf_op jit(solution)/shard_map/ppermute | solution.py:261
  62.6 236.7 %collective-permute-start.12 = (bf16[2,4,2,32,768]{4,3,2,1,0:T(8,128)(2,1)}, bf16[2,4,2,32,768]{4,3,2,1,0:T(8,128)(2,1)}, u32[]{:S(2)}, u32[]{:S(2)}) collective-permute-start(bf16[2,4,2,32,768]{4,3,2,1,0:T(8,128)(2,1)} %collective-permute-done.6.vl.v1), channel_id=1, source_target_pairs={{0,48},{16,0},{32,16},{48,32},{64,112},{80,64},{96,80},{112,96},{1... | collective-permute-start | bytes 2359304 | tf_op jit(solution)/shard_map/ppermute | solution.py:261
  294.5 27.6 %collective-permute-start.16 = (bf16[544,768]{1,0:T(8,128)(2,1)}, bf16[544,768]{1,0:T(8,128)(2,1)S(1)}, u32[]{:S(2)}, u32[]{:S(2)}) collective-permute-start(bf16[544,768]{1,0:T(8,128)(2,1)} %get-tuple-element.17), channel_id=1, source_target_pairs={{0,2},{2,4},{4,6},{6,8},{8,10},{10,12},{12,14},{1,3},{3,5},{5,7},{... | collective-permute-start | bytes 2506760 | tf_op jit(solution)/shard_map/ppermute | solution.py:267
  296.5 65.3 %copy-start.1 = (bf16[544,768]{1,0:T(8,128)(2,1)S(1)}, bf16[544,768]{1,0:T(8,128)(2,1)}, u32[]{:S(2)}) copy-start(bf16[544,768]{1,0:T(8,128)(2,1)} %get-tuple-element.12.refs_0_.refs_7_) | copy-start | bytes 2506756
  296.5 25.7 %collective-permute-start.17 = (bf16[544,768]{1,0:T(8,128)(2,1)}, bf16[544,768]{1,0:T(8,128)(2,1)S(1)}, u32[]{:S(2)}, u32[]{:S(2)}) collective-permute-start(bf16[544,768]{1,0:T(8,128)(2,1)} %get-tuple-element.18), channel_id=1, source_target_pairs={{2,0},{4,2},{6,4},{8,6},{10,8},{12,10},{14,12},{3,1},{5,3},{7,5},{... | collective-permute-start | bytes 2506760 | tf_op jit(solution)/shard_map/ppermute | solution.py:266
  320.6 20.9 %collective-permute-start.13 = (bf16[544,768]{1,0:T(8,128)(2,1)}, bf16[544,768]{1,0:T(8,128)(2,1)S(1)}, u32[]{:S(2)}, u32[]{:S(2)}) collective-permute-start(bf16[544,768]{1,0:T(8,128)(2,1)} %get-tuple-element.14), channel_id=1, source_target_pairs={{0,192},{16,208},{32,224},{48,240},{64,0},{80,16},{96,32},{112,48}... | collective-permute-start | bytes 2506760 | tf_op jit(solution)/shard_map/ppermute | solution.py:271
  320.7 22.2 %collective-permute-start.14 = (bf16[544,768]{1,0:T(8,128)(2,1)}, bf16[544,768]{1,0:T(8,128)(2,1)S(1)}, u32[]{:S(2)}, u32[]{:S(2)}) collective-permute-start(bf16[544,768]{1,0:T(8,128)(2,1)} %get-tuple-element.15), channel_id=1, source_target_pairs={{0,128},{16,144},{32,160},{48,176},{64,192},{80,208},{96,224},{112... | collective-permute-start | bytes 2506760 | tf_op jit(solution)/shard_map/ppermute | solution.py:271
  320.8 40.1 %collective-permute-start.15 = (bf16[544,768]{1,0:T(8,128)(2,1)}, bf16[544,768]{1,0:T(8,128)(2,1)S(1)}, u32[]{:S(2)}, u32[]{:S(2)}) collective-permute-start(bf16[544,768]{1,0:T(8,128)(2,1)} %get-tuple-element.16), channel_id=1, source_target_pairs={{0,64},{16,80},{32,96},{48,112},{64,128},{80,144},{96,160},{112,17... | collective-permute-start | bytes 2506760 | tf_op jit(solution)/shard_map/ppermute | solution.py:271
  322.1 38.7 %copy-start.10 = (bf16[544,768]{1,0:T(8,128)(2,1)}, bf16[544,768]{1,0:T(8,128)(2,1)S(1)}, u32[]{:S(2)}) copy-start(bf16[544,768]{1,0:T(8,128)(2,1)S(1)} %collective-permute-done.16.refs_5_.refs_12_) | copy-start | bytes 2506756
  322.1 38.7 %copy-start.11 = (bf16[544,768]{1,0:T(8,128)(2,1)}, bf16[544,768]{1,0:T(8,128)(2,1)S(1)}, u32[]{:S(2)}) copy-start(bf16[544,768]{1,0:T(8,128)(2,1)S(1)} %collective-permute-done.17.refs_6_.refs_13_) | copy-start | bytes 2506756
  (12 other events, 13.8 us)

commit v2 on v1

v2 whole, which is shorter than its diff:
```python
import functools
import jax
import jax.numpy as jnp
import numpy as np
from jax import lax
from jax.experimental import pallas as pl
from jax.experimental.pallas import tpu as pltpu
from jax.sharding import PartitionSpec as P

HEAD = 128
TILE = 128
SEL = 4
SIDE = 4
TA = SIDE * SIDE
HA = 8
STAT = 32
TABLE = 16
CHOSEN = 32
EDGE = 8
CHUNKS = 1
NONE = -1e30
SCALE = float(HEAD ** -0.5)
LOG2E = float(np.log2(np.e))
VMEM_LIMIT = 50 * 1024 * 1024
F32 = jnp.float32
BF16 = jnp.bfloat16


def along_x(step):
    return [(SIDE * y + x, SIDE * y + (x + step) % SIDE) for y in range(SIDE) for x in range(SIDE)]


def along_y(step):
    return [(SIDE * y + x, SIDE * ((y + step) % SIDE) + x) for y in range(SIDE) for x in range(SIDE)]


def attend_tile(heads, tile, count, listed, q_ref, k_ref, v_ref, o_ref, a_ref):
    stat_rows = pl.ds(pl.multiple_of((4 * heads) * TILE + STAT * tile, STAT), STAT)

    def out_rows(h):
        return pl.ds(pl.multiple_of((tile * heads + h) * TILE, TILE), TILE)

    def score(h, keys):
        q = q_ref[tile, h]
        return lax.dot_general(keys, q, (((1,), (1,)), ((), ())), preferred_element_type=F32) * (SCALE * LOG2E)

    def pair(i, h):
        a, b = listed[2 * i], listed[2 * i + 1]
        s = score(h, jnp.concatenate([k_ref[a, h], k_ref[b, h]], 0))
        s = jnp.concatenate([s[:TILE], jnp.where(2 * i + 1 < count, s[TILE:], NONE)], 0)
        return s, jnp.concatenate([v_ref[a, h], v_ref[b, h]], 1)

    def mix(values, p):
        return jnp.dot(values, p.astype(BF16), preferred_element_type=F32)

    def write(results):
        row = lax.broadcasted_iota(jnp.int32, (8, TILE), 0)
        stats = jnp.zeros((8, TILE), F32)
        for h, (top, total, mixed) in enumerate(results):
            o_ref[out_rows(h), :] = (mixed * (1.0 / total)).astype(BF16)
            stats = jnp.where(row == h, top + jnp.log2(total), stats)
        high = stats.astype(BF16).astype(F32)
        mid = (stats - high).astype(BF16).astype(F32)
        parts = jnp.concatenate([high, mid, stats - high - mid, jnp.zeros_like(stats)], 0)
        o_ref[stat_rows, :] = parts.astype(BF16)

    def once(scores):
        results = []
        for s, v in scores:
            top = jnp.max(s, axis=0, keepdims=True)
            p = jnp.exp2(s - top)
            results.append((top, jnp.sum(p, axis=0, keepdims=True), mix(v, p)))
        write(results)

    @pl.when(count == 0)
    def _():
        for h in range(heads):
            o_ref[out_rows(h), :] = jnp.zeros((TILE, TILE), BF16)
        row = lax.broadcasted_iota(jnp.int32, (STAT, TILE), 0)
        o_ref[stat_rows, :] = jnp.where(row < 8, NONE, 0.0).astype(BF16)

    @pl.when(count == 1)
    def _():
        once([(score(h, k_ref[listed[0], h]), v_ref[listed[0], h]) for h in range(heads)])

    @pl.when(count == 2)
    def _():
        once([pair(0, h) for h in range(heads)])

    @pl.when(count > 2)
    def _():
        for h in range(heads):
            a_ref[h] = jnp.zeros((TILE, TILE), F32)

        def step(i, carry):
            after = []
            for h in range(heads):
                top, total = carry[h]
                s, v = pair(i, h)
                higher = jnp.maximum(top, jnp.max(s, axis=0, keepdims=True))
                fade = jnp.exp2(top - higher)
                p = jnp.exp2(s - higher)
                a_ref[h] = a_ref[h] * fade + mix(v, p)
                after.append((higher, total * fade + jnp.sum(p, axis=0, keepdims=True)))
            return tuple(after)

        start = ((jnp.full((1, TILE), NONE, F32), jnp.zeros((1, TILE), F32)),) * heads
        ends = lax.fori_loop(0, (count + 1) // 2, step, start)
        write([(top, total, a_ref[h]) for h, (top, total) in enumerate(ends)])


def attend_kernel(heads, chunk, sets, pieces, edged, earlier, place, *refs):
    refs = list(refs)
    queries = [refs.pop(0) for _ in sets]
    held = [[refs.pop(0), refs.pop(0)] if piece else None for piece in pieces]
    edge = refs.pop(0) if edged else None
    del refs[:earlier]
    outs = [refs.pop(0) for _ in sets]
    q_bufs = [refs.pop(0) for _ in sets]
    kb, vb, marks, ints, table, listed, a_ref, sems, table_sem = refs
    tx, ty, height = place[0], place[1], place[2]
    shard = ty * SIDE + tx
    copies = []

    def copy(src, dst):
        c = pltpu.make_async_copy(src, dst, sems.at[len(copies)])
        c.start()
        copies.append(c)

    for n, (src, dst) in enumerate(zip(queries, q_bufs)):
        copy(src.at[4, 0, pl.ds(0, TABLE)], marks.at[n])
    for src, dst in zip(queries, q_bufs):
        copy(src.at[pl.ds(0, 4), pl.ds(chunk * heads, heads)], dst)
    for n, piece in enumerate(pieces):
        if piece:
            first, many = piece
            for m, dst in enumerate((kb, vb)):
                src = held[n][m]
                src = src.at[m] if len(src.shape) == 5 else src
                copy(src.at[pl.ds(2 * first, 2 * many)], dst.at[pl.ds(2 * (2 * n + first), 2 * many)])
    if edged:
        for m, dst in enumerate((kb, vb)):
            copy(edge.at[m, :, pl.ds(chunk * heads, heads)], dst.at[pl.ds(2 * EDGE, 2)])
    for c in copies[:len(sets)]:
        c.wait()
    for n in range(len(sets)):
        ints[pl.ds(8 * n, 8), :] = marks[n].astype(F32)[0:8].astype(jnp.int32)
    tables = pltpu.make_async_copy(ints, table, table_sem)
    tables.start()
    tables.wait()
    for c in copies[len(sets):]:
        c.wait()

    for n, (dh, window, far) in enumerate(sets):
        asker = height - dh
        there = (asker >= 0) & (asker < HA)

        def one_tile(tile, carry):
            frame, col = tile // 2, tile % 2
            count = jnp.int32(0)
            if window:
                for df in range(3):
                    near = 2 * shard + frame + df - 1
                    inside = there & (near >= 0) & (near < 2 * TA)
                    at = 2 * tx + frame + df - 1
                    piece = (at + 2 * SIDE) // 2 - tx
                    slot = 2 * (piece & (SIDE - 1)) + (at & 1)
                    slot = jnp.where((at < 0) | (at >= 2 * SIDE), EDGE, slot)
                    for kw in range(2):
                        number = df * 9 + (dh + 1) * 3 + (kw - col + 1)
                        used = (table[8 * n + tile, number] == 1) | ((dh == 0) & (number == 13))
                        listed[count] = slot * 2 + kw
                        count = count + (used & inside).astype(jnp.int32)
            if far:
                for j in range(SEL):
                    owner = table[8 * n + tile, CHOSEN + j]
                    piece = (owner + SIDE - tx) & (SIDE - 1)
                    listed[count] = (piece * 2 + frame) * 2 + col
                    count = count + (owner // SIDE == ty).astype(jnp.int32)
            listed[count] = listed[0]
            attend_tile(heads, tile, count, listed, q_bufs[n], kb, vb, outs[n], a_ref)
            return carry

        lax.fori_loop(0, 4, one_tile, 0)


def call_attend(heads, chunk, place, sets, queries, pieces, held, edge, earlier=()):
    anywhere = pl.BlockSpec(memory_space=pl.ANY)
    smem = pl.BlockSpec(memory_space=pltpu.SMEM)
    keys = pltpu.VMEM((18, heads, TILE, TILE), BF16)
    operands = list(queries)
    for piece, pair in zip(pieces, held):
        operands += list(pair) if piece else []
    operands += [] if edge is None else [edge]
    operands += list(earlier)
    count = 2 * len(sets) + 2 * sum(piece is not None for piece in pieces) + 2 * (edge is not None)
    rows = 4 * (heads * TILE + STAT)
    return pl.pallas_call(
        functools.partial(attend_kernel, heads, chunk, sets, pieces, edge is not None, len(earlier)),
        out_shape=[jax.ShapeDtypeStruct((rows, TILE), BF16)] * len(sets),
        in_specs=[smem] + [anywhere] * len(operands),
        out_specs=[pl.BlockSpec(memory_space=pltpu.VMEM)] * len(sets),
        scratch_shapes=[pltpu.VMEM((4, heads, TILE, TILE), BF16) for _ in sets]
        + [keys, keys, pltpu.VMEM((len(sets), TABLE, TILE), BF16)]
        + [pltpu.VMEM((8 * len(sets), TILE), jnp.int32), pltpu.SMEM((8 * len(sets), TILE), jnp.int32)]
        + [pltpu.SMEM((16,), jnp.int32), pltpu.VMEM((heads, TILE, TILE), F32)]
        + [pltpu.SemaphoreType.DMA((count,)), pltpu.SemaphoreType.DMA],
        compiler_params=pltpu.CompilerParams(vmem_limit_bytes=VMEM_LIMIT),
    )(place, *operands)


def arrange_kernel(heads, place, chosen, window, q_in, k_in, v_in, *refs):
    outs, (q, k, v, marks, sems) = refs[:-5], refs[-5:]
    q_out, edge, both = outs[0], outs[1], outs[2:]
    copies = [pltpu.make_async_copy(src, dst, sems.at[n]) for n, (src, dst) in enumerate(((k_in, k), (v_in, v), (q_in, q)))]
    for c in copies:
        c.start()
    marks[...] = jnp.zeros_like(marks)
    marks[pl.ds(0, 4), pl.ds(0, 27)] = window[...].astype(F32)
    marks[pl.ds(0, 4), pl.ds(CHOSEN, SEL)] = chosen[...].astype(F32)
    q_out[4, 0, pl.ds(0, TABLE)] = marks[...].astype(BF16)
    per = heads // CHUNKS
    tiles = [(tile, h, h // per, h % per, pl.ds(h * HEAD, HEAD)) for tile in range(4) for h in range(heads)]
    copies[0].wait()
    for tile, h, chunk, at, lanes in tiles:
        both[chunk][0, tile, at] = k[tile // 2, :, tile % 2, :, lanes].reshape(TILE, HEAD)
    copies[1].wait()
    for tile, h, chunk, at, lanes in tiles:
        both[chunk][1, tile, at] = v[tile // 2, :, tile % 2, :, lanes].reshape(TILE, HEAD).T
    copies[2].wait()
    for tile, h, chunk, at, lanes in tiles:
        q_out[tile, h] = q[tile // 2, :, tile % 2, :, lanes].reshape(TILE, HEAD)
    first = jnp.where(place[0] == 0, 0, 2)
    for chunk in range(CHUNKS):
        for n in range(2):
            for col in range(2):
                edge[n, col, pl.ds(chunk * per, per)] = both[chunk][n, first + col]


def tie_kernel(*refs):
    del refs


def tie(arrays, earlier):
    anywhere = pl.BlockSpec(memory_space=pl.ANY)
    return pl.pallas_call(
        tie_kernel,
        out_shape=[jax.ShapeDtypeStruct(a.shape, a.dtype) for a in arrays],
        in_specs=[anywhere] * (len(arrays) + len(earlier)),
        out_specs=[anywhere] * len(arrays),
        input_output_aliases={n: n for n in range(len(arrays))},
    )(*arrays, *earlier)


def combine_kernel(heads, parts, place, *refs):
    sources, out = refs[:-1], refs[-1]
    height = place[2]
    there = {parts - 2: height > 0, parts - 1: height < HA - 1}
    for chunk in range(CHUNKS):
        mine = sources[chunk * 2 * parts:(chunk + 1) * 2 * parts]
        tokens, stats = mine[:parts], mine[parts:]
        logs = []
        for n in range(parts):
            s = stats[n][...].astype(F32)
            log = s[0:8] + s[8:16] + s[16:24]
            logs.append(jnp.where(there[n], log, NONE) if n in there else log)
        top = functools.reduce(jnp.maximum, logs)
        raised = [jnp.exp2(log - top) for log in logs]
        under = 1.0 / functools.reduce(jnp.add, raised)
        weights = [r * under for r in raised]
        for h in range(heads):
            terms = [weights[n][h:h + 1] * tokens[n][pl.ds(h * TILE, TILE), :].astype(F32) for n in range(parts)]
            mixed = functools.reduce(jnp.add, terms).T.astype(BF16)
            lanes = pl.ds((chunk * heads + h) * HEAD, HEAD)
            out[0, :, 0, :, lanes] = mixed.reshape(4, 32, HEAD)


def body(query, keys, values, selected, window_mask):
    frames, rows, cols, channels = query.shape
    heads = channels // HEAD // CHUNKS
    shard = lax.axis_index("ta")
    height = lax.axis_index("ha")
    tx, ty = shard % SIDE, shard // SIDE
    place = jnp.stack([tx, ty, height]).astype(jnp.int32)
    right, left, up, down = along_x(1), along_x(-1), along_y(1), along_y(-1)
    opposite = along_y(2)
    ends = [(SIDE * y + 3, SIDE * y + 4) for y in range(SIDE - 1)]
    ends = ends + [(b, a) for a, b in ends]
    higher = [(i, i + 1) for i in range(HA - 1)]
    lower = [(b, a) for a, b in higher]

    def permute(array, pairs, axis="ta"):
        return lax.ppermute(array, axis, pairs)

    smem, vmem, anywhere = [pl.BlockSpec(memory_space=m) for m in (pltpu.SMEM, pltpu.VMEM, pl.ANY)]
    blocks = [a.reshape(frames, rows, 2, 32, channels) for a in (query, keys, values)]
    q, edge, *both = pl.pallas_call(
        functools.partial(arrange_kernel, heads * CHUNKS),
        out_shape=[jax.ShapeDtypeStruct((5, heads * CHUNKS, TILE, TILE), BF16)]
        + [jax.ShapeDtypeStruct((2, 2, heads * CHUNKS, TILE, TILE), BF16)]
        + [jax.ShapeDtypeStruct((2, 4, heads, TILE, TILE), BF16)] * CHUNKS,
        in_specs=[smem, vmem, vmem] + [anywhere] * 3,
        out_specs=[vmem] * (2 + CHUNKS),
        scratch_shapes=[pltpu.VMEM(blocks[0].shape, BF16) for _ in range(3)]
        + [pltpu.VMEM((TABLE, TILE), F32), pltpu.SemaphoreType.DMA((3,))],
        compiler_params=pltpu.CompilerParams(vmem_limit_bytes=60 * 1024 * 1024),
    )(place, selected.reshape(4, SEL), window_mask.reshape(4, 27), *blocks)

    from_left = [permute(b, right) for b in both]
    from_right = [permute(b, left) for b in both]
    far_k = [permute(b[0], right) for b in from_left]
    far_v = [permute(b[1], left) for b in from_right]
    q1, q3 = permute(q, up), permute(q, down)
    q_low = permute(q, higher, "ha")
    again, edge = tie((q, edge), (q1, q3, q_low))
    q_high = permute(again, lower, "ha")
    q2 = permute(again, opposite)
    edge = permute(edge, ends)

    partial = []
    whole = ((0, 2),) * SIDE
    for c in range(CHUNKS):
        held = ((both[c],) * 2, (from_right[c],) * 2, (far_k[c], far_v[c]), (from_left[c],) * 2)
        for_low, for_high = call_attend(
            heads, c, place, ((1, True, False), (-1, True, False)), (q_low, q_high),
            ((0, 2), (0, 1), None, (1, 1)), held, edge,
        )
        o1, o2, o3 = call_attend(heads, c, place, ((0, False, True),) * 3, (q1, q2, q3), whole, held, None)
        f2, f1, f3 = permute(o2, opposite), permute(o1, down), permute(o3, up)
        for_low, for_high = tie((for_low, for_high), (o1,))
        from_high, from_low = permute(for_low, lower, "ha"), permute(for_high, higher, "ha")
        (mine,) = call_attend(heads, c, place, ((0, True, True),), (q,), whole, held, edge, (o1,))
        partial.append([mine, f1, f2, f3, from_low, from_high])

    count = len(partial[0])
    token_spec = pl.BlockSpec((heads * TILE, TILE), lambda t: (t, 0))
    stat_spec = pl.BlockSpec((STAT, TILE), lambda t: (4 * heads * TILE // STAT + t, 0))
    out = pl.pallas_call(
        functools.partial(combine_kernel, heads, count),
        out_shape=jax.ShapeDtypeStruct((frames, rows, 2, 32, channels), BF16),
        grid=(4,),
        in_specs=[pl.BlockSpec(memory_space=pltpu.SMEM)] + ([token_spec] * count + [stat_spec] * count) * CHUNKS,
        out_specs=pl.BlockSpec((1, rows, 1, 32, channels), lambda t: (t // 2, 0, t % 2, 0, 0)),
        compiler_params=pltpu.CompilerParams(vmem_limit_bytes=VMEM_LIMIT),
    )(place, *[a for some in partial for a in some + some])
    return out.reshape(frames, rows, cols, channels)


def solution(mesh):
    block = P("ta", "ha", None, "hd")
    table = P("ta", "ha", None, None)
    return jax.shard_map(
        body, mesh=mesh, in_specs=(block, block, block, table, table), out_specs=block, check_vma=False
    )
```

time: 368 us -> 149 us (0.40)
  the two profiles are of different devices: /device:TPU:1 before, /device:TPU:175 now
where the time goes in v2:
time: 149 us; the launch traced here: 148 us
  waiting for transfers between devices  61.7 us (41%)
  Pallas kernels  42.5 us (29%)
  starting transfers between devices  31.3 us (21%)
  local copies, waits for them, and re-layouts  11.2 us (8%)
    ppermute x15, waiting for transfers between devices, permute(): return lax.ppermute(array, axis, pairs)  61.7 us
    pallas_call x3, Pallas kernels, call_attend(): pl.pallas_call(functools.partial(attend_kernel, heads, chunk, sets, piece...  34.2 us
    ppermute x15, starting transfers between devices, permute(): return lax.ppermute(array, axis, pairs)  31.3 us
    unnamed x29, local copies, waits for them, and re-layouts  9.99 us
    pallas_call x1, Pallas kernels, body(): pl.pallas_call(functools.partial(arrange_kernel, heads * CHUNKS), out_sha...  4.31 us
    pallas_call x1, Pallas kernels, body(): pl.pallas_call(functools.partial(combine_kernel, heads, count), out_shape...  3.94 us
  transfers between devices with their start and end apart: 15, of which 7 were waited for; matrix products, arithmetic and copies ran while one was open for 2% of the time, Pallas kernels for 17%

profile of v2, /device:TPU:175, one launch (start us, length us, event | category | flops | bytes accessed | tf_op | source)
XLA Modules:
  0.0 147.6 jit_solution(12271643768643203999)
XLA Ops:
  0.6 4.3 %shard_map.55 = (bf16[5,6,128,128]{3,2,1,0:T(8,128)(2,1)}, bf16[2,2,6,128,128]{4,3,2,1,0:T(8,128)(2,1)}, bf16[2,4,6,128,128]{4,3,2,1,0:T(8,128)(2,1)}) custom-call(s32[3]{0:T(128)} %pad_add_fusion.place, s32[4,4]{1,0:T(4,128)} %bitcast.16, s32[4,27]{1,0:T(4,128)} %bitcast.17, bf16[2,4,2,32,768]{4,3,2,1,0:T(8,128)(2,1)} %bitcast.13, ...), custom_call_target="tpu_custom_call" | custom-call | tf_op jit(solution)/shard_map/pallas_call | solution.py:297
  5.2 1.3 collective-permute-start
  6.5 4.2 %collective-permute-start.6 = (bf16[5,6,128,128]{3,2,1,0:T(8,128)(2,1)}, bf16[5,6,128,128]{3,2,1,0:T(8,128)(2,1)S(1)}, u32[]{:S(2)}, u32[]{:S(2)}) collective-permute-start(bf16[5,6,128,128]{3,2,1,0:T(8,128)(2,1)} %get-tuple-element.17.refs_0_), channel_id=1, source_target_pairs={{0,2},{2,4},{4,6},{6,8},{8,10},{10,12},{12,14},{1,3},{3,5},{5,7},{... | collective-permute-start | bytes 2949128 | tf_op jit(solution)/shard_map/ppermute | solution.py:293
  10.9 1.3 collective-permute-start.4
  12.2 2.3 %copy.10.refs_0_ = bf16[5,6,128,128]{3,2,1,0:T(8,128)(2,1)} copy(bf16[5,6,128,128]{3,2,1,0:T(8,128)(2,1)} %get-tuple-element.17.refs_0_) | data formatting | bytes 1966080
  14.5 17.7 %collective-permute-done.6.refs_4_.refs_0_ = bf16[5,6,128,128]{3,2,1,0:T(8,128)(2,1)S(1)} collective-permute-done((bf16[5,6,128,128]{3,2,1,0:T(8,128)(2,1)}, bf16[5,6,128,128]{3,2,1,0:T(8,128)(2,1)S(1)}, u32[]{:S(2)}, u32[]{:S(2)}) %collective-permute-start.6) | collective-permute-done | bytes 983072 | tf_op jit(solution)/shard_map/ppermute | solution.py:293
  32.2 2.0 %collective-permute-done.5.refs_3_.refs_2_ = bf16[5,6,128,128]{3,2,1,0:T(8,128)(2,1)S(1)} collective-permute-done((bf16[5,6,128,128]{3,2,1,0:T(8,128)(2,1)}, bf16[5,6,128,128]{3,2,1,0:T(8,128)(2,1)S(1)}, u32[]{:S(2)}, u32[]{:S(2)}) %collective-permute-start.5) | collective-permute-done | bytes 983072 | tf_op jit(solution)/shard_map/ppermute | solution.py:293
  34.2 1.5 collective-permute-done.4.refs_2_.refs_0_
  35.7 1.9 %collective-permute-start.12 = (bf16[5,6,128,128]{3,2,1,0:T(8,128)(2,1)}, bf16[5,6,128,128]{3,2,1,0:T(8,128)(2,1)S(1)}, u32[]{:S(2)}, u32[]{:S(2)}) collective-permute-start(bf16[5,6,128,128]{3,2,1,0:T(8,128)(2,1)} %get-tuple-element.21), channel_id=1, source_target_pairs={{2,0},{4,2},{6,4},{8,6},{10,8},{12,10},{14,12},{3,1},{5,3},{7,5},{... | collective-permute-start | bytes 2949128 | tf_op jit(solution)/shard_map/ppermute | solution.py:293
  37.6 2.8 %collective-permute-start.8 = (bf16[5,6,128,128]{3,2,1,0:T(8,128)(2,1)}, bf16[5,6,128,128]{3,2,1,0:T(8,128)(2,1)S(1)}, u32[]{:S(2)}, u32[]{:S(2)}) collective-permute-start(bf16[5,6,128,128]{3,2,1,0:T(8,128)(2,1)} %get-tuple-element.21), channel_id=1, source_target_pairs={{0,128},{16,144},{32,160},{48,176},{64,192},{80,208},{96,224},{112... | collective-permute-start | bytes 2949128 | tf_op jit(solution)/shard_map/ppermute | solution.py:293
  40.4 4.6 %collective-permute-start.7 = (bf16[2,2,6,128,128]{4,3,2,1,0:T(8,128)(2,1)}, bf16[2,2,6,128,128]{4,3,2,1,0:T(8,128)(2,1)S(1)}, u32[]{:S(2)}, u32[]{:S(2)}) collective-permute-start(bf16[2,2,6,128,128]{4,3,2,1,0:T(8,128)(2,1)} %get-tuple-element.20), channel_id=1, source_target_pairs={{48,64},{112,128},{176,192},{64,48},{128,112},{192,176},{49,65},{1... | collective-permute-start | bytes 2359304 | tf_op jit(solution)/shard_map/ppermute | solution.py:293
  46.5 1.2 slice_bitcast_fusion
  47.7 1.6 %collective-permute-start.3 = (bf16[4,6,128,128]{3,2,1,0:T(8,128)(2,1)S(1)}, bf16[4,6,128,128]{3,2,1,0:T(8,128)(2,1)S(1)}, u32[]{:S(2)}, u32[]{:S(2)}) collective-permute-start(bf16[4,6,128,128]{3,2,1,0:T(8,128)(2,1)S(1)} %slice_bitcast_fusion), channel_id=1, source_target_pairs={{0,48},{16,0},{32,16},{48,32},{64,112},{80,64},{96,80},{112,96},{1... | collective-permute-start | bytes 2359304 | tf_op jit(solution)/shard_map/ppermute | solution.py:293
  49.3 14.7 %collective-permute-done.7.refs_9_.refs_8_ = bf16[2,2,6,128,128]{4,3,2,1,0:T(8,128)(2,1)S(1)} collective-permute-done((bf16[2,2,6,128,128]{4,3,2,1,0:T(8,128)(2,1)}, bf16[2,2,6,128,128]{4,3,2,1,0:T(8,128)(2,1)S(1)}, u32[]{:S(2)}, u32[]{:S(2)}) %collective-permute-start.7) | collective-permute-done | bytes 786464 | tf_op jit(solution)/shard_map/ppermute | solution.py:293
  65.0 12.5 %shard_map.59 = (bf16[3200,128]{1,0:T(8,128)(2,1)S(1)}, bf16[3200,128]{1,0:T(8,128)(2,1)S(1)}) custom-call(s32[3]{0:T(128)S(1)} %copy-done.6, bf16[5,6,128,128]{3,2,1,0:T(8,128)(2,1)S(1)} %copy-done.1, bf16[5,6,128,128]{3,2,1,0:T(8,128)(2,1)} %copy-done.12, bf16[2,4,6,128,128]{4,3,2,1,0:T(8,128)(2,1)} %get-tuple-element.18.refs_3_.refs_4_.refs_1_.refs_2_, ...), custom_call_target="tpu_custom_call" | custom-call | tf_op jit(solution)/shard_map/pallas_call | solution.py:198
  80.3 9.7 %shard_map.57 = (bf16[3200,128]{1,0:T(8,128)(2,1)S(1)}, bf16[3200,128]{1,0:T(8,128)(2,1)S(1)}, bf16[3200,128]{1,0:T(8,128)(2,1)S(1)}) custom-call(s32[3]{0:T(128)S(1)} %copy-done.6, bf16[5,6,128,128]{3,2,1,0:T(8,128)(2,1)} %collective-permute-done.4.refs_2_.refs_0_, bf16[5,6,128,128]{3,2,1,0:T(8,128)(2,1)} %copy-done.13, ...), custom_call_target="tpu_custom_call" | custom-call | tf_op jit(solution)/shard_map/pallas_call | solution.py:198
  92.8 4.3 %collective-permute-start.13 = (bf16[3200,128]{1,0:T(8,128)(2,1)}, bf16[3200,128]{1,0:T(8,128)(2,1)S(1)}, u32[]{:S(2)}, u32[]{:S(2)}) collective-permute-start(bf16[3200,128]{1,0:T(8,128)(2,1)} %get-tuple-element.27), channel_id=1, source_target_pairs={{0,2},{2,4},{4,6},{6,8},{8,10},{10,12},{12,14},{1,3},{3,5},{5,7},{... | collective-permute-start | bytes 2457608 | tf_op jit(solution)/shard_map/ppermute | solution.py:293
  97.1 7.0 %collective-permute-start.14 = (bf16[3200,128]{1,0:T(8,128)(2,1)}, bf16[3200,128]{1,0:T(8,128)(2,1)S(1)}, u32[]{:S(2)}, u32[]{:S(2)}) collective-permute-start(bf16[3200,128]{1,0:T(8,128)(2,1)} %get-tuple-element.28), channel_id=1, source_target_pairs={{2,0},{4,2},{6,4},{8,6},{10,8},{12,10},{14,12},{3,1},{5,3},{7,5},{... | collective-permute-start | bytes 2457608 | tf_op jit(solution)/shard_map/ppermute | solution.py:293
  104.3 1.4 collective-permute-start.9
  105.8 12.1 %shard_map.58.refs_0_.refs_6_ = bf16[3200,128]{1,0:T(8,128)(2,1)S(1)} custom-call(s32[3]{0:T(128)S(1)} %copy-done.6, bf16[5,6,128,128]{3,2,1,0:T(8,128)(2,1)} %get-tuple-element.17.refs_0_, bf16[2,4,6,128,128]{4,3,2,1,0:T(8,128)(2,1)} %get-tuple-element.18.refs_3_.refs_4_.refs_1_.refs_2_, ...), custom_call_target="tpu_custom_call" | custom-call | tf_op jit(solution)/shard_map/pallas_call | solution.py:198
  117.8 4.0 %collective-permute-done.10.refs_2_.refs_8_ = bf16[3200,128]{1,0:T(8,128)(2,1)S(1)} collective-permute-done((bf16[3200,128]{1,0:T(8,128)(2,1)}, bf16[3200,128]{1,0:T(8,128)(2,1)S(1)}, u32[]{:S(2)}, u32[]{:S(2)}) %collective-permute-start.10) | collective-permute-done | bytes 819232 | tf_op jit(solution)/shard_map/ppermute | solution.py:293
  121.9 18.2 %collective-permute-done.11.refs_3_.refs_9_ = bf16[3200,128]{1,0:T(8,128)(2,1)S(1)} collective-permute-done((bf16[3200,128]{1,0:T(8,128)(2,1)}, bf16[3200,128]{1,0:T(8,128)(2,1)S(1)}, u32[]{:S(2)}, u32[]{:S(2)}) %collective-permute-start.11) | collective-permute-done | bytes 819232 | tf_op jit(solution)/shard_map/ppermute | solution.py:293
  140.1 3.6 %collective-permute-done.9.refs_1_.refs_7_ = bf16[3200,128]{1,0:T(8,128)(2,1)S(1)} collective-permute-done((bf16[3200,128]{1,0:T(8,128)(2,1)S(1)}, bf16[3200,128]{1,0:T(8,128)(2,1)S(1)}, u32[]{:S(2)}, u32[]{:S(2)}) %collective-permute-start.9) | collective-permute-done | bytes 819232 | tf_op jit(solution)/shard_map/ppermute | solution.py:293
  143.6 3.9 %shard_map.61 = bf16[2,4,2,32,768]{4,3,2,1,0:T(8,128)(2,1)} custom-call(s32[3]{0:T(128)S(1)} %copy-done.6, bf16[3200,128]{1,0:T(8,128)(2,1)S(1)} %shard_map.58.refs_0_.refs_6_, bf16[3200,128]{1,0:T(8,128)(2,1)S(1)} %collective-permute-done.9.refs_1_.refs_7_, bf16[3200,128]{1,0:T(8,128)(2,1)S(1)} %collective-permute-done.10.refs_2_.refs_8_, ...), custom_call_target="tpu_custom_call" | custom-call | tf_op jit(solution)/shard_map/pallas_call | solution.py:338
  (45 shorter events, 9.3 us)
Async XLA Ops:
  4.9 40.1 %collective-permute-start.1 = (bf16[2,4,6,128,128]{4,3,2,1,0:T(8,128)(2,1)}, bf16[2,4,6,128,128]{4,3,2,1,0:T(8,128)(2,1)S(1)}, u32[]{:S(2)}, u32[]{:S(2)}) collective-permute-start(bf16[2,4,6,128,128]{4,3,2,1,0:T(8,128)(2,1)} %get-tuple-element.18.refs_3_.refs_4_.refs_1_.refs_2_), channel_id=1, source_target_pairs={{0,16},{16,32},{32,48},{48,0},{64,80},{80,96},{96,112},{112,64},{1... | collective-permute-start | bytes 4718600 | tf_op jit(solution)/shard_map/ppermute | solution.py:293
  5.2 41.3 %collective-permute-start = (bf16[2,4,6,128,128]{4,3,2,1,0:T(8,128)(2,1)}, bf16[2,4,6,128,128]{4,3,2,1,0:T(8,128)(2,1)}, u32[]{:S(2)}, u32[]{:S(2)}) collective-permute-start(bf16[2,4,6,128,128]{4,3,2,1,0:T(8,128)(2,1)} %get-tuple-element.18.refs_3_.refs_4_.refs_1_.refs_2_), channel_id=1, source_target_pairs={{0,48},{16,0},{32,16},{48,32},{64,112},{80,64},{96,80},{112,96},{1... | collective-permute-start | bytes 4718600 | tf_op jit(solution)/shard_map/ppermute | solution.py:293
  6.5 25.8 %collective-permute-start.6 = (bf16[5,6,128,128]{3,2,1,0:T(8,128)(2,1)}, bf16[5,6,128,128]{3,2,1,0:T(8,128)(2,1)S(1)}, u32[]{:S(2)}, u32[]{:S(2)}) collective-permute-start(bf16[5,6,128,128]{3,2,1,0:T(8,128)(2,1)} %get-tuple-element.17.refs_0_), channel_id=1, source_target_pairs={{0,2},{2,4},{4,6},{6,8},{8,10},{10,12},{12,14},{1,3},{3,5},{5,7},{... | collective-permute-start | bytes 2949128 | tf_op jit(solution)/shard_map/ppermute | solution.py:293
  10.7 23.6 %collective-permute-start.5 = (bf16[5,6,128,128]{3,2,1,0:T(8,128)(2,1)}, bf16[5,6,128,128]{3,2,1,0:T(8,128)(2,1)S(1)}, u32[]{:S(2)}, u32[]{:S(2)}) collective-permute-start(bf16[5,6,128,128]{3,2,1,0:T(8,128)(2,1)} %get-tuple-element.17.refs_0_), channel_id=1, source_target_pairs={{0,192},{16,208},{32,224},{48,240},{64,0},{80,16},{96,32},{112,48}... | collective-permute-start | bytes 2949128 | tf_op jit(solution)/shard_map/ppermute | solution.py:293
  10.9 24.8 %collective-permute-start.4 = (bf16[5,6,128,128]{3,2,1,0:T(8,128)(2,1)}, bf16[5,6,128,128]{3,2,1,0:T(8,128)(2,1)}, u32[]{:S(2)}, u32[]{:S(2)}) collective-permute-start(bf16[5,6,128,128]{3,2,1,0:T(8,128)(2,1)} %get-tuple-element.17.refs_0_), channel_id=1, source_target_pairs={{0,64},{16,80},{32,96},{48,112},{64,128},{80,144},{96,160},{112,17... | collective-permute-start | bytes 2949128 | tf_op jit(solution)/shard_map/ppermute | solution.py:293
  32.2 3.5 %copy-start = (bf16[5,6,128,128]{3,2,1,0:T(8,128)(2,1)}, bf16[5,6,128,128]{3,2,1,0:T(8,128)(2,1)S(1)}, u32[]{:S(2)}) copy-start(bf16[5,6,128,128]{3,2,1,0:T(8,128)(2,1)S(1)} %collective-permute-done.6.refs_4_.refs_0_) | copy-start | bytes 2949124
  34.2 1.5 %copy-start.10 = (bf16[5,6,128,128]{3,2,1,0:T(8,128)(2,1)}, bf16[5,6,128,128]{3,2,1,0:T(8,128)(2,1)S(1)}, u32[]{:S(2)}) copy-start(bf16[5,6,128,128]{3,2,1,0:T(8,128)(2,1)S(1)} %collective-permute-done.5.refs_3_.refs_2_) | copy-start | bytes 2949124
  35.7 28.3 %collective-permute-start.12 = (bf16[5,6,128,128]{3,2,1,0:T(8,128)(2,1)}, bf16[5,6,128,128]{3,2,1,0:T(8,128)(2,1)S(1)}, u32[]{:S(2)}, u32[]{:S(2)}) collective-permute-start(bf16[5,6,128,128]{3,2,1,0:T(8,128)(2,1)} %get-tuple-element.21), channel_id=1, source_target_pairs={{2,0},{4,2},{6,4},{8,6},{10,8},{12,10},{14,12},{3,1},{5,3},{7,5},{... | collective-permute-start | bytes 2949128 | tf_op jit(solution)/shard_map/ppermute | solution.py:293
  37.6 41.6 %collective-permute-start.8 = (bf16[5,6,128,128]{3,2,1,0:T(8,128)(2,1)}, bf16[5,6,128,128]{3,2,1,0:T(8,128)(2,1)S(1)}, u32[]{:S(2)}, u32[]{:S(2)}) collective-permute-start(bf16[5,6,128,128]{3,2,1,0:T(8,128)(2,1)} %get-tuple-element.21), channel_id=1, source_target_pairs={{0,128},{16,144},{32,160},{48,176},{64,192},{80,208},{96,224},{112... | collective-permute-start | bytes 2949128 | tf_op jit(solution)/shard_map/ppermute | solution.py:293
  40.4 24.6 %copy-start.1 = (bf16[5,6,128,128]{3,2,1,0:T(8,128)(2,1)S(1)}, bf16[5,6,128,128]{3,2,1,0:T(8,128)(2,1)}, u32[]{:S(2)}) copy-start(bf16[5,6,128,128]{3,2,1,0:T(8,128)(2,1)} %copy-done) | copy-start | bytes 2949124
  40.4 24.6 %copy-start.6 = (s32[3]{0:T(128)S(1)}, s32[3]{0:T(128)}, u32[]{:S(2)}) copy-start(s32[3]{0:T(128)} %pad_add_fusion.place) | copy-start | bytes 40
  40.4 23.6 %collective-permute-start.7 = (bf16[2,2,6,128,128]{4,3,2,1,0:T(8,128)(2,1)}, bf16[2,2,6,128,128]{4,3,2,1,0:T(8,128)(2,1)S(1)}, u32[]{:S(2)}, u32[]{:S(2)}) collective-permute-start(bf16[2,2,6,128,128]{4,3,2,1,0:T(8,128)(2,1)} %get-tuple-element.20), channel_id=1, source_target_pairs={{48,64},{112,128},{176,192},{64,48},{128,112},{192,176},{49,65},{1... | collective-permute-start | bytes 2359304 | tf_op jit(solution)/shard_map/ppermute | solution.py:293
  45.1 1.2 copy-start.9
  46.3 33.0 %collective-permute-start.2 = (bf16[4,6,128,128]{3,2,1,0:T(8,128)(2,1)S(1)}, bf16[4,6,128,128]{3,2,1,0:T(8,128)(2,1)S(1)}, u32[]{:S(2)}, u32[]{:S(2)}) collective-permute-start(bf16[4,6,128,128]{3,2,1,0:T(8,128)(2,1)S(1)} %slice_bitcast_fusion.1), channel_id=1, source_target_pairs={{0,16},{16,32},{32,48},{48,0},{64,80},{80,96},{96,112},{112,64},{1... | collective-permute-start | bytes 2359304 | tf_op jit(solution)/shard_map/ppermute | solution.py:293
  47.7 31.6 %collective-permute-start.3 = (bf16[4,6,128,128]{3,2,1,0:T(8,128)(2,1)S(1)}, bf16[4,6,128,128]{3,2,1,0:T(8,128)(2,1)S(1)}, u32[]{:S(2)}, u32[]{:S(2)}) collective-permute-start(bf16[4,6,128,128]{3,2,1,0:T(8,128)(2,1)S(1)} %slice_bitcast_fusion), channel_id=1, source_target_pairs={{0,48},{16,0},{32,16},{48,32},{64,112},{80,64},{96,80},{112,96},{1... | collective-permute-start | bytes 2359304 | tf_op jit(solution)/shard_map/ppermute | solution.py:293
  79.3 1.0 copy-start.13
  90.0 1.0 copy-start.2
  92.8 11.5 %copy-start.3 = (bf16[3200,128]{1,0:T(8,128)(2,1)S(1)}, bf16[3200,128]{1,0:T(8,128)(2,1)}, u32[]{:S(2)}) copy-start(bf16[3200,128]{1,0:T(8,128)(2,1)} %copy-done.2) | copy-start | bytes 2457604
  92.8 25.0 %collective-permute-start.13 = (bf16[3200,128]{1,0:T(8,128)(2,1)}, bf16[3200,128]{1,0:T(8,128)(2,1)S(1)}, u32[]{:S(2)}, u32[]{:S(2)}) collective-permute-start(bf16[3200,128]{1,0:T(8,128)(2,1)} %get-tuple-element.27), channel_id=1, source_target_pairs={{0,2},{2,4},{4,6},{6,8},{8,10},{10,12},{12,14},{1,3},{3,5},{5,7},{... | collective-permute-start | bytes 2457608 | tf_op jit(solution)/shard_map/ppermute | solution.py:293
  97.1 20.8 %collective-permute-start.14 = (bf16[3200,128]{1,0:T(8,128)(2,1)}, bf16[3200,128]{1,0:T(8,128)(2,1)S(1)}, u32[]{:S(2)}, u32[]{:S(2)}) collective-permute-start(bf16[3200,128]{1,0:T(8,128)(2,1)} %get-tuple-element.28), channel_id=1, source_target_pairs={{2,0},{4,2},{6,4},{8,6},{10,8},{12,10},{14,12},{3,1},{5,3},{7,5},{... | collective-permute-start | bytes 2457608 | tf_op jit(solution)/shard_map/ppermute | solution.py:293
  104.1 17.8 %collective-permute-start.10 = (bf16[3200,128]{1,0:T(8,128)(2,1)}, bf16[3200,128]{1,0:T(8,128)(2,1)S(1)}, u32[]{:S(2)}, u32[]{:S(2)}) collective-permute-start(bf16[3200,128]{1,0:T(8,128)(2,1)} %copy-done.8), channel_id=1, source_target_pairs={{0,128},{16,144},{32,160},{48,176},{64,192},{80,208},{96,224},{112... | collective-permute-start | bytes 2457608 | tf_op jit(solution)/shard_map/ppermute | solution.py:293
  104.2 35.9 %collective-permute-start.11 = (bf16[3200,128]{1,0:T(8,128)(2,1)}, bf16[3200,128]{1,0:T(8,128)(2,1)S(1)}, u32[]{:S(2)}, u32[]{:S(2)}) collective-permute-start(bf16[3200,128]{1,0:T(8,128)(2,1)} %copy-done.7), channel_id=1, source_target_pairs={{0,64},{16,80},{32,96},{48,112},{64,128},{80,144},{96,160},{112,17... | collective-permute-start | bytes 2457608 | tf_op jit(solution)/shard_map/ppermute | solution.py:293
  104.3 39.3 %collective-permute-start.9 = (bf16[3200,128]{1,0:T(8,128)(2,1)S(1)}, bf16[3200,128]{1,0:T(8,128)(2,1)S(1)}, u32[]{:S(2)}, u32[]{:S(2)}) collective-permute-start(bf16[3200,128]{1,0:T(8,128)(2,1)S(1)} %copy-done.3), channel_id=1, source_target_pairs={{0,192},{16,208},{32,224},{48,240},{64,0},{80,16},{96,32},{112,48}... | collective-permute-start | bytes 2457608 | tf_op jit(solution)/shard_map/ppermute | solution.py:293
  117.8 25.8 %copy-start.11 = (bf16[3200,128]{1,0:T(8,128)(2,1)}, bf16[3200,128]{1,0:T(8,128)(2,1)S(1)}, u32[]{:S(2)}) copy-start(bf16[3200,128]{1,0:T(8,128)(2,1)S(1)} %collective-permute-done.14.refs_5_.refs_11_) | copy-start | bytes 2457604
  (5 other events, 4.6 us)

commit v3 on v2

--- a/solution.py
+++ b/solution.py
@@ -21,7 +21,7 @@
 NONE = -1e30
 SCALE = float(HEAD ** -0.5)
 LOG2E = float(np.log2(np.e))
-VMEM_LIMIT = 50 * 1024 * 1024
+VMEM_LIMIT = 60 * 1024 * 1024
 F32 = jnp.float32
 BF16 = jnp.bfloat16
 
@@ -109,17 +109,19 @@
         write([(top, total, a_ref[h]) for h, (top, total) in enumerate(ends)])
 
 
-def attend_kernel(heads, chunk, sets, pieces, edged, earlier, place, *refs):
+def attend_kernel(heads, chunk, sets, pieces, edged, earlier, together, place, *refs):
     refs = list(refs)
     queries = [refs.pop(0) for _ in sets]
     held = [[refs.pop(0), refs.pop(0)] if piece else None for piece in pieces]
     edge = refs.pop(0) if edged else None
     del refs[:earlier]
-    outs = [refs.pop(0) for _ in sets]
+    outs = [refs.pop(0) for _ in range(1 if together else len(sets))]
     q_bufs = [refs.pop(0) for _ in sets]
     kb, vb, marks, ints, table, listed, a_ref, sems, table_sem = refs
     tx, ty, height = place[0], place[1], place[2]
     shard = ty * SIDE + tx
+    if together:
+        outs = [outs[0].at[(ty + SIDE - n) & (SIDE - 1)] for n in range(SIDE)]
     copies = []
 
     def copy(src, dst):
@@ -184,7 +186,7 @@
         lax.fori_loop(0, 4, one_tile, 0)
 
 
-def call_attend(heads, chunk, place, sets, queries, pieces, held, edge, earlier=()):
+def call_attend(heads, chunk, place, sets, queries, pieces, held, edge, earlier=(), together=False):
     anywhere = pl.BlockSpec(memory_space=pl.ANY)
     smem = pl.BlockSpec(memory_space=pltpu.SMEM)
     keys = pltpu.VMEM((18, heads, TILE, TILE), BF16)
@@ -196,10 +198,12 @@
     count = 2 * len(sets) + 2 * sum(piece is not None for piece in pieces) + 2 * (edge is not None)
     rows = 4 * (heads * TILE + STAT)
     return pl.pallas_call(
-        functools.partial(attend_kernel, heads, chunk, sets, pieces, edge is not None, len(earlier)),
-        out_shape=[jax.ShapeDtypeStruct((rows, TILE), BF16)] * len(sets),
+        functools.partial(attend_kernel, heads, chunk, sets, pieces, edge is not None, len(earlier), together),
+        out_shape=[jax.ShapeDtypeStruct((SIDE, rows, TILE), BF16)]
+        if together
+        else [jax.ShapeDtypeStruct((rows, TILE), BF16)] * len(sets),
         in_specs=[smem] + [anywhere] * len(operands),
-        out_specs=[pl.BlockSpec(memory_space=pltpu.VMEM)] * len(sets),
+        out_specs=[pl.BlockSpec(memory_space=pltpu.VMEM)] * (1 if together else len(sets)),
         scratch_shapes=[pltpu.VMEM((4, heads, TILE, TILE), BF16) for _ in sets]
         + [keys, keys, pltpu.VMEM((len(sets), TABLE, TILE), BF16)]
         + [pltpu.VMEM((8 * len(sets), TILE), jnp.int32), pltpu.SMEM((8 * len(sets), TILE), jnp.int32)]
@@ -209,9 +213,9 @@
     )(place, *operands)
 
 
-def arrange_kernel(heads, place, chosen, window, q_in, k_in, v_in, *refs):
+def arrange_kernel(heads, chosen, window, q_in, k_in, v_in, *refs):
     outs, (q, k, v, marks, sems) = refs[:-5], refs[-5:]
-    q_out, edge, both = outs[0], outs[1], outs[2:]
+    q_out, both = outs[0], outs[1:]
     copies = [pltpu.make_async_copy(src, dst, sems.at[n]) for n, (src, dst) in enumerate(((k_in, k), (v_in, v), (q_in, q)))]
     for c in copies:
         c.start()
@@ -230,11 +234,6 @@
     copies[2].wait()
     for tile, h, chunk, at, lanes in tiles:
         q_out[tile, h] = q[tile // 2, :, tile % 2, :, lanes].reshape(TILE, HEAD)
-    first = jnp.where(place[0] == 0, 0, 2)
-    for chunk in range(CHUNKS):
-        for n in range(2):
-            for col in range(2):
-                edge[n, col, pl.ds(chunk * per, per)] = both[chunk][n, first + col]
 
 
 def tie_kernel(*refs):
@@ -284,62 +283,68 @@
     place = jnp.stack([tx, ty, height]).astype(jnp.int32)
     right, left, up, down = along_x(1), along_x(-1), along_y(1), along_y(-1)
     opposite = along_y(2)
-    ends = [(SIDE * y + 3, SIDE * y + 4) for y in range(SIDE - 1)]
-    ends = ends + [(b, a) for a, b in ends]
+    columns = [[SIDE * y + x for y in range(SIDE)] for x in range(SIDE)]
+    ends = [(SIDE * y, SIDE * y + SIDE) for y in range(SIDE - 1)]
+    ends = ends + [(SIDE * y + SIDE + 3, SIDE * y + 3) for y in range(SIDE - 1)]
     higher = [(i, i + 1) for i in range(HA - 1)]
     lower = [(b, a) for a, b in higher]
 
     def permute(array, pairs, axis="ta"):
         return lax.ppermute(array, axis, pairs)
 
-    smem, vmem, anywhere = [pl.BlockSpec(memory_space=m) for m in (pltpu.SMEM, pltpu.VMEM, pl.ANY)]
+    vmem, anywhere = [pl.BlockSpec(memory_space=m) for m in (pltpu.VMEM, pl.ANY)]
     blocks = [a.reshape(frames, rows, 2, 32, channels) for a in (query, keys, values)]
-    q, edge, *both = pl.pallas_call(
+    q, *both = pl.pallas_call(
         functools.partial(arrange_kernel, heads * CHUNKS),
         out_shape=[jax.ShapeDtypeStruct((5, heads * CHUNKS, TILE, TILE), BF16)]
-        + [jax.ShapeDtypeStruct((2, 2, heads * CHUNKS, TILE, TILE), BF16)]
         + [jax.ShapeDtypeStruct((2, 4, heads, TILE, TILE), BF16)] * CHUNKS,
-        in_specs=[smem, vmem, vmem] + [anywhere] * 3,
-        out_specs=[vmem] * (2 + CHUNKS),
+        in_specs=[vmem, vmem] + [anywhere] * 3,
+        out_specs=[vmem] * (1 + CHUNKS),
         scratch_shapes=[pltpu.VMEM(blocks[0].shape, BF16) for _ in range(3)]
         + [pltpu.VMEM((TABLE, TILE), F32), pltpu.SemaphoreType.DMA((3,))],
-        compiler_params=pltpu.CompilerParams(vmem_limit_bytes=60 * 1024 * 1024),
-    )(place, selected.reshape(4, SEL), window_mask.reshape(4, 27), *blocks)
-
-    from_left = [permute(b, right) for b in both]
-    from_right = [permute(b, left) for b in both]
+        compiler_params=pltpu.CompilerParams(vmem_limit_bytes=VMEM_LIMIT),
+    )(selected.reshape(4, SEL), window_mask.reshape(4, 27), *blocks)
+
+    q1, q2, q3 = permute(q, up), permute(q, opposite), permute(q, down)
+    (q,) = tie((q,), (q1, q3))
+    q_low, q_high = permute(q, higher, "ha"), permute(q, lower, "ha")
+    from_left, from_right = [], []
+    for c in range(CHUNKS):
+        if c:
+            (both[c],) = tie((both[c],), (from_left[-1], from_right[-1]))
+        from_left.append(permute(both[c], right))
+        from_right.append(permute(both[c], left))
     far_k = [permute(b[0], right) for b in from_left]
     far_v = [permute(b[1], left) for b in from_right]
-    q1, q3 = permute(q, up), permute(q, down)
-    q_low = permute(q, higher, "ha")
-    again, edge = tie((q, edge), (q1, q3, q_low))
-    q_high = permute(again, lower, "ha")
-    q2 = permute(again, opposite)
-    edge = permute(edge, ends)
+    edge = [jnp.where(tx == 0, a[:, 2:], b[:, :2]) for a, b in zip(from_left, from_right)]
+    edge = permute(jnp.concatenate(edge, 2), ends)
 
     partial = []
     whole = ((0, 2),) * SIDE
     for c in range(CHUNKS):
         held = ((both[c],) * 2, (from_right[c],) * 2, (far_k[c], far_v[c]), (from_left[c],) * 2)
+        far_sets = ((0, False, True),) * SIDE
+        (parts,) = call_attend(heads, c, place, far_sets, (q, q1, q2, q3), whole, held, None, (edge,), True)
+        arrived = lax.all_to_all(parts, "ta", 0, 0, axis_index_groups=columns, tiled=True)
+        near = ((0, 2), (0, 1), None, (1, 1))
         for_low, for_high = call_attend(
-            heads, c, place, ((1, True, False), (-1, True, False)), (q_low, q_high),
-            ((0, 2), (0, 1), None, (1, 1)), held, edge,
+            heads, c, place, ((1, True, False), (-1, True, False)), (q_low, q_high), near, held, edge, (parts,)
         )
-        o1, o2, o3 = call_attend(heads, c, place, ((0, False, True),) * 3, (q1, q2, q3), whole, held, None)
-        f2, f1, f3 = permute(o2, opposite), permute(o1, down), permute(o3, up)
-        for_low, for_high = tie((for_low, for_high), (o1,))
         from_high, from_low = permute(for_low, lower, "ha"), permute(for_high, higher, "ha")
-        (mine,) = call_attend(heads, c, place, ((0, True, True),), (q,), whole, held, edge, (o1,))
-        partial.append([mine, f1, f2, f3, from_low, from_high])
+        (mine,) = call_attend(heads, c, place, ((0, True, False),), (q,), near, held, edge, (for_low,))
+        partial.append([arrived] * SIDE + [mine, from_low, from_high])
 
     count = len(partial[0])
-    token_spec = pl.BlockSpec((heads * TILE, TILE), lambda t: (t, 0))
-    stat_spec = pl.BlockSpec((STAT, TILE), lambda t: (4 * heads * TILE // STAT + t, 0))
+    tokens, stats = [], []
+    for n in range(count):
+        lead, at = ((None,), (n,)) if n < SIDE else ((), ())
+        tokens.append(pl.BlockSpec(lead + (heads * TILE, TILE), lambda t, at=at: at + (t, 0)))
+        stats.append(pl.BlockSpec(lead + (STAT, TILE), lambda t, at=at: at + (4 * heads * TILE // STAT + t, 0)))
     out = pl.pallas_call(
         functools.partial(combine_kernel, heads, count),
         out_shape=jax.ShapeDtypeStruct((frames, rows, 2, 32, channels), BF16),
         grid=(4,),
-        in_specs=[pl.BlockSpec(memory_space=pltpu.SMEM)] + ([token_spec] * count + [stat_spec] * count) * CHUNKS,
+        in_specs=[pl.BlockSpec(memory_space=pltpu.SMEM)] + (tokens + stats) * CHUNKS,
         out_specs=pl.BlockSpec((1, rows, 1, 32, channels), lambda t: (t // 2, 0, t % 2, 0, 0)),
         compiler_params=pltpu.CompilerParams(vmem_limit_bytes=VMEM_LIMIT),
     )(place, *[a for some in partial for a in some + some])

time: 149 us -> 175 us (1.17)
  the two profiles are of different devices: /device:TPU:175 before, /device:TPU:119 now
where the time goes in v3:
time: 175 us; the launch traced here: 173 us
  waiting for transfers between devices  87.4 us (50%)
  Pallas kernels  51.3 us (29%)
  starting transfers between devices  28.9 us (17%)
  local copies, waits for them, and re-layouts  3.63 us (2%)
    ppermute x12, waiting for transfers between devices, permute(): return lax.ppermute(array, axis, pairs)  87.4 us
    pallas_call x3, Pallas kernels, call_attend(): pl.pallas_call(functools.partial(attend_kernel, heads, chunk, sets, piece...  42.3 us
    ppermute x12, starting transfers between devices, permute(): return lax.ppermute(array, axis, pairs)  24.2 us
    pallas_call x1, Pallas kernels, body(): pl.pallas_call(functools.partial(combine_kernel, heads, count), out_shape...  5.01 us
    all_to_all x1, starting transfers between devices, body(): lax.all_to_all(parts, 'ta', 0, 0, axis_index_groups=columns, tiled=True)  4.68 us
    pallas_call x1, Pallas kernels, body(): pl.pallas_call(functools.partial(arrange_kernel, heads * CHUNKS), out_sha...  3.99 us
  transfers between devices with their start and end apart: 13, of which 7 were waited for; matrix products, arithmetic and copies ran while one was open for 2% of the time, Pallas kernels for 16%

profile of v3, /device:TPU:119, one launch (start us, length us, event | category | flops | bytes accessed | tf_op | source)
XLA Modules:
  0.0 173.2 jit_solution(11972588600057999529)
XLA Ops:
  0.0 4.0 %shard_map.55 = (bf16[5,6,128,128]{3,2,1,0:T(8,128)(2,1)}, bf16[2,4,6,128,128]{4,3,2,1,0:T(8,128)(2,1)}) custom-call(s32[4,4]{1,0:T(4,128)} %bitcast.16, s32[4,27]{1,0:T(4,128)} %bitcast.17, bf16[2,4,2,32,768]{4,3,2,1,0:T(8,128)(2,1)} %bitcast.13, bf16[2,4,2,32,768]{4,3,2,1,0:T(8,128)(2,1)} %bitcast.14, bf16[2,4,2,32,768]{4,3,2,1,0:T(8,128)(2,1)} %bitcast.15), custom_call_target="tpu_custom_call" | custom-call | tf_op jit(solution)/shard_map/pallas_call | solution.py:297
  4.6 2.1 %collective-permute-start.4 = (bf16[2,4,6,128,128]{4,3,2,1,0:T(8,128)(2,1)}, bf16[2,4,6,128,128]{4,3,2,1,0:T(8,128)(2,1)S(1)}, u32[]{:S(2)}, u32[]{:S(2)}) collective-permute-start(bf16[2,4,6,128,128]{4,3,2,1,0:T(8,128)(2,1)} %get-tuple-element.10.refs_4_.refs_5_.refs_2_.refs_3_.refs_1_), channel_id=1, source_target_pairs={{0,16},{16,32},{32,48},{48,0},{64,80},{80,96},{96,112},{112,64},{1... | collective-permute-start | bytes 4718600 | tf_op jit(solution)/shard_map/ppermute | solution.py:293
  6.7 1.0 collective-permute-start
  8.2 1.3 collective-permute-start.2
  9.5 31.2 %collective-permute-done.3.refs_6_.refs_7_.refs_4_.refs_5_.refs_3_ = bf16[2,4,6,128,128]{4,3,2,1,0:T(8,128)(2,1)S(1)} collective-permute-done((bf16[2,4,6,128,128]{4,3,2,1,0:T(8,128)(2,1)}, bf16[2,4,6,128,128]{4,3,2,1,0:T(8,128)(2,1)S(1)}, u32[]{:S(2)}, u32[]{:S(2)}) %collective-permute-start.3) | collective-permute-done | bytes 1572896 | tf_op jit(solution)/shard_map/ppermute | solution.py:293
  40.8 1.1 slice_select_fusion
  41.8 2.1 %collective-permute-start.7 = (bf16[2,2,6,128,128]{4,3,2,1,0:T(8,128)(2,1)}, bf16[2,2,6,128,128]{4,3,2,1,0:T(8,128)(2,1)}, u32[]{:S(2)}, u32[]{:S(2)}) collective-permute-start(bf16[2,2,6,128,128]{4,3,2,1,0:T(8,128)(2,1)} %slice_select_fusion), channel_id=1, source_target_pairs={{0,64},{64,128},{128,192},{112,48},{176,112},{240,176},{1,65},{65,... | collective-permute-start | bytes 2359304 | tf_op jit(solution)/shard_map/ppermute | solution.py:293
  44.8 3.3 %collective-permute-start.5 = (bf16[4,6,128,128]{3,2,1,0:T(8,128)(2,1)}, bf16[4,6,128,128]{3,2,1,0:T(8,128)(2,1)}, u32[]{:S(2)}, u32[]{:S(2)}) collective-permute-start(bf16[4,6,128,128]{3,2,1,0:T(8,128)(2,1)} %slice_bitcast_fusion.1), channel_id=1, source_target_pairs={{0,16},{16,32},{32,48},{48,0},{64,80},{80,96},{96,112},{112,64},{1... | collective-permute-start | bytes 2359304 | tf_op jit(solution)/shard_map/ppermute | solution.py:293
  49.0 1.1 collective-permute-done.2.refs_2_
  50.1 18.6 %collective-permute-done.7.refs_12_.refs_8_.refs_7_ = bf16[2,2,6,128,128]{4,3,2,1,0:T(8,128)(2,1)} collective-permute-done((bf16[2,2,6,128,128]{4,3,2,1,0:T(8,128)(2,1)}, bf16[2,2,6,128,128]{4,3,2,1,0:T(8,128)(2,1)}, u32[]{:S(2)}, u32[]{:S(2)}) %collective-permute-start.7) | collective-permute-done | bytes 786464 | tf_op jit(solution)/shard_map/ppermute | solution.py:293
  69.5 14.3 %shard_map.57.refs_9_ = bf16[4,3200,128]{2,1,0:T(8,128)(2,1)} custom-call(s32[3]{0:T(128)} %pad_add_fusion.place, bf16[5,6,128,128]{3,2,1,0:T(8,128)(2,1)} %shard_map.56.refs_0_, bf16[5,6,128,128]{3,2,1,0:T(8,128)(2,1)} %collective-permute-done.refs_1_, bf16[5,6,128,128]{3,2,1,0:T(8,128)(2,1)} %collective-permute-done.2.refs_2_, ...), custom_call_target="tpu_custom_call" | custom-call | tf_op jit(solution)/shard_map/pallas_call | solution.py:200
  83.9 4.7 %all-to-all-start = ((bf16[4,3200,128]{2,1,0:T(8,128)(2,1)}), bf16[4,3200,128]{2,1,0:T(8,128)(2,1)S(1)}, u32[]{:S(2)}, u32[]{:S(2)}) async-start(bf16[4,3200,128]{2,1,0:T(8,128)(2,1)} %shard_map.57.refs_9_), calls=%async_computation | async-start | bytes 6553600 | tf_op jit(solution)/shard_map/all_to_all | solution.py:328
  88.5 6.8 %collective-permute-start.8 = (bf16[5,6,128,128]{3,2,1,0:T(8,128)(2,1)}, bf16[5,6,128,128]{3,2,1,0:T(8,128)(2,1)}, u32[]{:S(2)}, u32[]{:S(2)}) collective-permute-start(bf16[5,6,128,128]{3,2,1,0:T(8,128)(2,1)} %shard_map.56.refs_0_), channel_id=1, source_target_pairs={{0,2},{2,4},{4,6},{6,8},{8,10},{10,12},{12,14},{1,3},{3,5},{5,7},{... | collective-permute-start | bytes 2949128 | tf_op jit(solution)/shard_map/ppermute | solution.py:293
  95.3 2.1 %collective-permute-start.9 = (bf16[5,6,128,128]{3,2,1,0:T(8,128)(2,1)}, bf16[5,6,128,128]{3,2,1,0:T(8,128)(2,1)}, u32[]{:S(2)}, u32[]{:S(2)}) collective-permute-start(bf16[5,6,128,128]{3,2,1,0:T(8,128)(2,1)} %shard_map.56.refs_0_), channel_id=1, source_target_pairs={{2,0},{4,2},{6,4},{8,6},{10,8},{12,10},{14,12},{3,1},{5,3},{7,5},{... | collective-permute-start | bytes 2949128 | tf_op jit(solution)/shard_map/ppermute | solution.py:293
  97.4 17.8 %collective-permute-done.8.refs_0_ = bf16[5,6,128,128]{3,2,1,0:T(8,128)(2,1)} collective-permute-done((bf16[5,6,128,128]{3,2,1,0:T(8,128)(2,1)}, bf16[5,6,128,128]{3,2,1,0:T(8,128)(2,1)}, u32[]{:S(2)}, u32[]{:S(2)}) %collective-permute-start.8) | collective-permute-done | bytes 983072 | tf_op jit(solution)/shard_map/ppermute | solution.py:293
  115.3 8.2 %collective-permute-done.9.refs_1_ = bf16[5,6,128,128]{3,2,1,0:T(8,128)(2,1)} collective-permute-done((bf16[5,6,128,128]{3,2,1,0:T(8,128)(2,1)}, bf16[5,6,128,128]{3,2,1,0:T(8,128)(2,1)}, u32[]{:S(2)}, u32[]{:S(2)}) %collective-permute-start.9) | collective-permute-done | bytes 983072 | tf_op jit(solution)/shard_map/ppermute | solution.py:293
  123.4 16.1 %shard_map.58 = (bf16[3200,128]{1,0:T(8,128)(2,1)}, bf16[3200,128]{1,0:T(8,128)(2,1)}) custom-call(s32[3]{0:T(128)} %pad_add_fusion.place, bf16[5,6,128,128]{3,2,1,0:T(8,128)(2,1)} %collective-permute-done.8.refs_0_, bf16[5,6,128,128]{3,2,1,0:T(8,128)(2,1)} %collective-permute-done.9.refs_1_, ...), custom_call_target="tpu_custom_call" | custom-call | tf_op jit(solution)/shard_map/pallas_call | solution.py:200
  139.5 1.9 %collective-permute-start.10 = (bf16[3200,128]{1,0:T(8,128)(2,1)}, bf16[3200,128]{1,0:T(8,128)(2,1)}, u32[]{:S(2)}, u32[]{:S(2)}) collective-permute-start(bf16[3200,128]{1,0:T(8,128)(2,1)} %get-tuple-element.12), channel_id=1, source_target_pairs={{0,2},{2,4},{4,6},{6,8},{8,10},{10,12},{12,14},{1,3},{3,5},{5,7},{... | collective-permute-start | bytes 2457608 | tf_op jit(solution)/shard_map/ppermute | solution.py:293
  141.4 2.4 %collective-permute-start.11 = (bf16[3200,128]{1,0:T(8,128)(2,1)}, bf16[3200,128]{1,0:T(8,128)(2,1)}, u32[]{:S(2)}, u32[]{:S(2)}) collective-permute-start(bf16[3200,128]{1,0:T(8,128)(2,1)} %get-tuple-element.11.refs_8_), channel_id=1, source_target_pairs={{2,0},{4,2},{6,4},{8,6},{10,8},{12,10},{14,12},{3,1},{5,3},{7,5},{... | collective-permute-start | bytes 2457608 | tf_op jit(solution)/shard_map/ppermute | solution.py:293
  143.8 11.9 %shard_map.59.refs_4_.refs_11_ = bf16[3200,128]{1,0:T(8,128)(2,1)} custom-call(s32[3]{0:T(128)} %pad_add_fusion.place, bf16[5,6,128,128]{3,2,1,0:T(8,128)(2,1)} %shard_map.56.refs_0_, bf16[2,4,6,128,128]{4,3,2,1,0:T(8,128)(2,1)} %get-tuple-element.10.refs_4_.refs_5_.refs_2_.refs_3_.refs_1_, ...), custom_call_target="tpu_custom_call" | custom-call | tf_op jit(solution)/shard_map/pallas_call | solution.py:200
  155.8 4.0 %collective-permute-done.10.refs_5_.refs_12_ = bf16[3200,128]{1,0:T(8,128)(2,1)} collective-permute-done((bf16[3200,128]{1,0:T(8,128)(2,1)}, bf16[3200,128]{1,0:T(8,128)(2,1)}, u32[]{:S(2)}, u32[]{:S(2)}) %collective-permute-start.10) | collective-permute-done | bytes 819232 | tf_op jit(solution)/shard_map/ppermute | solution.py:293
  159.8 6.5 %collective-permute-done.11.refs_6_.refs_13_ = bf16[3200,128]{1,0:T(8,128)(2,1)} collective-permute-done((bf16[3200,128]{1,0:T(8,128)(2,1)}, bf16[3200,128]{1,0:T(8,128)(2,1)}, u32[]{:S(2)}, u32[]{:S(2)}) %collective-permute-start.11) | collective-permute-done | bytes 819232 | tf_op jit(solution)/shard_map/ppermute | solution.py:293
  166.3 1.7 %copy-done = bf16[4,3200,128]{2,1,0:T(8,128)(2,1)} copy-done((bf16[4,3200,128]{2,1,0:T(8,128)(2,1)}, bf16[4,3200,128]{2,1,0:T(8,128)(2,1)S(1)}, u32[]{:S(2)}) %copy-start) | copy-done | bytes 3276824
  168.0 5.0 %shard_map.60 = bf16[2,4,2,32,768]{4,3,2,1,0:T(8,128)(2,1)} custom-call(s32[3]{0:T(128)} %pad_add_fusion.place, bf16[4,3200,128]{2,1,0:T(8,128)(2,1)} %copy-done, bf16[4,3200,128]{2,1,0:T(8,128)(2,1)} %copy-done, bf16[4,3200,128]{2,1,0:T(8,128)(2,1)} %copy-done, bf16[4,3200,128]{2,1,0:T(8,128)(2,1)} %copy-done, ...), custom_call_target="tpu_custom_call" | custom-call | tf_op jit(solution)/shard_map/pallas_call | solution.py:343
  (20 shorter events, 3.7 us)
Async XLA Ops:
  4.0 36.8 %collective-permute-start.3 = (bf16[2,4,6,128,128]{4,3,2,1,0:T(8,128)(2,1)}, bf16[2,4,6,128,128]{4,3,2,1,0:T(8,128)(2,1)S(1)}, u32[]{:S(2)}, u32[]{:S(2)}) collective-permute-start(bf16[2,4,6,128,128]{4,3,2,1,0:T(8,128)(2,1)} %get-tuple-element.10.refs_4_.refs_5_.refs_2_.refs_3_.refs_1_), channel_id=1, source_target_pairs={{0,48},{16,0},{32,16},{48,32},{64,112},{80,64},{96,80},{112,96},{1... | collective-permute-start | bytes 4718600 | tf_op jit(solution)/shard_map/ppermute | solution.py:293
  4.6 36.1 %collective-permute-start.4 = (bf16[2,4,6,128,128]{4,3,2,1,0:T(8,128)(2,1)}, bf16[2,4,6,128,128]{4,3,2,1,0:T(8,128)(2,1)S(1)}, u32[]{:S(2)}, u32[]{:S(2)}) collective-permute-start(bf16[2,4,6,128,128]{4,3,2,1,0:T(8,128)(2,1)} %get-tuple-element.10.refs_4_.refs_5_.refs_2_.refs_3_.refs_1_), channel_id=1, source_target_pairs={{0,16},{16,32},{32,48},{48,0},{64,80},{80,96},{96,112},{112,64},{1... | collective-permute-start | bytes 4718600 | tf_op jit(solution)/shard_map/ppermute | solution.py:293
  6.7 41.5 %collective-permute-start = (bf16[5,6,128,128]{3,2,1,0:T(8,128)(2,1)}, bf16[5,6,128,128]{3,2,1,0:T(8,128)(2,1)}, u32[]{:S(2)}, u32[]{:S(2)}) collective-permute-start(bf16[5,6,128,128]{3,2,1,0:T(8,128)(2,1)} %get-tuple-element.9.refs_0_), channel_id=1, source_target_pairs={{0,64},{16,80},{32,96},{48,112},{64,128},{80,144},{96,160},{112,17... | collective-permute-start | bytes 2949128 | tf_op jit(solution)/shard_map/ppermute | solution.py:293
  7.8 41.2 %collective-permute-start.1 = (bf16[5,6,128,128]{3,2,1,0:T(8,128)(2,1)}, bf16[5,6,128,128]{3,2,1,0:T(8,128)(2,1)}, u32[]{:S(2)}, u32[]{:S(2)}) collective-permute-start(bf16[5,6,128,128]{3,2,1,0:T(8,128)(2,1)} %get-tuple-element.9.refs_0_), channel_id=1, source_target_pairs={{0,192},{16,208},{32,224},{48,240},{64,0},{80,16},{96,32},{112,48}... | collective-permute-start | bytes 2949128 | tf_op jit(solution)/shard_map/ppermute | solution.py:293
  8.2 41.9 %collective-permute-start.2 = (bf16[5,6,128,128]{3,2,1,0:T(8,128)(2,1)}, bf16[5,6,128,128]{3,2,1,0:T(8,128)(2,1)}, u32[]{:S(2)}, u32[]{:S(2)}) collective-permute-start(bf16[5,6,128,128]{3,2,1,0:T(8,128)(2,1)} %get-tuple-element.9.refs_0_), channel_id=1, source_target_pairs={{0,128},{16,144},{32,160},{48,176},{64,192},{80,208},{96,224},{112... | collective-permute-start | bytes 2949128 | tf_op jit(solution)/shard_map/ppermute | solution.py:293
  40.8 7.4 %copy-start.1 = (bf16[2,4,6,128,128]{4,3,2,1,0:T(8,128)(2,1)}, bf16[2,4,6,128,128]{4,3,2,1,0:T(8,128)(2,1)S(1)}, u32[]{:S(2)}) copy-start(bf16[2,4,6,128,128]{4,3,2,1,0:T(8,128)(2,1)S(1)} %collective-permute-done.3.refs_6_.refs_7_.refs_4_.refs_5_.refs_3_) | copy-start | bytes 4718596
  40.8 4.1 %copy-start.2 = (bf16[2,4,6,128,128]{4,3,2,1,0:T(8,128)(2,1)}, bf16[2,4,6,128,128]{4,3,2,1,0:T(8,128)(2,1)S(1)}, u32[]{:S(2)}) copy-start(bf16[2,4,6,128,128]{4,3,2,1,0:T(8,128)(2,1)S(1)} %collective-permute-done.4.refs_10_.refs_11_.refs_6_.refs_7_.refs_5_) | copy-start | bytes 4718596
  41.8 26.8 %collective-permute-start.7 = (bf16[2,2,6,128,128]{4,3,2,1,0:T(8,128)(2,1)}, bf16[2,2,6,128,128]{4,3,2,1,0:T(8,128)(2,1)}, u32[]{:S(2)}, u32[]{:S(2)}) collective-permute-start(bf16[2,2,6,128,128]{4,3,2,1,0:T(8,128)(2,1)} %slice_select_fusion), channel_id=1, source_target_pairs={{0,64},{64,128},{128,192},{112,48},{176,112},{240,176},{1,65},{65,... | collective-permute-start | bytes 2359304 | tf_op jit(solution)/shard_map/ppermute | solution.py:293
  44.8 23.8 %collective-permute-start.5 = (bf16[4,6,128,128]{3,2,1,0:T(8,128)(2,1)}, bf16[4,6,128,128]{3,2,1,0:T(8,128)(2,1)}, u32[]{:S(2)}, u32[]{:S(2)}) collective-permute-start(bf16[4,6,128,128]{3,2,1,0:T(8,128)(2,1)} %slice_bitcast_fusion.1), channel_id=1, source_target_pairs={{0,16},{16,32},{32,48},{48,0},{64,80},{80,96},{96,112},{112,64},{1... | collective-permute-start | bytes 2359304 | tf_op jit(solution)/shard_map/ppermute | solution.py:293
  48.2 20.4 %collective-permute-start.6 = (bf16[4,6,128,128]{3,2,1,0:T(8,128)(2,1)S(1)}, bf16[4,6,128,128]{3,2,1,0:T(8,128)(2,1)S(1)}, u32[]{:S(2)}, u32[]{:S(2)}) collective-permute-start(bf16[4,6,128,128]{3,2,1,0:T(8,128)(2,1)S(1)} %slice_bitcast_fusion), channel_id=1, source_target_pairs={{0,48},{16,0},{32,16},{48,32},{64,112},{80,64},{96,80},{112,96},{1... | collective-permute-start | bytes 2359304 | tf_op jit(solution)/shard_map/ppermute | solution.py:293
  68.7 0.9 copy-start.3
  83.9 82.4 %all-to-all-start = ((bf16[4,3200,128]{2,1,0:T(8,128)(2,1)}), bf16[4,3200,128]{2,1,0:T(8,128)(2,1)S(1)}, u32[]{:S(2)}, u32[]{:S(2)}) async-start(bf16[4,3200,128]{2,1,0:T(8,128)(2,1)} %shard_map.57.refs_9_), calls=%async_computation | async-start | bytes 6553600 | tf_op jit(solution)/shard_map/all_to_all | solution.py:328
  88.5 26.7 %collective-permute-start.8 = (bf16[5,6,128,128]{3,2,1,0:T(8,128)(2,1)}, bf16[5,6,128,128]{3,2,1,0:T(8,128)(2,1)}, u32[]{:S(2)}, u32[]{:S(2)}) collective-permute-start(bf16[5,6,128,128]{3,2,1,0:T(8,128)(2,1)} %shard_map.56.refs_0_), channel_id=1, source_target_pairs={{0,2},{2,4},{4,6},{6,8},{8,10},{10,12},{12,14},{1,3},{3,5},{5,7},{... | collective-permute-start | bytes 2949128 | tf_op jit(solution)/shard_map/ppermute | solution.py:293
  95.3 28.1 %collective-permute-start.9 = (bf16[5,6,128,128]{3,2,1,0:T(8,128)(2,1)}, bf16[5,6,128,128]{3,2,1,0:T(8,128)(2,1)}, u32[]{:S(2)}, u32[]{:S(2)}) collective-permute-start(bf16[5,6,128,128]{3,2,1,0:T(8,128)(2,1)} %shard_map.56.refs_0_), channel_id=1, source_target_pairs={{2,0},{4,2},{6,4},{8,6},{10,8},{12,10},{14,12},{3,1},{5,3},{7,5},{... | collective-permute-start | bytes 2949128 | tf_op jit(solution)/shard_map/ppermute | solution.py:293
  139.5 20.3 %collective-permute-start.10 = (bf16[3200,128]{1,0:T(8,128)(2,1)}, bf16[3200,128]{1,0:T(8,128)(2,1)}, u32[]{:S(2)}, u32[]{:S(2)}) collective-permute-start(bf16[3200,128]{1,0:T(8,128)(2,1)} %get-tuple-element.12), channel_id=1, source_target_pairs={{0,2},{2,4},{4,6},{6,8},{8,10},{10,12},{12,14},{1,3},{3,5},{5,7},{... | collective-permute-start | bytes 2457608 | tf_op jit(solution)/shard_map/ppermute | solution.py:293
  141.4 24.9 %collective-permute-start.11 = (bf16[3200,128]{1,0:T(8,128)(2,1)}, bf16[3200,128]{1,0:T(8,128)(2,1)}, u32[]{:S(2)}, u32[]{:S(2)}) collective-permute-start(bf16[3200,128]{1,0:T(8,128)(2,1)} %get-tuple-element.11.refs_8_), channel_id=1, source_target_pairs={{2,0},{4,2},{6,4},{8,6},{10,8},{12,10},{14,12},{3,1},{5,3},{7,5},{... | collective-permute-start | bytes 2457608 | tf_op jit(solution)/shard_map/ppermute | solution.py:293
  166.3 1.7 %copy-start = (bf16[4,3200,128]{2,1,0:T(8,128)(2,1)}, bf16[4,3200,128]{2,1,0:T(8,128)(2,1)S(1)}, u32[]{:S(2)}) copy-start(bf16[4,3200,128]{2,1,0:T(8,128)(2,1)S(1)} %all-to-all-done.refs_0_.refs_1_.refs_2_.refs_3_.refs_7_.refs_8_.refs_9_.refs_10_) | copy-start | bytes 9830404

commit v4 on v3

--- a/solution.py
+++ b/solution.py
@@ -324,7 +324,7 @@
     for c in range(CHUNKS):
         held = ((both[c],) * 2, (from_right[c],) * 2, (far_k[c], far_v[c]), (from_left[c],) * 2)
         far_sets = ((0, False, True),) * SIDE
-        (parts,) = call_attend(heads, c, place, far_sets, (q, q1, q2, q3), whole, held, None, (edge,), True)
+        (parts,) = call_attend(heads, c, place, far_sets, (q, q1, q2, q3), whole, held, None, (edge, q_low, q_high), True)
         arrived = lax.all_to_all(parts, "ta", 0, 0, axis_index_groups=columns, tiled=True)
         near = ((0, 2), (0, 1), None, (1, 1))
         for_low, for_high = call_attend(

time: 175 us -> 161 us (0.920)
  the two profiles are of different devices: /device:TPU:119 before, /device:TPU:113 now
where the time goes in v4:
time: 161 us; the launch traced here: 159 us
  waiting for transfers between devices  76.2 us (47%)
  Pallas kernels  43.7 us (27%)
  starting transfers between devices  32.9 us (20%)
  local copies, waits for them, and re-layouts  4.56 us (3%)
  other arithmetic  1.66 us (1%)
    ppermute x12, waiting for transfers between devices, permute(): return lax.ppermute(array, axis, pairs)  76.2 us
    pallas_call x3, Pallas kernels, call_attend(): pl.pallas_call(functools.partial(attend_kernel, heads, chunk, sets, piece...  34.8 us
    ppermute x12, starting transfers between devices, permute(): return lax.ppermute(array, axis, pairs)  28.5 us
    pallas_call x1, Pallas kernels, body(): pl.pallas_call(functools.partial(combine_kernel, heads, count), out_shape...  5.01 us
    all_to_all x1, starting transfers between devices, body(): lax.all_to_all(parts, 'ta', 0, 0, axis_index_groups=columns, tiled=True)  4.43 us
    pallas_call x1, Pallas kernels, body(): pl.pallas_call(functools.partial(arrange_kernel, heads * CHUNKS), out_sha...  3.94 us
  transfers between devices with their start and end apart: 13, of which 9 were waited for; matrix products, arithmetic and copies ran while one was open for 2% of the time, Pallas kernels for 13%

profile of v4, /device:TPU:113, one launch (start us, length us, event | category | flops | bytes accessed | tf_op | source)
XLA Modules:
  0.0 159.4 jit_solution(1596597881240751517)
XLA Ops:
  0.0 3.9 %shard_map.55 = (bf16[5,6,128,128]{3,2,1,0:T(8,128)(2,1)}, bf16[2,4,6,128,128]{4,3,2,1,0:T(8,128)(2,1)}) custom-call(s32[4,4]{1,0:T(4,128)} %bitcast.16, s32[4,27]{1,0:T(4,128)} %bitcast.17, bf16[2,4,2,32,768]{4,3,2,1,0:T(8,128)(2,1)} %bitcast.13, bf16[2,4,2,32,768]{4,3,2,1,0:T(8,128)(2,1)} %bitcast.14, bf16[2,4,2,32,768]{4,3,2,1,0:T(8,128)(2,1)} %bitcast.15), custom_call_target="tpu_custom_call" | custom-call | tf_op jit(solution)/shard_map/pallas_call | solution.py:297
  3.9 1.3 collective-permute-start.4
  5.2 1.5 collective-permute-start.3
  6.8 2.1 %collective-permute-start.1 = (bf16[5,6,128,128]{3,2,1,0:T(8,128)(2,1)}, bf16[5,6,128,128]{3,2,1,0:T(8,128)(2,1)}, u32[]{:S(2)}, u32[]{:S(2)}) collective-permute-start(bf16[5,6,128,128]{3,2,1,0:T(8,128)(2,1)} %get-tuple-element.9.refs_0_), channel_id=1, source_target_pairs={{0,192},{16,208},{32,224},{48,240},{64,0},{80,16},{96,32},{112,48}... | collective-permute-start | bytes 2949128 | tf_op jit(solution)/shard_map/ppermute | solution.py:293
  8.9 21.7 %collective-permute-done.2.refs_2_ = bf16[5,6,128,128]{3,2,1,0:T(8,128)(2,1)} collective-permute-done((bf16[5,6,128,128]{3,2,1,0:T(8,128)(2,1)}, bf16[5,6,128,128]{3,2,1,0:T(8,128)(2,1)}, u32[]{:S(2)}, u32[]{:S(2)}) %collective-permute-start.2) | collective-permute-done | bytes 983072 | tf_op jit(solution)/shard_map/ppermute | solution.py:293
  30.6 20.7 %collective-permute-done.1.refs_2_.refs_3_ = bf16[5,6,128,128]{3,2,1,0:T(8,128)(2,1)} collective-permute-done((bf16[5,6,128,128]{3,2,1,0:T(8,128)(2,1)}, bf16[5,6,128,128]{3,2,1,0:T(8,128)(2,1)}, u32[]{:S(2)}, u32[]{:S(2)}) %collective-permute-start.1) | collective-permute-done | bytes 983072 | tf_op jit(solution)/shard_map/ppermute | solution.py:293
  51.2 2.0 %collective-permute-done.refs_1_ = bf16[5,6,128,128]{3,2,1,0:T(8,128)(2,1)} collective-permute-done((bf16[5,6,128,128]{3,2,1,0:T(8,128)(2,1)}, bf16[5,6,128,128]{3,2,1,0:T(8,128)(2,1)}, u32[]{:S(2)}, u32[]{:S(2)}) %collective-permute-start) | collective-permute-done | bytes 983072 | tf_op jit(solution)/shard_map/ppermute | solution.py:293
  53.3 2.4 %collective-permute-start.9 = (bf16[5,6,128,128]{3,2,1,0:T(8,128)(2,1)}, bf16[5,6,128,128]{3,2,1,0:T(8,128)(2,1)}, u32[]{:S(2)}, u32[]{:S(2)}) collective-permute-start(bf16[5,6,128,128]{3,2,1,0:T(8,128)(2,1)} %shard_map.56.refs_0_), channel_id=1, source_target_pairs={{2,0},{4,2},{6,4},{8,6},{10,8},{12,10},{14,12},{3,1},{5,3},{7,5},{... | collective-permute-start | bytes 2949128 | tf_op jit(solution)/shard_map/ppermute | solution.py:293
  55.7 5.3 %collective-permute-start.8 = (bf16[5,6,128,128]{3,2,1,0:T(8,128)(2,1)}, bf16[5,6,128,128]{3,2,1,0:T(8,128)(2,1)}, u32[]{:S(2)}, u32[]{:S(2)}) collective-permute-start(bf16[5,6,128,128]{3,2,1,0:T(8,128)(2,1)} %shard_map.56.refs_0_), channel_id=1, source_target_pairs={{0,2},{2,4},{4,6},{6,8},{8,10},{10,12},{12,14},{1,3},{3,5},{5,7},{... | collective-permute-start | bytes 2949128 | tf_op jit(solution)/shard_map/ppermute | solution.py:293
  63.0 2.7 %collective-permute-start.6 = (bf16[4,6,128,128]{3,2,1,0:T(8,128)(2,1)}, bf16[4,6,128,128]{3,2,1,0:T(8,128)(2,1)}, u32[]{:S(2)}, u32[]{:S(2)}) collective-permute-start(bf16[4,6,128,128]{3,2,1,0:T(8,128)(2,1)} %slice_bitcast_fusion), channel_id=1, source_target_pairs={{0,48},{16,0},{32,16},{48,32},{64,112},{80,64},{96,80},{112,96},{1... | collective-permute-start | bytes 2359304 | tf_op jit(solution)/shard_map/ppermute | solution.py:293
  66.6 2.9 %collective-permute-start.7 = (bf16[2,2,6,128,128]{4,3,2,1,0:T(8,128)(2,1)}, bf16[2,2,6,128,128]{4,3,2,1,0:T(8,128)(2,1)S(1)}, u32[]{:S(2)}, u32[]{:S(2)}) collective-permute-start(bf16[2,2,6,128,128]{4,3,2,1,0:T(8,128)(2,1)} %slice_select_fusion), channel_id=1, source_target_pairs={{0,64},{64,128},{128,192},{112,48},{176,112},{240,176},{1,65},{65,... | collective-permute-start | bytes 2359304 | tf_op jit(solution)/shard_map/ppermute | solution.py:293
  70.2 1.5 collective-permute-done.9.refs_14_.refs_1_
  71.7 9.2 %collective-permute-done.8.refs_13_.refs_0_ = bf16[5,6,128,128]{3,2,1,0:T(8,128)(2,1)} collective-permute-done((bf16[5,6,128,128]{3,2,1,0:T(8,128)(2,1)}, bf16[5,6,128,128]{3,2,1,0:T(8,128)(2,1)}, u32[]{:S(2)}, u32[]{:S(2)}) %collective-permute-start.8) | collective-permute-done | bytes 983072 | tf_op jit(solution)/shard_map/ppermute | solution.py:293
  81.2 5.0 %collective-permute-done.7.refs_12_.refs_8_.refs_7_ = bf16[2,2,6,128,128]{4,3,2,1,0:T(8,128)(2,1)S(1)} collective-permute-done((bf16[2,2,6,128,128]{4,3,2,1,0:T(8,128)(2,1)}, bf16[2,2,6,128,128]{4,3,2,1,0:T(8,128)(2,1)S(1)}, u32[]{:S(2)}, u32[]{:S(2)}) %collective-permute-start.7) | collective-permute-done | bytes 786464 | tf_op jit(solution)/shard_map/ppermute | solution.py:293
  87.0 14.2 %shard_map.57.refs_9_ = bf16[4,3200,128]{2,1,0:T(8,128)(2,1)} custom-call(s32[3]{0:T(128)} %pad_add_fusion.place, bf16[5,6,128,128]{3,2,1,0:T(8,128)(2,1)} %shard_map.56.refs_0_, bf16[5,6,128,128]{3,2,1,0:T(8,128)(2,1)} %collective-permute-done.refs_1_, bf16[5,6,128,128]{3,2,1,0:T(8,128)(2,1)} %collective-permute-done.2.refs_2_, ...), custom_call_target="tpu_custom_call" | custom-call | tf_op jit(solution)/shard_map/pallas_call | solution.py:200
  101.3 4.4 %all-to-all-start = ((bf16[4,3200,128]{2,1,0:T(8,128)(2,1)}), bf16[4,3200,128]{2,1,0:T(8,128)(2,1)S(1)}, u32[]{:S(2)}, u32[]{:S(2)}) async-start(bf16[4,3200,128]{2,1,0:T(8,128)(2,1)} %shard_map.57.refs_9_), calls=%async_computation | async-start | bytes 6553600 | tf_op jit(solution)/shard_map/all_to_all | solution.py:328
  105.7 14.0 %shard_map.58 = (bf16[3200,128]{1,0:T(8,128)(2,1)}, bf16[3200,128]{1,0:T(8,128)(2,1)}) custom-call(s32[3]{0:T(128)} %pad_add_fusion.place, bf16[5,6,128,128]{3,2,1,0:T(8,128)(2,1)} %collective-permute-done.8.refs_13_.refs_0_, bf16[5,6,128,128]{3,2,1,0:T(8,128)(2,1)} %collective-permute-done.9.refs_14_.refs_1_, ...), custom_call_target="tpu_custom_call" | custom-call | tf_op jit(solution)/shard_map/pallas_call | solution.py:200
  119.8 8.4 %collective-permute-start.10 = (bf16[3200,128]{1,0:T(8,128)(2,1)}, bf16[3200,128]{1,0:T(8,128)(2,1)}, u32[]{:S(2)}, u32[]{:S(2)}) collective-permute-start(bf16[3200,128]{1,0:T(8,128)(2,1)} %get-tuple-element.12), channel_id=1, source_target_pairs={{0,2},{2,4},{4,6},{6,8},{8,10},{10,12},{12,14},{1,3},{3,5},{5,7},{... | collective-permute-start | bytes 2457608 | tf_op jit(solution)/shard_map/ppermute | solution.py:293
  128.2 1.9 %collective-permute-start.11 = (bf16[3200,128]{1,0:T(8,128)(2,1)}, bf16[3200,128]{1,0:T(8,128)(2,1)}, u32[]{:S(2)}, u32[]{:S(2)}) collective-permute-start(bf16[3200,128]{1,0:T(8,128)(2,1)} %get-tuple-element.11.refs_8_), channel_id=1, source_target_pairs={{2,0},{4,2},{6,4},{8,6},{10,8},{12,10},{14,12},{3,1},{5,3},{7,5},{... | collective-permute-start | bytes 2457608 | tf_op jit(solution)/shard_map/ppermute | solution.py:293
  130.1 6.5 %shard_map.59.refs_4_.refs_11_ = bf16[3200,128]{1,0:T(8,128)(2,1)} custom-call(s32[3]{0:T(128)} %pad_add_fusion.place, bf16[5,6,128,128]{3,2,1,0:T(8,128)(2,1)} %shard_map.56.refs_0_, bf16[2,4,6,128,128]{4,3,2,1,0:T(8,128)(2,1)} %get-tuple-element.10.refs_4_.refs_5_.refs_2_.refs_3_.refs_1_, ...), custom_call_target="tpu_custom_call" | custom-call | tf_op jit(solution)/shard_map/pallas_call | solution.py:200
  136.6 6.8 %collective-permute-done.10.refs_5_.refs_12_ = bf16[3200,128]{1,0:T(8,128)(2,1)} collective-permute-done((bf16[3200,128]{1,0:T(8,128)(2,1)}, bf16[3200,128]{1,0:T(8,128)(2,1)}, u32[]{:S(2)}, u32[]{:S(2)}) %collective-permute-start.10) | collective-permute-done | bytes 819232 | tf_op jit(solution)/shard_map/ppermute | solution.py:293
  143.4 9.2 %collective-permute-done.11.refs_6_.refs_13_ = bf16[3200,128]{1,0:T(8,128)(2,1)} collective-permute-done((bf16[3200,128]{1,0:T(8,128)(2,1)}, bf16[3200,128]{1,0:T(8,128)(2,1)}, u32[]{:S(2)}, u32[]{:S(2)}) %collective-permute-start.11) | collective-permute-done | bytes 819232 | tf_op jit(solution)/shard_map/ppermute | solution.py:293
  152.6 1.7 %copy-done = bf16[4,3200,128]{2,1,0:T(8,128)(2,1)} copy-done((bf16[4,3200,128]{2,1,0:T(8,128)(2,1)}, bf16[4,3200,128]{2,1,0:T(8,128)(2,1)S(1)}, u32[]{:S(2)}) %copy-start) | copy-done | bytes 3276824
  154.2 5.0 %shard_map.60 = bf16[2,4,2,32,768]{4,3,2,1,0:T(8,128)(2,1)} custom-call(s32[3]{0:T(128)} %pad_add_fusion.place, bf16[4,3200,128]{2,1,0:T(8,128)(2,1)} %copy-done, bf16[4,3200,128]{2,1,0:T(8,128)(2,1)} %copy-done, bf16[4,3200,128]{2,1,0:T(8,128)(2,1)} %copy-done, bf16[4,3200,128]{2,1,0:T(8,128)(2,1)} %copy-done, ...), custom_call_target="tpu_custom_call" | custom-call | tf_op jit(solution)/shard_map/pallas_call | solution.py:343
  (20 shorter events, 4.9 us)
Async XLA Ops:
  3.9 57.0 %collective-permute-start.4 = (bf16[2,4,6,128,128]{4,3,2,1,0:T(8,128)(2,1)}, bf16[2,4,6,128,128]{4,3,2,1,0:T(8,128)(2,1)S(1)}, u32[]{:S(2)}, u32[]{:S(2)}) collective-permute-start(bf16[2,4,6,128,128]{4,3,2,1,0:T(8,128)(2,1)} %get-tuple-element.10.refs_4_.refs_5_.refs_2_.refs_3_.refs_1_), channel_id=1, source_target_pairs={{0,16},{16,32},{32,48},{48,0},{64,80},{80,96},{96,112},{112,64},{1... | collective-permute-start | bytes 4718600 | tf_op jit(solution)/shard_map/ppermute | solution.py:293
  5.2 56.7 %collective-permute-start.3 = (bf16[2,4,6,128,128]{4,3,2,1,0:T(8,128)(2,1)}, bf16[2,4,6,128,128]{4,3,2,1,0:T(8,128)(2,1)S(1)}, u32[]{:S(2)}, u32[]{:S(2)}) collective-permute-start(bf16[2,4,6,128,128]{4,3,2,1,0:T(8,128)(2,1)} %get-tuple-element.10.refs_4_.refs_5_.refs_2_.refs_3_.refs_1_), channel_id=1, source_target_pairs={{0,48},{16,0},{32,16},{48,32},{64,112},{80,64},{96,80},{112,96},{1... | collective-permute-start | bytes 4718600 | tf_op jit(solution)/shard_map/ppermute | solution.py:293
  6.7 23.9 %collective-permute-start.2 = (bf16[5,6,128,128]{3,2,1,0:T(8,128)(2,1)}, bf16[5,6,128,128]{3,2,1,0:T(8,128)(2,1)}, u32[]{:S(2)}, u32[]{:S(2)}) collective-permute-start(bf16[5,6,128,128]{3,2,1,0:T(8,128)(2,1)} %get-tuple-element.9.refs_0_), channel_id=1, source_target_pairs={{0,128},{16,144},{32,160},{48,176},{64,192},{80,208},{96,224},{112... | collective-permute-start | bytes 2949128 | tf_op jit(solution)/shard_map/ppermute | solution.py:293
  6.8 44.5 %collective-permute-start.1 = (bf16[5,6,128,128]{3,2,1,0:T(8,128)(2,1)}, bf16[5,6,128,128]{3,2,1,0:T(8,128)(2,1)}, u32[]{:S(2)}, u32[]{:S(2)}) collective-permute-start(bf16[5,6,128,128]{3,2,1,0:T(8,128)(2,1)} %get-tuple-element.9.refs_0_), channel_id=1, source_target_pairs={{0,192},{16,208},{32,224},{48,240},{64,0},{80,16},{96,32},{112,48}... | collective-permute-start | bytes 2949128 | tf_op jit(solution)/shard_map/ppermute | solution.py:293
  8.9 44.4 %collective-permute-start = (bf16[5,6,128,128]{3,2,1,0:T(8,128)(2,1)}, bf16[5,6,128,128]{3,2,1,0:T(8,128)(2,1)}, u32[]{:S(2)}, u32[]{:S(2)}) collective-permute-start(bf16[5,6,128,128]{3,2,1,0:T(8,128)(2,1)} %get-tuple-element.9.refs_0_), channel_id=1, source_target_pairs={{0,64},{16,80},{32,96},{48,112},{64,128},{80,144},{96,160},{112,17... | collective-permute-start | bytes 2949128 | tf_op jit(solution)/shard_map/ppermute | solution.py:293
  53.3 18.4 %collective-permute-start.9 = (bf16[5,6,128,128]{3,2,1,0:T(8,128)(2,1)}, bf16[5,6,128,128]{3,2,1,0:T(8,128)(2,1)}, u32[]{:S(2)}, u32[]{:S(2)}) collective-permute-start(bf16[5,6,128,128]{3,2,1,0:T(8,128)(2,1)} %shard_map.56.refs_0_), channel_id=1, source_target_pairs={{2,0},{4,2},{6,4},{8,6},{10,8},{12,10},{14,12},{3,1},{5,3},{7,5},{... | collective-permute-start | bytes 2949128 | tf_op jit(solution)/shard_map/ppermute | solution.py:293
  55.7 25.2 %collective-permute-start.8 = (bf16[5,6,128,128]{3,2,1,0:T(8,128)(2,1)}, bf16[5,6,128,128]{3,2,1,0:T(8,128)(2,1)}, u32[]{:S(2)}, u32[]{:S(2)}) collective-permute-start(bf16[5,6,128,128]{3,2,1,0:T(8,128)(2,1)} %shard_map.56.refs_0_), channel_id=1, source_target_pairs={{0,2},{2,4},{4,6},{6,8},{8,10},{10,12},{12,14},{1,3},{3,5},{5,7},{... | collective-permute-start | bytes 2949128 | tf_op jit(solution)/shard_map/ppermute | solution.py:293
  61.0 4.7 %copy-start.1 = (bf16[2,4,6,128,128]{4,3,2,1,0:T(8,128)(2,1)}, bf16[2,4,6,128,128]{4,3,2,1,0:T(8,128)(2,1)S(1)}, u32[]{:S(2)}) copy-start(bf16[2,4,6,128,128]{4,3,2,1,0:T(8,128)(2,1)S(1)} %collective-permute-done.4.refs_10_.refs_11_.refs_6_.refs_7_.refs_5_) | copy-start | bytes 4718596
  62.0 18.9 %collective-permute-start.5 = (bf16[4,6,128,128]{3,2,1,0:T(8,128)(2,1)}, bf16[4,6,128,128]{3,2,1,0:T(8,128)(2,1)}, u32[]{:S(2)}, u32[]{:S(2)}) collective-permute-start(bf16[4,6,128,128]{3,2,1,0:T(8,128)(2,1)} %slice_bitcast_fusion.1), channel_id=1, source_target_pairs={{0,16},{16,32},{32,48},{48,0},{64,80},{80,96},{96,112},{112,64},{1... | collective-permute-start | bytes 2359304 | tf_op jit(solution)/shard_map/ppermute | solution.py:293
  62.0 4.7 %copy-start.2 = (bf16[2,4,6,128,128]{4,3,2,1,0:T(8,128)(2,1)}, bf16[2,4,6,128,128]{4,3,2,1,0:T(8,128)(2,1)S(1)}, u32[]{:S(2)}) copy-start(bf16[2,4,6,128,128]{4,3,2,1,0:T(8,128)(2,1)S(1)} %collective-permute-done.3.refs_6_.refs_7_.refs_4_.refs_5_.refs_3_) | copy-start | bytes 4718596
  63.0 18.2 %collective-permute-start.6 = (bf16[4,6,128,128]{3,2,1,0:T(8,128)(2,1)}, bf16[4,6,128,128]{3,2,1,0:T(8,128)(2,1)}, u32[]{:S(2)}, u32[]{:S(2)}) collective-permute-start(bf16[4,6,128,128]{3,2,1,0:T(8,128)(2,1)} %slice_bitcast_fusion), channel_id=1, source_target_pairs={{0,48},{16,0},{32,16},{48,32},{64,112},{80,64},{96,80},{112,96},{1... | collective-permute-start | bytes 2359304 | tf_op jit(solution)/shard_map/ppermute | solution.py:293
  66.6 19.5 %collective-permute-start.7 = (bf16[2,2,6,128,128]{4,3,2,1,0:T(8,128)(2,1)}, bf16[2,2,6,128,128]{4,3,2,1,0:T(8,128)(2,1)S(1)}, u32[]{:S(2)}, u32[]{:S(2)}) collective-permute-start(bf16[2,2,6,128,128]{4,3,2,1,0:T(8,128)(2,1)} %slice_select_fusion), channel_id=1, source_target_pairs={{0,64},{64,128},{128,192},{112,48},{176,112},{240,176},{1,65},{65,... | collective-permute-start | bytes 2359304 | tf_op jit(solution)/shard_map/ppermute | solution.py:293
  86.2 0.9 copy-start.3
  101.3 51.3 %all-to-all-start = ((bf16[4,3200,128]{2,1,0:T(8,128)(2,1)}), bf16[4,3200,128]{2,1,0:T(8,128)(2,1)S(1)}, u32[]{:S(2)}, u32[]{:S(2)}) async-start(bf16[4,3200,128]{2,1,0:T(8,128)(2,1)} %shard_map.57.refs_9_), calls=%async_computation | async-start | bytes 6553600 | tf_op jit(solution)/shard_map/all_to_all | solution.py:328
  119.8 23.6 %collective-permute-start.10 = (bf16[3200,128]{1,0:T(8,128)(2,1)}, bf16[3200,128]{1,0:T(8,128)(2,1)}, u32[]{:S(2)}, u32[]{:S(2)}) collective-permute-start(bf16[3200,128]{1,0:T(8,128)(2,1)} %get-tuple-element.12), channel_id=1, source_target_pairs={{0,2},{2,4},{4,6},{6,8},{8,10},{10,12},{12,14},{1,3},{3,5},{5,7},{... | collective-permute-start | bytes 2457608 | tf_op jit(solution)/shard_map/ppermute | solution.py:293
  128.2 24.4 %collective-permute-start.11 = (bf16[3200,128]{1,0:T(8,128)(2,1)}, bf16[3200,128]{1,0:T(8,128)(2,1)}, u32[]{:S(2)}, u32[]{:S(2)}) collective-permute-start(bf16[3200,128]{1,0:T(8,128)(2,1)} %get-tuple-element.11.refs_8_), channel_id=1, source_target_pairs={{2,0},{4,2},{6,4},{8,6},{10,8},{12,10},{14,12},{3,1},{5,3},{7,5},{... | collective-permute-start | bytes 2457608 | tf_op jit(solution)/shard_map/ppermute | solution.py:293
  152.6 1.7 %copy-start = (bf16[4,3200,128]{2,1,0:T(8,128)(2,1)}, bf16[4,3200,128]{2,1,0:T(8,128)(2,1)S(1)}, u32[]{:S(2)}) copy-start(bf16[4,3200,128]{2,1,0:T(8,128)(2,1)S(1)} %all-to-all-done.refs_0_.refs_1_.refs_2_.refs_3_.refs_7_.refs_8_.refs_9_.refs_10_) | copy-start | bytes 9830404

commit v5 on v2

--- a/solution.py
+++ b/solution.py
@@ -21,7 +21,7 @@
 NONE = -1e30
 SCALE = float(HEAD ** -0.5)
 LOG2E = float(np.log2(np.e))
-VMEM_LIMIT = 50 * 1024 * 1024
+VMEM_LIMIT = 60 * 1024 * 1024
 F32 = jnp.float32
 BF16 = jnp.bfloat16
 
@@ -303,19 +303,22 @@
         out_specs=[vmem] * (2 + CHUNKS),
         scratch_shapes=[pltpu.VMEM(blocks[0].shape, BF16) for _ in range(3)]
         + [pltpu.VMEM((TABLE, TILE), F32), pltpu.SemaphoreType.DMA((3,))],
-        compiler_params=pltpu.CompilerParams(vmem_limit_bytes=60 * 1024 * 1024),
+        compiler_params=pltpu.CompilerParams(vmem_limit_bytes=VMEM_LIMIT),
     )(place, selected.reshape(4, SEL), window_mask.reshape(4, 27), *blocks)
 
-    from_left = [permute(b, right) for b in both]
-    from_right = [permute(b, left) for b in both]
+    q_low, q_high = permute(q, higher, "ha"), permute(q, lower, "ha")
+    q2 = permute(q, opposite)
+    q, edge = tie((q, edge), (q2, q_low, q_high))
+    q1, q3 = permute(q, up), permute(q, down)
+    edge = permute(edge, ends)
+    from_left, from_right = [], []
+    for c in range(CHUNKS):
+        if c:
+            (both[c],) = tie((both[c],), (from_left[-1], from_right[-1]))
+        from_left.append(permute(both[c], right))
+        from_right.append(permute(both[c], left))
     far_k = [permute(b[0], right) for b in from_left]
     far_v = [permute(b[1], left) for b in from_right]
-    q1, q3 = permute(q, up), permute(q, down)
-    q_low = permute(q, higher, "ha")
-    again, edge = tie((q, edge), (q1, q3, q_low))
-    q_high = permute(again, lower, "ha")
-    q2 = permute(again, opposite)
-    edge = permute(edge, ends)
 
     partial = []
     whole = ((0, 2),) * SIDE

time: 149 us -> 146 us (0.980)
  the two profiles are of different devices: /device:TPU:175 before, /device:TPU:1 now
where the time goes in v5:
time: 146 us; the launch traced here: 144 us
  waiting for transfers between devices  62.6 us (43%)
  Pallas kernels  46.3 us (32%)
  starting transfers between devices  32.4 us (22%)
  local copies, waits for them, and re-layouts  2.07 us (1%)
    ppermute x15, waiting for transfers between devices, permute(): return lax.ppermute(array, axis, pairs)  62.6 us
    pallas_call x3, Pallas kernels, call_attend(): pl.pallas_call(functools.partial(attend_kernel, heads, chunk, sets, piece...  37.2 us
    ppermute x15, starting transfers between devices, permute(): return lax.ppermute(array, axis, pairs)  32.4 us
    pallas_call x1, Pallas kernels, body(): pl.pallas_call(functools.partial(combine_kernel, heads, count), out_shape...  4.79 us
    pallas_call x1, Pallas kernels, body(): pl.pallas_call(functools.partial(arrange_kernel, heads * CHUNKS), out_sha...  4.3 us
  transfers between devices with their start and end apart: 15, of which 9 were waited for; matrix products, arithmetic and copies ran while one was open for 1% of the time, Pallas kernels for 18%

profile of v5, /device:TPU:1, one launch (start us, length us, event | category | flops | bytes accessed | tf_op | source)
XLA Modules:
  0.0 144.3 jit_solution(7421356417368729265)
XLA Ops:
  0.7 4.3 %shard_map.55 = (bf16[5,6,128,128]{3,2,1,0:T(8,128)(2,1)}, bf16[2,2,6,128,128]{4,3,2,1,0:T(8,128)(2,1)}, bf16[2,4,6,128,128]{4,3,2,1,0:T(8,128)(2,1)}) custom-call(s32[3]{0:T(128)} %pad_add_fusion.place, s32[4,4]{1,0:T(4,128)} %bitcast.16, s32[4,27]{1,0:T(4,128)} %bitcast.17, bf16[2,4,2,32,768]{4,3,2,1,0:T(8,128)(2,1)} %bitcast.13, ...), custom_call_target="tpu_custom_call" | custom-call | tf_op jit(solution)/shard_map/pallas_call | solution.py:297
  5.0 2.1 %collective-permute-start.4 = (bf16[2,4,6,128,128]{4,3,2,1,0:T(8,128)(2,1)}, bf16[2,4,6,128,128]{4,3,2,1,0:T(8,128)(2,1)S(1)}, u32[]{:S(2)}, u32[]{:S(2)}) collective-permute-start(bf16[2,4,6,128,128]{4,3,2,1,0:T(8,128)(2,1)} %get-tuple-element.20.refs_3_.refs_4_.refs_1_.refs_2_), channel_id=1, source_target_pairs={{0,16},{16,32},{32,48},{48,0},{64,80},{80,96},{96,112},{112,64},{1... | collective-permute-start | bytes 4718600 | tf_op jit(solution)/shard_map/ppermute | solution.py:293
  7.1 1.4 collective-permute-start.3
  8.4 5.0 %collective-permute-start.2 = (bf16[5,6,128,128]{3,2,1,0:T(8,128)(2,1)}, bf16[5,6,128,128]{3,2,1,0:T(8,128)(2,1)}, u32[]{:S(2)}, u32[]{:S(2)}) collective-permute-start(bf16[5,6,128,128]{3,2,1,0:T(8,128)(2,1)} %get-tuple-element.17.refs_0_), channel_id=1, source_target_pairs={{2,0},{4,2},{6,4},{8,6},{10,8},{12,10},{14,12},{3,1},{5,3},{7,5},{... | collective-permute-start | bytes 2949128 | tf_op jit(solution)/shard_map/ppermute | solution.py:293
  13.4 3.1 %collective-permute-start.1 = (bf16[5,6,128,128]{3,2,1,0:T(8,128)(2,1)}, bf16[5,6,128,128]{3,2,1,0:T(8,128)(2,1)}, u32[]{:S(2)}, u32[]{:S(2)}) collective-permute-start(bf16[5,6,128,128]{3,2,1,0:T(8,128)(2,1)} %get-tuple-element.17.refs_0_), channel_id=1, source_target_pairs={{0,2},{2,4},{4,6},{6,8},{8,10},{10,12},{12,14},{1,3},{3,5},{5,7},{... | collective-permute-start | bytes 2949128 | tf_op jit(solution)/shard_map/ppermute | solution.py:293
  16.5 3.0 %collective-permute-start = (bf16[5,6,128,128]{3,2,1,0:T(8,128)(2,1)}, bf16[5,6,128,128]{3,2,1,0:T(8,128)(2,1)}, u32[]{:S(2)}, u32[]{:S(2)}) collective-permute-start(bf16[5,6,128,128]{3,2,1,0:T(8,128)(2,1)} %get-tuple-element.17.refs_0_), channel_id=1, source_target_pairs={{0,128},{16,144},{32,160},{48,176},{64,192},{80,208},{96,224},{112... | collective-permute-start | bytes 2949128 | tf_op jit(solution)/shard_map/ppermute | solution.py:293
  19.5 18.0 %collective-permute-done.2.refs_4_.refs_1_ = bf16[5,6,128,128]{3,2,1,0:T(8,128)(2,1)} collective-permute-done((bf16[5,6,128,128]{3,2,1,0:T(8,128)(2,1)}, bf16[5,6,128,128]{3,2,1,0:T(8,128)(2,1)}, u32[]{:S(2)}, u32[]{:S(2)}) %collective-permute-start.2) | collective-permute-done | bytes 983072 | tf_op jit(solution)/shard_map/ppermute | solution.py:293
  37.5 3.9 %collective-permute-done.refs_2_.refs_1_ = bf16[5,6,128,128]{3,2,1,0:T(8,128)(2,1)} collective-permute-done((bf16[5,6,128,128]{3,2,1,0:T(8,128)(2,1)}, bf16[5,6,128,128]{3,2,1,0:T(8,128)(2,1)}, u32[]{:S(2)}, u32[]{:S(2)}) %collective-permute-start) | collective-permute-done | bytes 983072 | tf_op jit(solution)/shard_map/ppermute | solution.py:293
  41.4 2.2 %collective-permute-start.9 = (bf16[5,6,128,128]{3,2,1,0:T(8,128)(2,1)}, bf16[5,6,128,128]{3,2,1,0:T(8,128)(2,1)}, u32[]{:S(2)}, u32[]{:S(2)}) collective-permute-start(bf16[5,6,128,128]{3,2,1,0:T(8,128)(2,1)} %get-tuple-element.19.refs_0_), channel_id=1, source_target_pairs={{0,192},{16,208},{32,224},{48,240},{64,0},{80,16},{96,32},{112,48}... | collective-permute-start | bytes 2949128 | tf_op jit(solution)/shard_map/ppermute | solution.py:293
  43.7 1.5 %collective-permute-start.7 = (bf16[2,2,6,128,128]{4,3,2,1,0:T(8,128)(2,1)}, bf16[2,2,6,128,128]{4,3,2,1,0:T(8,128)(2,1)}, u32[]{:S(2)}, u32[]{:S(2)}) collective-permute-start(bf16[2,2,6,128,128]{4,3,2,1,0:T(8,128)(2,1)} %get-tuple-element.21), channel_id=1, source_target_pairs={{48,64},{112,128},{176,192},{64,48},{128,112},{192,176},{49,65},{1... | collective-permute-start | bytes 2359304 | tf_op jit(solution)/shard_map/ppermute | solution.py:293
  47.3 3.0 %collective-permute-start.6 = (bf16[4,6,128,128]{3,2,1,0:T(8,128)(2,1)}, bf16[4,6,128,128]{3,2,1,0:T(8,128)(2,1)}, u32[]{:S(2)}, u32[]{:S(2)}) collective-permute-start(bf16[4,6,128,128]{3,2,1,0:T(8,128)(2,1)} %slice_bitcast_fusion), channel_id=1, source_target_pairs={{0,48},{16,0},{32,16},{48,32},{64,112},{80,64},{96,80},{112,96},{1... | collective-permute-start | bytes 2359304 | tf_op jit(solution)/shard_map/ppermute | solution.py:293
  50.3 13.2 %shard_map.59 = (bf16[3200,128]{1,0:T(8,128)(2,1)}, bf16[3200,128]{1,0:T(8,128)(2,1)}) custom-call(s32[3]{0:T(128)} %pad_add_fusion.place, bf16[5,6,128,128]{3,2,1,0:T(8,128)(2,1)} %collective-permute-done.1.refs_3_.refs_0_, bf16[5,6,128,128]{3,2,1,0:T(8,128)(2,1)} %collective-permute-done.2.refs_4_.refs_1_, ...), custom_call_target="tpu_custom_call" | custom-call | tf_op jit(solution)/shard_map/pallas_call | solution.py:198
  63.5 1.9 %collective-permute-done.9.refs_2_ = bf16[5,6,128,128]{3,2,1,0:T(8,128)(2,1)} collective-permute-done((bf16[5,6,128,128]{3,2,1,0:T(8,128)(2,1)}, bf16[5,6,128,128]{3,2,1,0:T(8,128)(2,1)}, u32[]{:S(2)}, u32[]{:S(2)}) %collective-permute-start.9) | collective-permute-done | bytes 983072 | tf_op jit(solution)/shard_map/ppermute | solution.py:293
  65.3 16.0 %collective-permute-done.8.refs_0_ = bf16[5,6,128,128]{3,2,1,0:T(8,128)(2,1)} collective-permute-done((bf16[5,6,128,128]{3,2,1,0:T(8,128)(2,1)}, bf16[5,6,128,128]{3,2,1,0:T(8,128)(2,1)}, u32[]{:S(2)}, u32[]{:S(2)}) %collective-permute-start.8) | collective-permute-done | bytes 983072 | tf_op jit(solution)/shard_map/ppermute | solution.py:293
  81.4 1.2 collective-permute-done.5.refs_7_.refs_5_
  82.6 11.8 %shard_map.57 = (bf16[3200,128]{1,0:T(8,128)(2,1)}, bf16[3200,128]{1,0:T(8,128)(2,1)}, bf16[3200,128]{1,0:T(8,128)(2,1)}) custom-call(s32[3]{0:T(128)} %pad_add_fusion.place, bf16[5,6,128,128]{3,2,1,0:T(8,128)(2,1)} %collective-permute-done.8.refs_0_, bf16[5,6,128,128]{3,2,1,0:T(8,128)(2,1)} %collective-permute-done.refs_2_.refs_1_, ...), custom_call_target="tpu_custom_call" | custom-call | tf_op jit(solution)/shard_map/pallas_call | solution.py:198
  94.4 2.1 %collective-permute-start.13 = (bf16[3200,128]{1,0:T(8,128)(2,1)}, bf16[3200,128]{1,0:T(8,128)(2,1)S(1)}, u32[]{:S(2)}, u32[]{:S(2)}) collective-permute-start(bf16[3200,128]{1,0:T(8,128)(2,1)} %get-tuple-element.27), channel_id=1, source_target_pairs={{0,2},{2,4},{4,6},{6,8},{8,10},{10,12},{12,14},{1,3},{3,5},{5,7},{... | collective-permute-start | bytes 2457608 | tf_op jit(solution)/shard_map/ppermute | solution.py:293
  96.5 2.7 %collective-permute-start.14 = (bf16[3200,128]{1,0:T(8,128)(2,1)}, bf16[3200,128]{1,0:T(8,128)(2,1)S(1)}, u32[]{:S(2)}, u32[]{:S(2)}) collective-permute-start(bf16[3200,128]{1,0:T(8,128)(2,1)} %get-tuple-element.28), channel_id=1, source_target_pairs={{2,0},{4,2},{6,4},{8,6},{10,8},{12,10},{14,12},{3,1},{5,3},{7,5},{... | collective-permute-start | bytes 2457608 | tf_op jit(solution)/shard_map/ppermute | solution.py:293
  99.2 3.6 %collective-permute-start.11 = (bf16[3200,128]{1,0:T(8,128)(2,1)}, bf16[3200,128]{1,0:T(8,128)(2,1)S(1)}, u32[]{:S(2)}, u32[]{:S(2)}) collective-permute-start(bf16[3200,128]{1,0:T(8,128)(2,1)} %get-tuple-element.23), channel_id=1, source_target_pairs={{0,128},{16,144},{32,160},{48,176},{64,192},{80,208},{96,224},{112... | collective-permute-start | bytes 2457608 | tf_op jit(solution)/shard_map/ppermute | solution.py:293
  103.0 2.5 %collective-permute-start.10 = (bf16[3200,128]{1,0:T(8,128)(2,1)S(1)}, bf16[3200,128]{1,0:T(8,128)(2,1)}, u32[]{:S(2)}, u32[]{:S(2)}) collective-permute-start(bf16[3200,128]{1,0:T(8,128)(2,1)S(1)} %copy-done.2), channel_id=1, source_target_pairs={{0,192},{16,208},{32,224},{48,240},{64,0},{80,16},{96,32},{112,48}... | collective-permute-start | bytes 2457608 | tf_op jit(solution)/shard_map/ppermute | solution.py:293
  105.5 12.2 %shard_map.58.refs_0_.refs_6_ = bf16[3200,128]{1,0:T(8,128)(2,1)} custom-call(s32[3]{0:T(128)} %pad_add_fusion.place, bf16[5,6,128,128]{3,2,1,0:T(8,128)(2,1)} %get-tuple-element.19.refs_0_, bf16[2,4,6,128,128]{4,3,2,1,0:T(8,128)(2,1)} %get-tuple-element.20.refs_3_.refs_4_.refs_1_.refs_2_, ...), custom_call_target="tpu_custom_call" | custom-call | tf_op jit(solution)/shard_map/pallas_call | solution.py:198
  117.7 2.7 %collective-permute-done.14.refs_5_.refs_11_ = bf16[3200,128]{1,0:T(8,128)(2,1)S(1)} collective-permute-done((bf16[3200,128]{1,0:T(8,128)(2,1)}, bf16[3200,128]{1,0:T(8,128)(2,1)S(1)}, u32[]{:S(2)}, u32[]{:S(2)}) %collective-permute-start.14) | collective-permute-done | bytes 819232 | tf_op jit(solution)/shard_map/ppermute | solution.py:293
  121.5 17.5 %collective-permute-done.12.refs_3_.refs_9_ = bf16[3200,128]{1,0:T(8,128)(2,1)} collective-permute-done((bf16[3200,128]{1,0:T(8,128)(2,1)}, bf16[3200,128]{1,0:T(8,128)(2,1)}, u32[]{:S(2)}, u32[]{:S(2)}) %collective-permute-start.12) | collective-permute-done | bytes 819232 | tf_op jit(solution)/shard_map/ppermute | solution.py:293
  139.4 4.8 %shard_map.61 = bf16[2,4,2,32,768]{4,3,2,1,0:T(8,128)(2,1)} custom-call(s32[3]{0:T(128)} %pad_add_fusion.place, bf16[3200,128]{1,0:T(8,128)(2,1)} %shard_map.58.refs_0_.refs_6_, bf16[3200,128]{1,0:T(8,128)(2,1)} %collective-permute-done.10.refs_1_.refs_7_, bf16[3200,128]{1,0:T(8,128)(2,1)} %copy-done.5, ...), custom_call_target="tpu_custom_call" | custom-call | tf_op jit(solution)/shard_map/pallas_call | solution.py:341
  (28 shorter events, 4.3 us)
Async XLA Ops:
  5.0 40.2 %collective-permute-start.4 = (bf16[2,4,6,128,128]{4,3,2,1,0:T(8,128)(2,1)}, bf16[2,4,6,128,128]{4,3,2,1,0:T(8,128)(2,1)S(1)}, u32[]{:S(2)}, u32[]{:S(2)}) collective-permute-start(bf16[2,4,6,128,128]{4,3,2,1,0:T(8,128)(2,1)} %get-tuple-element.20.refs_3_.refs_4_.refs_1_.refs_2_), channel_id=1, source_target_pairs={{0,16},{16,32},{32,48},{48,0},{64,80},{80,96},{96,112},{112,64},{1... | collective-permute-start | bytes 4718600 | tf_op jit(solution)/shard_map/ppermute | solution.py:293
  7.1 39.1 %collective-permute-start.3 = (bf16[2,4,6,128,128]{4,3,2,1,0:T(8,128)(2,1)}, bf16[2,4,6,128,128]{4,3,2,1,0:T(8,128)(2,1)S(1)}, u32[]{:S(2)}, u32[]{:S(2)}) collective-permute-start(bf16[2,4,6,128,128]{4,3,2,1,0:T(8,128)(2,1)} %get-tuple-element.20.refs_3_.refs_4_.refs_1_.refs_2_), channel_id=1, source_target_pairs={{0,48},{16,0},{32,16},{48,32},{64,112},{80,64},{96,80},{112,96},{1... | collective-permute-start | bytes 4718600 | tf_op jit(solution)/shard_map/ppermute | solution.py:293
  8.4 29.0 %collective-permute-start.2 = (bf16[5,6,128,128]{3,2,1,0:T(8,128)(2,1)}, bf16[5,6,128,128]{3,2,1,0:T(8,128)(2,1)}, u32[]{:S(2)}, u32[]{:S(2)}) collective-permute-start(bf16[5,6,128,128]{3,2,1,0:T(8,128)(2,1)} %get-tuple-element.17.refs_0_), channel_id=1, source_target_pairs={{2,0},{4,2},{6,4},{8,6},{10,8},{12,10},{14,12},{3,1},{5,3},{7,5},{... | collective-permute-start | bytes 2949128 | tf_op jit(solution)/shard_map/ppermute | solution.py:293
  13.4 24.1 %collective-permute-start.1 = (bf16[5,6,128,128]{3,2,1,0:T(8,128)(2,1)}, bf16[5,6,128,128]{3,2,1,0:T(8,128)(2,1)}, u32[]{:S(2)}, u32[]{:S(2)}) collective-permute-start(bf16[5,6,128,128]{3,2,1,0:T(8,128)(2,1)} %get-tuple-element.17.refs_0_), channel_id=1, source_target_pairs={{0,2},{2,4},{4,6},{6,8},{8,10},{10,12},{12,14},{1,3},{3,5},{5,7},{... | collective-permute-start | bytes 2949128 | tf_op jit(solution)/shard_map/ppermute | solution.py:293
  16.5 24.9 %collective-permute-start = (bf16[5,6,128,128]{3,2,1,0:T(8,128)(2,1)}, bf16[5,6,128,128]{3,2,1,0:T(8,128)(2,1)}, u32[]{:S(2)}, u32[]{:S(2)}) collective-permute-start(bf16[5,6,128,128]{3,2,1,0:T(8,128)(2,1)} %get-tuple-element.17.refs_0_), channel_id=1, source_target_pairs={{0,128},{16,144},{32,160},{48,176},{64,192},{80,208},{96,224},{112... | collective-permute-start | bytes 2949128 | tf_op jit(solution)/shard_map/ppermute | solution.py:293
  41.4 23.9 %collective-permute-start.9 = (bf16[5,6,128,128]{3,2,1,0:T(8,128)(2,1)}, bf16[5,6,128,128]{3,2,1,0:T(8,128)(2,1)}, u32[]{:S(2)}, u32[]{:S(2)}) collective-permute-start(bf16[5,6,128,128]{3,2,1,0:T(8,128)(2,1)} %get-tuple-element.19.refs_0_), channel_id=1, source_target_pairs={{0,192},{16,208},{32,224},{48,240},{64,0},{80,16},{96,32},{112,48}... | collective-permute-start | bytes 2949128 | tf_op jit(solution)/shard_map/ppermute | solution.py:293
  43.7 37.7 %collective-permute-start.8 = (bf16[5,6,128,128]{3,2,1,0:T(8,128)(2,1)}, bf16[5,6,128,128]{3,2,1,0:T(8,128)(2,1)}, u32[]{:S(2)}, u32[]{:S(2)}) collective-permute-start(bf16[5,6,128,128]{3,2,1,0:T(8,128)(2,1)} %get-tuple-element.19.refs_0_), channel_id=1, source_target_pairs={{0,64},{16,80},{32,96},{48,112},{64,128},{80,144},{96,160},{112,17... | collective-permute-start | bytes 2949128 | tf_op jit(solution)/shard_map/ppermute | solution.py:293
  43.7 6.6 %collective-permute-start.7 = (bf16[2,2,6,128,128]{4,3,2,1,0:T(8,128)(2,1)}, bf16[2,2,6,128,128]{4,3,2,1,0:T(8,128)(2,1)}, u32[]{:S(2)}, u32[]{:S(2)}) collective-permute-start(bf16[2,2,6,128,128]{4,3,2,1,0:T(8,128)(2,1)} %get-tuple-element.21), channel_id=1, source_target_pairs={{48,64},{112,128},{176,192},{64,48},{128,112},{192,176},{49,65},{1... | collective-permute-start | bytes 2359304 | tf_op jit(solution)/shard_map/ppermute | solution.py:293
  45.2 2.1 %copy-start = (bf16[2,4,6,128,128]{4,3,2,1,0:T(8,128)(2,1)}, bf16[2,4,6,128,128]{4,3,2,1,0:T(8,128)(2,1)S(1)}, u32[]{:S(2)}) copy-start(bf16[2,4,6,128,128]{4,3,2,1,0:T(8,128)(2,1)S(1)} %collective-permute-done.4.refs_9_.refs_10_.refs_7_.refs_8_.refs_6_) | copy-start | bytes 4718596
  46.2 36.4 %collective-permute-start.5 = (bf16[4,6,128,128]{3,2,1,0:T(8,128)(2,1)}, bf16[4,6,128,128]{3,2,1,0:T(8,128)(2,1)}, u32[]{:S(2)}, u32[]{:S(2)}) collective-permute-start(bf16[4,6,128,128]{3,2,1,0:T(8,128)(2,1)} %slice_bitcast_fusion.1), channel_id=1, source_target_pairs={{0,16},{16,32},{32,48},{48,0},{64,80},{80,96},{96,112},{112,64},{1... | collective-permute-start | bytes 2359304 | tf_op jit(solution)/shard_map/ppermute | solution.py:293
  46.2 4.1 %copy-start.1 = (bf16[2,4,6,128,128]{4,3,2,1,0:T(8,128)(2,1)}, bf16[2,4,6,128,128]{4,3,2,1,0:T(8,128)(2,1)S(1)}, u32[]{:S(2)}) copy-start(bf16[2,4,6,128,128]{4,3,2,1,0:T(8,128)(2,1)S(1)} %collective-permute-done.3.refs_5_.refs_6_.refs_3_.refs_4_) | copy-start | bytes 4718596
  47.3 35.3 %collective-permute-start.6 = (bf16[4,6,128,128]{3,2,1,0:T(8,128)(2,1)}, bf16[4,6,128,128]{3,2,1,0:T(8,128)(2,1)}, u32[]{:S(2)}, u32[]{:S(2)}) collective-permute-start(bf16[4,6,128,128]{3,2,1,0:T(8,128)(2,1)} %slice_bitcast_fusion), channel_id=1, source_target_pairs={{0,48},{16,0},{32,16},{48,32},{64,112},{80,64},{96,80},{112,96},{1... | collective-permute-start | bytes 2359304 | tf_op jit(solution)/shard_map/ppermute | solution.py:293
  94.4 8.6 %copy-start.2 = (bf16[3200,128]{1,0:T(8,128)(2,1)S(1)}, bf16[3200,128]{1,0:T(8,128)(2,1)}, u32[]{:S(2)}) copy-start(bf16[3200,128]{1,0:T(8,128)(2,1)} %get-tuple-element.22.refs_10_.refs_2_) | copy-start | bytes 2457604
  94.4 23.3 %collective-permute-start.13 = (bf16[3200,128]{1,0:T(8,128)(2,1)}, bf16[3200,128]{1,0:T(8,128)(2,1)S(1)}, u32[]{:S(2)}, u32[]{:S(2)}) collective-permute-start(bf16[3200,128]{1,0:T(8,128)(2,1)} %get-tuple-element.27), channel_id=1, source_target_pairs={{0,2},{2,4},{4,6},{6,8},{8,10},{10,12},{12,14},{1,3},{3,5},{5,7},{... | collective-permute-start | bytes 2457608 | tf_op jit(solution)/shard_map/ppermute | solution.py:293
  96.5 23.9 %collective-permute-start.14 = (bf16[3200,128]{1,0:T(8,128)(2,1)}, bf16[3200,128]{1,0:T(8,128)(2,1)S(1)}, u32[]{:S(2)}, u32[]{:S(2)}) collective-permute-start(bf16[3200,128]{1,0:T(8,128)(2,1)} %get-tuple-element.28), channel_id=1, source_target_pairs={{2,0},{4,2},{6,4},{8,6},{10,8},{12,10},{14,12},{3,1},{5,3},{7,5},{... | collective-permute-start | bytes 2457608 | tf_op jit(solution)/shard_map/ppermute | solution.py:293
  99.2 22.3 %collective-permute-start.11 = (bf16[3200,128]{1,0:T(8,128)(2,1)}, bf16[3200,128]{1,0:T(8,128)(2,1)S(1)}, u32[]{:S(2)}, u32[]{:S(2)}) collective-permute-start(bf16[3200,128]{1,0:T(8,128)(2,1)} %get-tuple-element.23), channel_id=1, source_target_pairs={{0,128},{16,144},{32,160},{48,176},{64,192},{80,208},{96,224},{112... | collective-permute-start | bytes 2457608 | tf_op jit(solution)/shard_map/ppermute | solution.py:293
  102.8 36.2 %collective-permute-start.12 = (bf16[3200,128]{1,0:T(8,128)(2,1)}, bf16[3200,128]{1,0:T(8,128)(2,1)}, u32[]{:S(2)}, u32[]{:S(2)}) collective-permute-start(bf16[3200,128]{1,0:T(8,128)(2,1)} %get-tuple-element.24), channel_id=1, source_target_pairs={{0,64},{16,80},{32,96},{48,112},{64,128},{80,144},{96,160},{112,17... | collective-permute-start | bytes 2457608 | tf_op jit(solution)/shard_map/ppermute | solution.py:293
  103.0 36.4 %collective-permute-start.10 = (bf16[3200,128]{1,0:T(8,128)(2,1)S(1)}, bf16[3200,128]{1,0:T(8,128)(2,1)}, u32[]{:S(2)}, u32[]{:S(2)}) collective-permute-start(bf16[3200,128]{1,0:T(8,128)(2,1)S(1)} %copy-done.2), channel_id=1, source_target_pairs={{0,192},{16,208},{32,224},{48,240},{64,0},{80,16},{96,32},{112,48}... | collective-permute-start | bytes 2457608 | tf_op jit(solution)/shard_map/ppermute | solution.py:293
  117.7 21.6 %copy-start.3 = (bf16[3200,128]{1,0:T(8,128)(2,1)}, bf16[3200,128]{1,0:T(8,128)(2,1)S(1)}, u32[]{:S(2)}) copy-start(bf16[3200,128]{1,0:T(8,128)(2,1)S(1)} %collective-permute-done.13.refs_4_.refs_10_) | copy-start | bytes 2457604
  120.4 18.9 %copy-start.4 = (bf16[3200,128]{1,0:T(8,128)(2,1)}, bf16[3200,128]{1,0:T(8,128)(2,1)S(1)}, u32[]{:S(2)}) copy-start(bf16[3200,128]{1,0:T(8,128)(2,1)S(1)} %collective-permute-done.14.refs_5_.refs_11_) | copy-start | bytes 2457604
  121.5 17.9 %copy-start.5 = (bf16[3200,128]{1,0:T(8,128)(2,1)}, bf16[3200,128]{1,0:T(8,128)(2,1)S(1)}, u32[]{:S(2)}) copy-start(bf16[3200,128]{1,0:T(8,128)(2,1)S(1)} %collective-permute-done.11.refs_2_.refs_8_) | copy-start | bytes 2457604
